TPU v7x, 32 devices: a whole 2x2x4 slice. The times are simulated.
32 devices in a mesh: groups: 2 (over y), depth: 4 (over x, core), screen: 4 (over z).
Axes of the slice: x: 2, y: 2, z: 4, core: 2. Of those that a mesh axis runs over, the one named last changes fastest.
Arguments:
- density: float32 [128, 128, 512], P('groups', 'screen', 'depth'), parts along dimension 0, may hold values from 0.05 to 4
- emission: float32 [128, 128, 512], P('groups', 'screen', 'depth'), parts along dimension 0, may hold values from 0.2 to 2
- taps: float32 [8, 512], P('groups', 'depth'), parts along dimension 0, may hold values from 0.05 to 0.5
- shift: int32 [1024], P(('groups', 'depth')), parts along dimension 0, may hold values from -6 to 6
- row_taps: float32 [8, 512], P('groups', 'depth'), parts along dimension 0, may hold values from 0.05 to 0.5
- row_shift: int32 [1024], P(('groups', 'depth')), parts along dimension 0, may hold values from -6 to 6
- step_length: float32 [1024], P(('groups', 'depth')), parts along dimension 0, may hold values from 0.5 to 4
- cotangent: float32 [128, 128], P('groups', 'screen'), parts along dimension 0, may hold values from -1536 to 1536
Outputs:
- grad_density: float32 [128, 128, 512], P('groups', 'screen', 'depth'), parts along dimension 0
- grad_emission: float32 [128, 128, 512], P('groups', 'screen', 'depth'), parts along dimension 0
There are 2 independent parts, one for each index of `groups`. A program takes and returns all parts, laid end to end along the dimension named above; each array names one. Nothing has to cross between parts.
All inputs are finite; a program needn't handle non-finite values.
Results may differ from a plain program's by a relative error of at most 0.000092.
Values sent between devices are 32-bit elements; how exact they have to be, the bound alone decides.
No kernel may reach another device: no remote copies, remote signals or barrier semaphores. Data moves between devices by JAX's collectives and lax.ppermute only.
A program may use at most 64 MiB of HBM per device.

v0:
```python
import jax
import jax.numpy as jnp
from jax import lax
from jax.sharding import PartitionSpec as P

HALO = 8


def with_halo(cells, sides, width):
    for axis, dim in sides:
        count = lax.axis_size(axis)
        ends = count - 1
        head = lax.slice_in_dim(cells, 0, width, axis=dim)
        tail = lax.slice_in_dim(cells, cells.shape[dim] - width, cells.shape[dim], axis=dim)
        cells = jnp.concatenate(
            [
                lax.ppermute(tail, axis, [(i, (i + 1) % count) for i in range(ends)]),
                cells,
                lax.ppermute(head, axis, [((i + 1) % count, i) for i in range(ends)]),
            ],
            axis=dim,
        )
    return cells


def entering(value, axis, join, neutral, backward):
    count, mine = (lax.axis_size(axis), lax.axis_index(axis))
    pieces = lax.all_gather(value, axis)
    if backward:
        pieces = pieces[::-1]
        mine = count - 1 - mine
    running = jnp.full_like(value, 0) + jnp.asarray(neutral, value.dtype)

    def turn(position, running):
        longer = join(running, pieces[position])
        return jnp.where(position < mine, longer, running)

    return lax.fori_loop(0, count - 1, turn, running)


def coefficients(taps, shift):
    offsets = jnp.arange(2 * HALO + 1, dtype=jnp.int32)
    which_tap = jnp.arange(taps.shape[0], dtype=jnp.int32)
    placed = shift[None, None, :] + which_tap[:, None, None] - 1 + HALO
    matches = (placed == offsets[None, :, None]).astype(jnp.float32)
    return jnp.sum(matches * taps[:, None, :], axis=0)


def row_pass(field, row_coefficient, flipped):
    length = field.shape[1]
    padded = jnp.pad(field, ((0, 0), (HALO, HALO), (0, 0), (0, 0)))
    total = jnp.zeros(field.shape, jnp.float32)
    for offset in range(2 * HALO + 1):
        begin = 2 * HALO - offset if flipped else offset
        total = total + row_coefficient[offset] * padded[:, begin : begin + length]
    return total


def add_pair(earlier, later):
    return earlier + later


def on_device(density, emission, taps, shift, row_taps, row_shift, step_length, cotangent):
    coefficient = coefficients(taps, shift)
    row_coefficient = coefficients(row_taps, row_shift)
    columns = density.shape[1]
    planes = density.shape[2]
    all_planes = planes * lax.axis_size("depth")
    stacked = jnp.stack([density, emission])
    reach = HALO
    extended = with_halo(stacked, (("screen", 2),), reach)
    sampled = jnp.zeros((2, stacked.shape[1], columns, planes), jnp.float32)
    for offset in range(2 * HALO + 1):
        sampled = sampled + coefficient[offset] * extended[:, :, offset : offset + columns, :]
    sampled = row_pass(sampled, row_coefficient, False)
    sampled_density = sampled[0]
    sampled_emission = sampled[1]
    optical = step_length * sampled_density / all_planes
    plane_ids = jnp.arange(planes, dtype=jnp.int32)
    lower_ones = (plane_ids[:, None] < plane_ids[None, :]).astype(jnp.float32)
    upper_ones = (plane_ids[:, None] > plane_ids[None, :]).astype(jnp.float32)
    local_before = jnp.einsum("yxa,ab->yxb", optical, lower_ones, precision=lax.Precision.HIGHEST)
    slab_optical = jnp.sum(optical, axis=2)
    local_transmit = jnp.exp(-local_before)
    alpha = -jnp.expm1(-optical)
    local_light = local_transmit * alpha * sampled_emission
    slab_light = jnp.sum(local_light, axis=2)
    zeros_plane = jnp.zeros_like(slab_optical)
    front_depth = entering(slab_optical, "depth", add_pair, zeros_plane, False)
    absolute_light = jnp.exp(-front_depth) * slab_light
    back_light = entering(absolute_light, "depth", add_pair, zeros_plane, True)
    front_transmit = jnp.exp(-front_depth)
    transmit = front_transmit[..., None] * local_transmit
    light = front_transmit[..., None] * local_light
    local_behind = jnp.einsum("yxa,ab->yxb", light, upper_ones, precision=lax.Precision.HIGHEST)
    behind = back_light[..., None] + local_behind
    weight = cotangent[..., None]
    grad_optical = weight * (transmit * jnp.exp(-optical) * sampled_emission - behind)
    grad_sampled_density = step_length * grad_optical / all_planes
    grad_sampled_emission = weight * transmit * alpha
    grad_samples = row_pass(
        jnp.stack([grad_sampled_density, grad_sampled_emission]), row_coefficient, True
    )
    grad_extended = with_halo(grad_samples, (("screen", 2),), HALO)
    gradients = jnp.zeros(grad_samples.shape, jnp.float32)
    for offset in range(2 * HALO + 1):
        begin = 2 * HALO - offset
        gradients = (
            gradients + coefficient[offset] * grad_extended[:, :, begin : begin + columns, :]
        )
    return (gradients[0], gradients[1])


def solution(mesh):
    in_specs = (
        P("groups", "screen", "depth"),
        P("groups", "screen", "depth"),
        P("groups", "depth"),
        P(("groups", "depth")),
        P("groups", "depth"),
        P(("groups", "depth")),
        P(("groups", "depth")),
        P("groups", "screen"),
    )
    out_specs = (P("groups", "screen", "depth"), P("groups", "screen", "depth"))
    return jax.shard_map(
        on_device, mesh=mesh, in_specs=in_specs, out_specs=out_specs, check_vma=False
    )
```

profile of v0, /device:TPU:14, one launch (start us, length us, event | category | flops | bytes accessed | tf_op | source)
XLA Modules:
  0.0 78.6 jit_solution(12643032806770021830)
XLA Ops:
  0.6 0.0 copy-start.1
  0.6 0.0 copy-start
  0.7 0.0 copy-start.9
  0.7 0.0 copy-start.10
  0.7 0.0 copy-start.2
  0.7 0.0 copy-start.7
  0.7 0.0 copy-start.8
  0.7 2.4 %fusion.137 = (f32[2,64,8,128]{3,2,1,0:T(8,128)}, f32[2,64,8,128]{3,2,1,0:T(8,128)}) fusion(f32[1,64,32,128]{3,2,1,0:T(8,128)} %bitcast.132, f32[1,64,32,128]{3,2,1,0:T(8,128)} %bitcast.129), kind=kLoop, calls=%fused_computation.236 | loop fusion | flops 262144 | bytes 3145728 | tf_op jit(solution)/shard_map/stack | solution.py:69
  3.1 3.5 %collective-permute-start = (f32[2,64,8,128]{3,2,1,0:T(8,128)}, f32[2,64,8,128]{3,2,1,0:T(8,128)S(1)}, u32[]{:S(2)}, u32[]{:S(2)}) collective-permute-start(f32[2,64,8,128]{3,2,1,0:T(8,128)} %get-tuple-element.240), channel_id=1, source_target_pairs={{0,1},{1,2},{2,3},{4,5},{5,6},{6,7},{8,9},{9,10},{10,11},{12,13},{... | collective-permute-start | bytes 1572872 | tf_op jit(solution)/shard_map/ppermute | solution.py:17
  6.6 2.4 %collective-permute-start.1 = (f32[2,64,8,128]{3,2,1,0:T(8,128)}, f32[2,64,8,128]{3,2,1,0:T(8,128)S(1)}, u32[]{:S(2)}, u32[]{:S(2)}) collective-permute-start(f32[2,64,8,128]{3,2,1,0:T(8,128)} %get-tuple-element.241), channel_id=1, source_target_pairs={{1,0},{2,1},{3,2},{5,4},{6,5},{7,6},{9,8},{10,9},{11,10},{13,12},{... | collective-permute-start | bytes 1572872 | tf_op jit(solution)/shard_map/ppermute | solution.py:19
  9.0 0.0 copy-done.9
  9.0 0.0 copy-done.10
  9.0 0.0 copy-done.2
  9.0 0.1 copy.21
  9.1 0.0 copy-done.7
  9.3 9.6 %collective-permute-done = f32[2,64,8,128]{3,2,1,0:T(8,128)S(1)} collective-permute-done((f32[2,64,8,128]{3,2,1,0:T(8,128)}, f32[2,64,8,128]{3,2,1,0:T(8,128)S(1)}, u32[]{:S(2)}, u32[]{:S(2)}) %collective-permute-start) | collective-permute-done | bytes 524320 | tf_op jit(solution)/shard_map/ppermute | solution.py:17
  18.8 3.2 %collective-permute-done.1 = f32[2,64,8,128]{3,2,1,0:T(8,128)S(1)} collective-permute-done((f32[2,64,8,128]{3,2,1,0:T(8,128)}, f32[2,64,8,128]{3,2,1,0:T(8,128)S(1)}, u32[]{:S(2)}, u32[]{:S(2)}) %collective-permute-start.1) | collective-permute-done | bytes 524320 | tf_op jit(solution)/shard_map/ppermute | solution.py:19
  22.0 0.0 copy-done.1
  22.0 0.3 maximum_maximum_fusion
  22.4 4.4 %fusion.9 = f32[2,64,32,128]{3,2,1,0:T(8,128)S(1)} fusion(f32[1,64,32,128]{3,2,1,0:T(8,128)S(1)} %bitcast.131, f32[1,64,32,128]{3,2,1,0:T(8,128)S(1)} %bitcast.134, f32[2,64,40,128]{3,2,1,0:T(8,128)S(1)} %get-tuple-element.239, f32[2,64,40,128]{3,2,1,0:T(8,128)S(1)} %get-tuple-element.238, f32[128]{0:T(128)S(1)} %get-tuple-element.262, ...), kind=kLoop, calls=%fused_computation.80 | loop fusion | flops 17825792 | bytes 37757440 | tf_op jit(solution)/shard_map/add | solution.py:74
  26.8 0.0 copy-start.11
  26.8 5.8 %fusion.70 = f32[2,64,32,128]{3,2,1,0:T(8,128)S(1)} fusion(f32[2,64,32,128]{3,2,1,0:T(8,128)S(1)} %fusion.9, f32[128]{0:T(128)S(1)} %get-tuple-element.245, f32[128]{0:T(128)S(1)} %get-tuple-element.246, f32[128]{0:T(128)S(1)} %get-tuple-element.247, f32[128]{0:T(128)S(1)} %get-tuple-element.248, f32[128]{0:T(128)S(1)} %get-tuple-element.249, ...), kind=kLoop, calls=%fused_computation.141 | loop fusion | flops 17301504 | bytes 4203008 | tf_op jit(solution)/shard_map/add | solution.py:55
  32.6 0.0 copy-done.11
  32.6 1.2 %fusion.136 = (f32[64,32]{1,0:T(8,128)S(1)}, f32[64,32]{1,0:T(8,128)S(1)}, f32[64,32,128]{2,1,0:T(8,128)S(1)}) fusion(f32[2,64,32,128]{3,2,1,0:T(8,128)S(1)} %fusion.70, f32[128]{0:T(128)S(1)} %copy-done.11), kind=kOutput, calls=%fused_computation.235 | convolution fusion | flops 405549056 | bytes 4211712 | tf_op jit(solution)/shard_map/yxa,ab->yxb/dot_general | solution.py:82
  33.8 0.1 copy.22
  33.9 5.2 %all-gather.2 = f32[4,64,32]{1,2,0:T(8,128)S(1)} all-gather(f32[1,64,32]{1,2,0:T(8,128)S(1)} %copy.22), channel_id=2, replica_groups=mesh['groups'=2,'depth'=4,'screen'=4] {'depth'}, dimensions={0}, use_global_device_ids=true | all-gather | bytes 40960 | tf_op jit(solution)/shard_map/all_gather | solution.py:28
  39.1 0.4 while.28
  39.1 0.1 copy.30
  39.3 0.1 copy.30
  39.4 0.1 copy.30
  39.5 0.1 copy.24
  39.6 5.2 %all-gather.3 = f32[4,64,32]{1,2,0:T(8,128)S(1)} all-gather(f32[1,64,32]{1,2,0:T(8,128)S(1)} %copy.24), channel_id=3, replica_groups=mesh['groups'=2,'depth'=4,'screen'=4] {'depth'}, dimensions={0}, use_global_device_ids=true | all-gather | bytes 40960 | tf_op jit(solution)/shard_map/all_gather | solution.py:28
  44.8 0.4 while.29
  44.8 0.1 copy.31
  45.0 0.1 copy.31
  45.1 0.1 copy.31
  45.2 0.7 multiply_bitcast_fusion
  45.9 1.6 %fusion.131 = f32[1,64,32,128]{3,2,1,0:T(8,128)S(1)} fusion(f32[2,64,32,128]{3,2,1,0:T(8,128)S(1)} %fusion.70, f32[64,32,128]{2,1,0:T(8,128)S(1)} %get-tuple-element.278, f32[64,32]{1,0:T(8,128)S(1)} %get-tuple-element.161, f32[64,32]{1,0:T(8,128)S(1)} %get-tuple-element.243, f32[64,32]{1,0:T(8,128)S(1)} %copy.21, f32[128]{0:T(128)S(1)} %copy-done.11), kind=kOutput, calls=%fused_computation.222 | convolution fusion | flops 407388160 | bytes 7472128 | tf_op jit(solution)/shard_map/yxa,ab->yxb/dot_general | solution.py:95
  47.5 0.2 pad_maximum_fusion.4
  47.7 5.7 %fusion.102 = f32[2,64,32,128]{3,2,1,0:T(8,128)S(1)} fusion(f32[2,64,32,128]{3,2,1,0:T(8,128)S(1)} %pad_maximum_fusion.4, f32[128]{0:T(128)S(1)} %get-tuple-element.245, f32[128]{0:T(128)S(1)} %get-tuple-element.246, f32[128]{0:T(128)S(1)} %get-tuple-element.247, f32[128]{0:T(128)S(1)} %get-tuple-element.248, f32[128]{0:T(128)S(1)} %get-tuple-element.249, ...), kind=kLoop, calls=%fused_computation.173 | loop fusion | flops 17301504 | bytes 4203008 | tf_op jit(solution)/shard_map/add | solution.py:55
  53.4 0.1 fusion.149
  53.5 2.4 %collective-permute-start.2 = (f32[2,64,8,128]{3,2,1,0:T(8,128)S(1)}, f32[2,64,8,128]{3,2,1,0:T(8,128)S(1)}, u32[]{:S(2)}, u32[]{:S(2)}) collective-permute-start(f32[2,64,8,128]{3,2,1,0:T(8,128)S(1)} %get-tuple-element.236), channel_id=1, source_target_pairs={{1,0},{2,1},{3,2},{5,4},{6,5},{7,6},{9,8},{10,9},{11,10},{13,12},{... | collective-permute-start | bytes 1572872 | tf_op jit(solution)/shard_map/ppermute | solution.py:19
  55.9 3.5 %collective-permute-start.3 = (f32[2,64,8,128]{3,2,1,0:T(8,128)S(1)}, f32[2,64,8,128]{3,2,1,0:T(8,128)S(1)}, u32[]{:S(2)}, u32[]{:S(2)}) collective-permute-start(f32[2,64,8,128]{3,2,1,0:T(8,128)S(1)} %get-tuple-element.237), channel_id=1, source_target_pairs={{0,1},{1,2},{2,3},{4,5},{5,6},{6,7},{8,9},{9,10},{10,11},{12,13},{... | collective-permute-start | bytes 1572872 | tf_op jit(solution)/shard_map/ppermute | solution.py:17
  59.3 10.2 %collective-permute-done.2 = f32[2,64,8,128]{3,2,1,0:T(8,128)S(1)} collective-permute-done((f32[2,64,8,128]{3,2,1,0:T(8,128)S(1)}, f32[2,64,8,128]{3,2,1,0:T(8,128)S(1)}, u32[]{:S(2)}, u32[]{:S(2)}) %collective-permute-start.2) | collective-permute-done | bytes 524320 | tf_op jit(solution)/shard_map/ppermute | solution.py:19
  69.5 2.1 %collective-permute-done.3 = f32[2,64,8,128]{3,2,1,0:T(8,128)S(1)} collective-permute-done((f32[2,64,8,128]{3,2,1,0:T(8,128)S(1)}, f32[2,64,8,128]{3,2,1,0:T(8,128)S(1)}, u32[]{:S(2)}, u32[]{:S(2)}) %collective-permute-start.3) | collective-permute-done | bytes 524320 | tf_op jit(solution)/shard_map/ppermute | solution.py:17
  71.6 0.0 copy-done.4
  71.6 5.5 %fusion.13 = f32[2,64,32,128]{3,2,1,0:T(8,128)S(1)} fusion(f32[2,64,32,128]{3,2,1,0:T(8,128)S(1)} %fusion.102, f32[2,64,8,128]{3,2,1,0:T(8,128)S(1)} %collective-permute-done.3, f32[2,64,8,128]{3,2,1,0:T(8,128)S(1)} %collective-permute-done.2, f32[128]{0:T(128)S(1)} %get-tuple-element.262, f32[128]{0:T(128)S(1)} %get-tuple-element.263, ...), kind=kLoop, calls=%fused_computation.84 | loop fusion | flops 25690112 | bytes 5251584 | tf_op jit(solution)/shard_map/add | solution.py:109
  77.1 1.5 %slice_bitcast_fusion = (f32[64,32,128]{2,1,0:T(8,128)}, f32[64,32,128]{2,1,0:T(8,128)}) fusion(f32[2,64,32,128]{3,2,1,0:T(8,128)S(1)} %fusion.13), kind=kLoop, calls=%fused_computation.225 | loop fusion | bytes 4194304 | tf_op jit(solution)/shard_map/squeeze | solution.py:111
  (31 shorter events, 0.2 us)
Async XLA Ops:
  0.6 21.4 %copy-start.1 = (f32[64,32,128]{2,1,0:T(8,128)S(1)}, f32[64,32,128]{2,1,0:T(8,128)}, u32[]{:S(2)}) copy-start(f32[64,32,128]{2,1,0:T(8,128)} %param.12) | copy-start | bytes 3145732
  0.6 21.4 %copy-start = (f32[64,32,128]{2,1,0:T(8,128)S(1)}, f32[64,32,128]{2,1,0:T(8,128)}, u32[]{:S(2)}) copy-start(f32[64,32,128]{2,1,0:T(8,128)} %param.13) | copy-start | bytes 3145732
  0.7 8.3 %copy-start.9 = (s32[128]{0:T(128)S(1)}, s32[128]{0:T(128)}, u32[]{:S(2)}) copy-start(s32[128]{0:T(128)} %param.15) | copy-start | bytes 1540
  0.7 8.3 %copy-start.10 = (s32[128]{0:T(128)S(1)}, s32[128]{0:T(128)}, u32[]{:S(2)}) copy-start(s32[128]{0:T(128)} %param.17) | copy-start | bytes 1540
  0.7 8.3 %copy-start.2 = (f32[64,32]{0,1:T(8,128)S(1)}, f32[64,32]{0,1:T(8,128)}, u32[]{:S(2)}) copy-start(f32[64,32]{0,1:T(8,128)} %param.19) | copy-start | bytes 24580
  0.7 8.4 %copy-start.7 = (f32[4,128]{1,0:T(4,128)S(1)}, f32[4,128]{1,0:T(4,128)}, u32[]{:S(2)}) copy-start(f32[4,128]{1,0:T(4,128)} %param.14) | copy-start | bytes 6148
  0.7 8.5 %copy-start.8 = (f32[4,128]{1,0:T(4,128)S(1)}, f32[4,128]{1,0:T(4,128)}, u32[]{:S(2)}) copy-start(f32[4,128]{1,0:T(4,128)} %param.16) | copy-start | bytes 6148
  3.1 15.8 %collective-permute-start = (f32[2,64,8,128]{3,2,1,0:T(8,128)}, f32[2,64,8,128]{3,2,1,0:T(8,128)S(1)}, u32[]{:S(2)}, u32[]{:S(2)}) collective-permute-start(f32[2,64,8,128]{3,2,1,0:T(8,128)} %get-tuple-element.240), channel_id=1, source_target_pairs={{0,1},{1,2},{2,3},{4,5},{5,6},{6,7},{8,9},{9,10},{10,11},{12,13},{... | collective-permute-start | bytes 1572872 | tf_op jit(solution)/shard_map/ppermute | solution.py:17
  6.6 15.5 %collective-permute-start.1 = (f32[2,64,8,128]{3,2,1,0:T(8,128)}, f32[2,64,8,128]{3,2,1,0:T(8,128)S(1)}, u32[]{:S(2)}, u32[]{:S(2)}) collective-permute-start(f32[2,64,8,128]{3,2,1,0:T(8,128)} %get-tuple-element.241), channel_id=1, source_target_pairs={{1,0},{2,1},{3,2},{5,4},{6,5},{7,6},{9,8},{10,9},{11,10},{13,12},{... | collective-permute-start | bytes 1572872 | tf_op jit(solution)/shard_map/ppermute | solution.py:19
  9.2 13.2 %copy-start.3 = (f32[128]{0:T(128)}, f32[128]{0:T(128)S(1)}, u32[]{:S(2)}) copy-start(f32[128]{0:T(128)S(1)} %get-tuple-element.276) | copy-start | bytes 1540
  9.2 13.2 %copy-start.5 = (f32[128]{0:T(128)}, f32[128]{0:T(128)S(1)}, u32[]{:S(2)}) copy-start(f32[128]{0:T(128)S(1)} %get-tuple-element.277) | copy-start | bytes 1540
  26.8 5.8 %copy-start.11 = (f32[128]{0:T(128)S(1)}, f32[128]{0:T(128)}, u32[]{:S(2)}) copy-start(f32[128]{0:T(128)} %param.18) | copy-start | bytes 1540
  53.4 18.3 %copy-start.4 = (f32[128]{0:T(128)S(1)}, f32[128]{0:T(128)}, u32[]{:S(2)}) copy-start(f32[128]{0:T(128)} %copy-done.3) | copy-start | bytes 1540
  53.4 18.3 %copy-start.6 = (f32[128]{0:T(128)S(1)}, f32[128]{0:T(128)}, u32[]{:S(2)}) copy-start(f32[128]{0:T(128)} %copy-done.5) | copy-start | bytes 1540
  53.5 16.1 %collective-permute-start.2 = (f32[2,64,8,128]{3,2,1,0:T(8,128)S(1)}, f32[2,64,8,128]{3,2,1,0:T(8,128)S(1)}, u32[]{:S(2)}, u32[]{:S(2)}) collective-permute-start(f32[2,64,8,128]{3,2,1,0:T(8,128)S(1)} %get-tuple-element.236), channel_id=1, source_target_pairs={{1,0},{2,1},{3,2},{5,4},{6,5},{7,6},{9,8},{10,9},{11,10},{13,12},{... | collective-permute-start | bytes 1572872 | tf_op jit(solution)/shard_map/ppermute | solution.py:19
  55.9 15.8 %collective-permute-start.3 = (f32[2,64,8,128]{3,2,1,0:T(8,128)S(1)}, f32[2,64,8,128]{3,2,1,0:T(8,128)S(1)}, u32[]{:S(2)}, u32[]{:S(2)}) collective-permute-start(f32[2,64,8,128]{3,2,1,0:T(8,128)S(1)} %get-tuple-element.237), channel_id=1, source_target_pairs={{0,1},{1,2},{2,3},{4,5},{5,6},{6,7},{8,9},{9,10},{10,11},{12,13},{... | collective-permute-start | bytes 1572872 | tf_op jit(solution)/shard_map/ppermute | solution.py:17
where the time goes:
time: 79.4 us; the launch traced here: 78.6 us
  other arithmetic  25.1 us (32%)
  waiting for transfers between devices  25.1 us (32%)
  starting transfers between devices  11.7 us (15%)
  blocking collectives  10.5 us (13%)
  matrix products  2.77 us (3%)
  local copies, waits for them, and re-layouts  2.37 us (3%)
  between operations  0.97 us (1%)
    ppermute x2, waiting for transfers between devices, with_halo(): lax.ppermute(head, axis, [((i + 1) % count, i) for i in range(ends)])  13.4 us
    ppermute x2, waiting for transfers between devices, with_halo(): lax.ppermute(tail, axis, [(i, (i + 1) % count) for i in range(ends)])  11.7 us
    add x2, other arithmetic, row_pass(): total = total + row_coefficient[offset] * padded[:, begin:begin + length]  11.5 us
    all_gather x2, blocking collectives, entering(): pieces = lax.all_gather(value, axis)  10.5 us
    ppermute x2, starting transfers between devices, with_halo(): lax.ppermute(tail, axis, [(i, (i + 1) % count) for i in range(ends)])  6.93 us
    add x1, other arithmetic, on_device(): gradients + coefficient[offset] * grad_extended[:, :, begin:begin + colum...  5.49 us
    ppermute x2, starting transfers between devices, with_halo(): lax.ppermute(head, axis, [((i + 1) % count, i) for i in range(ends)])  4.77 us
    add x1, other arithmetic, on_device(): sampled + coefficient[offset] * extended[:, :, offset:offset + columns, :]  4.39 us
  transfers between devices with their start and end apart: 4, of which 4 were waited for; matrix products, arithmetic and copies ran while one was open for 0% of the time, Pallas kernels for 0%

commit v1 on v0

v1 whole, which is shorter than its diff:
```python
import functools

import jax
import jax.numpy as jnp
from jax import lax
from jax.experimental import pallas as pl
from jax.experimental.pallas import tpu as pltpu
from jax.sharding import PartitionSpec as P

HALO = 8
REACH = 6
SUB = 8
F32 = jnp.float32
BF16 = jnp.bfloat16
VMEM_LIMIT = 48 * 1024 * 1024


def bits_of(shift):
    moved = jnp.broadcast_to(shift, (SUB, shift.shape[-1])) + REACH
    return {b: (moved & b) != 0 for b in (8, 4, 2, 1)}


def rows_of(taps):
    return [jnp.broadcast_to(taps[k : k + 1, :], (SUB, taps.shape[-1])) for k in range(4)]


def choose(mask, yes, no):
    if yes is None and no is None:
        return None
    if yes is None:
        return jnp.where(mask, 0.0, no)
    if no is None:
        return jnp.where(mask, yes, 0.0)
    return jnp.where(mask, yes, no)


def resample(get, bits, taps, count, flipped):
    way = -1 if flipped else 1
    memo = {}

    def stage(b, i):
        if b == 16:
            key = (b, i)
            if key not in memo:
                memo[key] = get(i)
            return memo[key]
        key = (b, i)
        if key not in memo:
            memo[key] = choose(bits[b], stage(2 * b, i + way * b), stage(2 * b, i))
        return memo[key]

    for i in range(count):
        total = None
        for k in range(4):
            v = stage(1, i + 7 - k if flipped else i - 7 + k)
            if v is not None:
                total = taps[k] * v if total is None else total + taps[k] * v
        yield i, total


def halves(x):
    hi = x.astype(BF16)
    lo = (x - hi.astype(F32)).astype(BF16)
    return jnp.concatenate([hi, lo], axis=1)


def scan_matrix(planes, before):
    a = lax.broadcasted_iota(jnp.int32, (2 * planes, 2 * planes), 0)
    b = lax.broadcasted_iota(jnp.int32, (2 * planes, 2 * planes), 1)
    a = jnp.where(a >= planes, a - planes, a)
    ordered = (a < b) if before else (a > b)
    return jnp.where((b >= planes) | ordered, 1.0, 0.0).astype(BF16)


def edge_kernel(odd_ref, d_ref, e_ref, da, db, ea, eb, sems):
    columns = d_ref.shape[1]
    odd = odd_ref[0]
    first = pl.multiple_of(jnp.where(odd == 1, 0, columns - HALO), HALO)
    second = pl.multiple_of(jnp.where(odd == 1, columns - HALO, 0), HALO)
    copies = [
        pltpu.make_async_copy(ref.at[:, pl.ds(at, HALO), :], out, sems.at[n])
        for n, (ref, at, out) in enumerate(
            ((d_ref, first, da), (d_ref, second, db), (e_ref, first, ea), (e_ref, second, eb))
        )
    ]
    for c in copies:
        c.start()
    for c in copies:
        c.wait()


def row_kernel(d_ref, e_ref, taps_ref, shift_ref, rd_ref, re_ref):
    rows, columns, planes = d_ref.shape
    bits = bits_of(shift_ref[...])
    taps = rows_of(taps_ref[...])

    def body(t, carry):
        at = pl.multiple_of(t * SUB, SUB)
        for ref, out in ((d_ref, rd_ref), (e_ref, re_ref)):
            get = lambda y: ref[y, pl.ds(at, SUB), :] if 0 <= y < rows else None
            for y, v in resample(get, bits, taps, rows, False):
                out[pl.ds(pl.multiple_of(y * columns + at, SUB), SUB), :] = v
        return carry

    lax.fori_loop(0, columns // SUB, body, 0)


def row_halo(odd, a_ref, b_ref, halo_ref, bits, taps):
    rows = a_ref.shape[0]
    for side in range(2):
        use_a = odd == (1 - side)
        get = lambda y: jnp.where(use_a, a_ref[y], b_ref[y]) if 0 <= y < rows else None
        for y, v in resample(get, bits, taps, rows, False):
            halo_ref[pl.ds(y * 2 * HALO + side * HALO, SUB), :] = v


def column_get(r_ref, halo_ref, y0, columns):
    def get(x):
        if x < -HALO or x >= columns + HALO:
            return None
        if x < 0:
            return halo_ref[pl.ds(y0 * 2 * HALO + x + HALO, SUB, stride=2 * HALO), :]
        if x >= columns:
            return halo_ref[pl.ds(y0 * 2 * HALO + HALO + x - columns, SUB, stride=2 * HALO), :]
        return r_ref[pl.ds(y0 * columns + x, SUB, stride=columns), :]

    return get


def pack_totals(totals, dense_ref, group, columns):
    lane = lax.broadcasted_iota(jnp.int32, (SUB, 128), 1)
    per = 128 // columns
    packed = jnp.zeros((SUB, 128), F32)
    base = (group % per) * columns
    for x in range(columns):
        packed = jnp.where(lane == base + x, totals[x * SUB : (x + 1) * SUB, :], packed)
    dense_ref[group // per] += packed


def edges_out(odd, ref, a_ref, b_ref):
    columns = ref.shape[0]
    first = jnp.where(odd == 1, 0, columns - HALO)
    second = jnp.where(odd == 1, columns - HALO, 0)
    a_ref[...] = ref[pl.ds(first, HALO)]
    b_ref[...] = ref[pl.ds(second, HALO)]


def density_kernel(
    odd_ref, rd_ref, a_ref, b_ref, row_taps_ref, row_shift_ref, taps_ref, shift_ref, scale_ref,
    q_ref, n_ref, qa_ref, qb_ref, dense_ref, halo_ref,
):
    odd = odd_ref[0]
    columns, rows, planes = q_ref.shape
    row_halo(odd, a_ref, b_ref, halo_ref, bits_of(row_shift_ref[...]), rows_of(row_taps_ref[...]))
    bits = bits_of(shift_ref[...])
    taps = rows_of(taps_ref[...])
    scale = jnp.broadcast_to(scale_ref[...], (SUB, planes))
    matrix = scan_matrix(planes, True)
    dense_ref[...] = jnp.zeros_like(dense_ref)

    def body(group, carry):
        y0 = group * SUB
        get = column_get(rd_ref, halo_ref, y0, columns)
        pieces = [scale * v for _, v in resample(get, bits, taps, columns, False)]
        optical = jnp.concatenate(pieces, axis=0)
        sums = jnp.dot(halves(optical), matrix, preferred_element_type=F32)
        transmit = jnp.exp(-sums[:, :planes])
        series = optical * (1.0 - optical * (1 / 2) * (1.0 - optical * (1 / 3) * (1.0 - optical * (1 / 4) * (
            1.0 - optical * (1 / 5) * (1.0 - optical * (1 / 6))))))
        alpha = jnp.where(optical < 0.25, series, 1.0 - jnp.exp(-optical))
        q = transmit * alpha
        n = transmit - q
        at = pl.multiple_of(y0, SUB)
        for x in range(columns):
            q_ref[x, pl.ds(at, SUB), :] = q[x * SUB : (x + 1) * SUB]
            n_ref[x, pl.ds(at, SUB), :] = n[x * SUB : (x + 1) * SUB]
        pack_totals(sums[:, planes:], dense_ref, group, columns)
        return carry

    lax.fori_loop(0, rows // SUB, body, 0)
    edges_out(odd, q_ref, qa_ref, qb_ref)


def emission_kernel(
    odd_ref, re_ref, a_ref, b_ref, q_ref, n_ref, row_taps_ref, row_shift_ref, taps_ref, shift_ref, scale_ref,
    p_ref, pa_ref, pb_ref, dense_ref, halo_ref,
):
    odd = odd_ref[0]
    columns, rows, planes = p_ref.shape
    row_halo(odd, a_ref, b_ref, halo_ref, bits_of(row_shift_ref[...]), rows_of(row_taps_ref[...]))
    bits = bits_of(shift_ref[...])
    taps = rows_of(taps_ref[...])
    scale = jnp.broadcast_to(scale_ref[...], (SUB, planes))
    matrix = scan_matrix(planes, False)
    dense_ref[...] = jnp.zeros_like(dense_ref)

    def body(group, carry):
        y0 = group * SUB
        at = pl.multiple_of(y0, SUB)
        get = column_get(re_ref, halo_ref, y0, columns)
        pieces = [v for _, v in resample(get, bits, taps, columns, False)]
        light = jnp.concatenate([q_ref[x, pl.ds(at, SUB), :] * pieces[x] for x in range(columns)], axis=0)
        sums = jnp.dot(halves(light), matrix, preferred_element_type=F32)
        for x in range(columns):
            behind = sums[x * SUB : (x + 1) * SUB, :planes]
            p_ref[x, pl.ds(at, SUB), :] = scale * (n_ref[x, pl.ds(at, SUB), :] * pieces[x] - behind)
        pack_totals(sums[:, planes:], dense_ref, group, columns)
        return carry

    lax.fori_loop(0, rows // SUB, body, 0)
    edges_out(odd, p_ref, pa_ref, pb_ref)


def join_kernel(count, mine_ref, weight_ref, *refs):
    out_ref = refs[-1]
    mine = mine_ref[0]
    weight = weight_ref[...]
    own = refs[0]
    front = jnp.zeros_like(weight)
    for ahead in range(1, count):
        front += jnp.where(mine + ahead >= count, refs[ahead][0], 0.0)
    running = front + own[0]
    back = jnp.zeros_like(weight)
    for ahead in range(1, count):
        there = mine + ahead < count
        back += jnp.where(there, jnp.exp(-running) * refs[ahead][1], 0.0)
        running += jnp.where(there, refs[ahead][0], 0.0)
    out_ref[0] = weight * jnp.exp(-front)
    out_ref[1] = weight * back


def spread(dense, base, columns, first, last):
    lane = lax.broadcasted_iota(jnp.int32, (SUB, 128), 1)
    wanted = jnp.concatenate(
        [jnp.where(lane == base + x, dense, 0.0) for x in range(first, last)], axis=0
    )
    ones = jnp.ones((256, 128), BF16)
    return jnp.dot(halves(wanted), ones, preferred_element_type=F32)


def final_kernel(
    odd_ref, p_ref, q_ref, pa_ref, pb_ref, qa_ref, qb_ref, own_ref, wa_ref, wb_ref,
    row_taps_ref, row_shift_ref, taps_ref, shift_ref, scale_ref,
    gd_ref, ge_ref, cd_ref, ce_ref,
):
    odd = odd_ref[0]
    columns, rows, planes = p_ref.shape
    per = 128 // columns
    bits = bits_of(shift_ref[...])
    taps = rows_of(taps_ref[...])
    scale = jnp.broadcast_to(scale_ref[...], (SUB, planes))

    def body(group, carry):
        y0 = group * SUB
        at = pl.multiple_of(y0, SUB)
        chunk = group // per
        base = (group % per) * columns
        left_a = odd == 1
        left_w = [jnp.where(left_a, wa_ref[f, chunk], wb_ref[f, chunk]) for f in range(2)]
        right_w = [jnp.where(left_a, wb_ref[f, chunk], wa_ref[f, chunk]) for f in range(2)]
        own = [spread(own_ref[f, chunk], base, columns, 0, columns) for f in range(2)]
        left = [spread(left_w[f], base, columns, columns - HALO, columns) for f in range(2)]
        right = [spread(right_w[f], base, columns, 0, HALO) for f in range(2)]

        def weights(x):
            if x < 0:
                return [w[(x + HALO) * SUB : (x + HALO + 1) * SUB] for w in left]
            if x >= columns:
                return [w[(x - columns) * SUB : (x - columns + 1) * SUB] for w in right]
            return [w[x * SUB : (x + 1) * SUB] for w in own]

        def local(ref, ra, rb, x):
            if x < 0:
                return jnp.where(left_a, ra[x + HALO, pl.ds(at, SUB), :], rb[x + HALO, pl.ds(at, SUB), :])
            if x >= columns:
                return jnp.where(left_a, rb[x - columns, pl.ds(at, SUB), :], ra[x - columns, pl.ds(at, SUB), :])
            return ref[x, pl.ds(at, SUB), :]

        def get_d(x):
            if x < -HALO or x >= columns + HALO:
                return None
            f, b = weights(x)
            return f * local(p_ref, pa_ref, pb_ref, x) - b * scale

        def get_e(x):
            if x < -HALO or x >= columns + HALO:
                return None
            return weights(x)[0] * local(q_ref, qa_ref, qb_ref, x)

        for get, out in ((get_d, cd_ref), (get_e, ce_ref)):
            for x, v in resample(get, bits, taps, columns, True):
                out[pl.ds(y0 * columns + x, SUB, stride=columns), :] = v
        return carry

    lax.fori_loop(0, rows // SUB, body, 0)
    row_bits = bits_of(row_shift_ref[...])
    row_taps = rows_of(row_taps_ref[...])

    def row_body(t, carry):
        at = pl.multiple_of(t * SUB, SUB)
        for ref, out in ((cd_ref, gd_ref), (ce_ref, ge_ref)):
            get = lambda y: ref[pl.ds(pl.multiple_of(y * columns + at, SUB), SUB), :] if 0 <= y < rows else None
            for y, v in resample(get, row_bits, row_taps, rows, True):
                out[y, pl.ds(at, SUB), :] = v
        return carry

    lax.fori_loop(0, columns // SUB, row_body, 0)


def call(kernel, outs, scalars, vmem, scratch=(), anywhere=False, micros=2.0):
    space = pl.ANY if anywhere else pltpu.VMEM
    return pl.pallas_call(
        kernel,
        out_shape=[jax.ShapeDtypeStruct(s, F32) for s in outs],
        in_specs=[pl.BlockSpec(memory_space=pltpu.SMEM)] * len(scalars)
        + [pl.BlockSpec(memory_space=space)] * len(vmem),
        out_specs=[pl.BlockSpec(memory_space=space)] * len(outs),
        scratch_shapes=list(scratch),
        compiler_params=pltpu.CompilerParams(vmem_limit_bytes=VMEM_LIMIT),
        cost_estimate=pl.CostEstimate(
            flops=int(micros * 1e6), bytes_accessed=int(micros * 3.0e6), transcendentals=0
        ),
    )(*scalars, *vmem)


def swap(value, axis, parity):
    count = lax.axis_size(axis)
    pairs = []
    for i in range(parity, count - 1, 2):
        pairs += [(i, i + 1), (i + 1, i)]
    return lax.ppermute(value, axis, pairs)


def on_device(density, emission, taps, shift, row_taps, row_shift, step_length, cotangent):
    rows, columns, planes = density.shape
    slabs = lax.axis_size("depth")
    all_planes = planes * slabs
    per = 128 // columns
    chunks = rows // SUB // per
    shift, row_shift = shift[None, :], row_shift[None, :]
    scale = step_length[None, :] / all_planes
    odd = (lax.axis_index("screen") % 2).astype(jnp.int32)[None]
    mine = lax.axis_index("depth").astype(jnp.int32)[None]
    weight = cotangent.reshape(chunks, per, SUB, columns).transpose(0, 2, 1, 3).reshape(chunks, SUB, 128)

    edge = (rows, HALO, planes)
    da, db, ea, eb = call(
        edge_kernel, [edge] * 4, [odd], [density, emission], [pltpu.SemaphoreType.DMA((4,))], anywhere=True
    )
    da, db = swap(da, "screen", 0), swap(db, "screen", 1)
    ea, eb = swap(ea, "screen", 0), swap(eb, "screen", 1)
    flat = (rows * columns, planes)
    rd, re = call(row_kernel, [flat, flat], [], [density, emission, row_taps, row_shift])

    cells = (columns, rows, planes)
    side = (HALO, rows, planes)
    dense = (chunks, SUB, 128)
    halo = pltpu.VMEM((rows * 2 * HALO, planes), F32)
    q, n, qa, qb, slab_optical = call(
        density_kernel,
        [cells, cells, side, side, dense],
        [odd],
        [rd, da, db, row_taps, row_shift, taps, shift, scale],
        [halo],
    )
    qa, qb = swap(qa, "screen", 0), swap(qb, "screen", 1)
    p, pa, pb, slab_light = call(
        emission_kernel,
        [cells, side, side, dense],
        [odd],
        [re, ea, eb, q, n, row_taps, row_shift, taps, shift, scale],
        [halo],
    )
    pa, pb = swap(pa, "screen", 0), swap(pb, "screen", 1)
    sums = jnp.stack([slab_optical, slab_light])
    ahead = [sums] + [
        lax.ppermute(sums, "depth", [((i + e) % slabs, i) for i in range(slabs)]) for e in range(1, slabs)
    ]
    (own,) = call(
        functools.partial(join_kernel, slabs), [(2,) + dense], [mine], [weight] + ahead, micros=0.3
    )
    wa, wb = swap(own, "screen", 0), swap(own, "screen", 1)
    gd, ge = call(
        final_kernel,
        [density.shape, density.shape],
        [odd],
        [p, q, pa, pb, qa, qb, own, wa, wb, row_taps, row_shift, taps, shift, scale],
        [pltpu.VMEM(flat, F32), pltpu.VMEM(flat, F32)],
        micros=4.0,
    )
    return gd, ge


def solution(mesh):
    in_specs = (
        P("groups", "screen", "depth"),
        P("groups", "screen", "depth"),
        P("groups", "depth"),
        P(("groups", "depth")),
        P("groups", "depth"),
        P(("groups", "depth")),
        P(("groups", "depth")),
        P("groups", "screen"),
    )
    out_specs = (P("groups", "screen", "depth"), P("groups", "screen", "depth"))
    return jax.shard_map(
        on_device, mesh=mesh, in_specs=in_specs, out_specs=out_specs, check_vma=False
    )
```

time: 79.4 us -> 54.1 us (0.68)
  other arithmetic: 25.1 us -> 0.01 us
  Pallas kernels: 0 us -> 13.5 us
  blocking collectives: 10.5 us -> 0 us
  waiting for transfers between devices: 25.1 us -> 17.4 us
  starting transfers between devices: 11.7 us -> 17.3 us
  matrix products: 2.77 us -> 0 us
  local copies, waits for them, and re-layouts: 2.37 us -> 4.66 us
    add x6 -> x0, other arithmetic: 21.4 us -> none  [the longest x2 11.5 us: row_pass(): total = total + row_coefficient[offset] * padded[:, begin:begin + length]]
    pallas_call x0 -> x6, Pallas kernels: none -> 13.5 us  [call(): pl.pallas_call(kernel, out_shape=[jax.ShapeDtypeStruct(s, F32) for s in o...]
    all_gather x2 -> x0, blocking collectives: 10.5 us -> none  [entering(): pieces = lax.all_gather(value, axis)]
    ppermute x4 -> x13, waiting for transfers between devices: 25.1 us -> 17.4 us  [the longest x10 11.1 us: swap(): return lax.ppermute(value, axis, pairs)]
    ppermute x4 -> x13, starting transfers between devices: 11.7 us -> 17.3 us  [the longest x10 16.7 us: swap(): return lax.ppermute(value, axis, pairs)]
    unnamed x27 -> x17, local copies, waits for them, and re-layouts: 0.26 us -> 3.81 us
    another operation x3 -> x1, other arithmetic: 3.26 us -> 0.01 us  [on_device(): sums = jnp.stack([slab_optical, slab_light])]
    dot_general x2 -> x0, matrix products: 2.77 us -> none  [the longest x1 1.58 us: on_device(): jnp.einsum('yxa,ab->yxb', light, upper_ones, precision=lax.Precision.HIGH...]
  transfers between devices with their start and end apart: 4 -> 13, of which waited for: 4 -> 8; matrix products, arithmetic and copies ran while one was open for 0% -> 3% of each run, Pallas kernels for 0% -> 7%
where the time goes in v1:
time: 54.1 us; the launch traced here: 53.8 us
  waiting for transfers between devices  17.4 us (32%)
  starting transfers between devices  17.3 us (32%)
  Pallas kernels  13.5 us (25%)
  local copies, waits for them, and re-layouts  4.66 us (9%)
  between operations  0.85 us (2%)
    ppermute x10, starting transfers between devices, swap(): return lax.ppermute(value, axis, pairs)  16.7 us
    pallas_call x6, Pallas kernels, call(): pl.pallas_call(kernel, out_shape=[jax.ShapeDtypeStruct(s, F32) for s in o...  13.5 us
    ppermute x10, waiting for transfers between devices, swap(): return lax.ppermute(value, axis, pairs)  11.1 us
    ppermute x3, waiting for transfers between devices, on_device(): lax.ppermute(sums, 'depth', [((i + e) % slabs, i) for i in range(slabs)])  6.38 us
    unnamed x17, local copies, waits for them, and re-layouts  3.81 us
  transfers between devices with their start and end apart: 13, of which 8 were waited for; matrix products, arithmetic and copies ran while one was open for 3% of the time, Pallas kernels for 7%

profile of v1, /device:TPU:14, one launch (start us, length us, event | category | flops | bytes accessed | tf_op | source)
XLA Modules:
  0.0 53.8 jit_solution(13232895608443507159)
XLA Ops:
  0.6 0.0 copy-start
  0.7 1.2 %copy-done = f32[64,32,128]{2,1,0:T(8,128)S(1)} copy-done((f32[64,32,128]{2,1,0:T(8,128)S(1)}, f32[64,32,128]{2,1,0:T(8,128)}, u32[]{:S(2)}) %copy-start) | copy-done | bytes 1048600
  1.9 1.2 %copy-done.1 = f32[64,32,128]{2,1,0:T(8,128)S(1)} copy-done((f32[64,32,128]{2,1,0:T(8,128)S(1)}, f32[64,32,128]{2,1,0:T(8,128)}, u32[]{:S(2)}) %copy-start.1) | copy-done | bytes 1048600
  3.1 0.2 shard_map.96
  3.3 0.5 collective-permute-start.2
  3.8 4.6 %collective-permute-start.3 = (f32[64,8,128]{2,1,0:T(8,128)S(1)}, f32[64,8,128]{2,1,0:T(8,128)S(1)}, u32[]{:S(2)}, u32[]{:S(2)}) collective-permute-start(f32[64,8,128]{2,1,0:T(8,128)S(1)} %get-tuple-element.22), channel_id=1, source_target_pairs={{1,2},{2,1},{5,6},{6,5},{9,10},{10,9},{13,14},{14,13},{17,18},{18,... | collective-permute-start | bytes 786440 | tf_op jit(solution)/shard_map/ppermute | solution.py:331
  8.4 0.0 copy-start.2
  8.4 0.1 collective-permute-start
  8.5 0.0 copy-start.4
  8.5 1.9 %collective-permute-start.1 = (f32[64,8,128]{2,1,0:T(8,128)S(1)}, f32[64,8,128]{2,1,0:T(8,128)S(1)}, u32[]{:S(2)}, u32[]{:S(2)}) collective-permute-start(f32[64,8,128]{2,1,0:T(8,128)S(1)} %get-tuple-element.19), channel_id=1, source_target_pairs={{1,2},{2,1},{5,6},{6,5},{9,10},{10,9},{13,14},{14,13},{17,18},{18,... | collective-permute-start | bytes 786440 | tf_op jit(solution)/shard_map/ppermute | solution.py:331
  10.4 0.0 copy-done.2
  10.4 0.0 copy-done.4
  10.5 0.0 copy-start.7
  10.5 0.8 %shard_map.95 = (f32[2048,128]{1,0:T(8,128)S(1)}, f32[2048,128]{1,0:T(8,128)S(1)}) custom-call(f32[64,32,128]{2,1,0:T(8,128)S(1)} %copy-done, f32[64,32,128]{2,1,0:T(8,128)S(1)} %copy-done.1, f32[4,128]{1,0:T(4,128)S(1)} %copy-done.2, s32[1,128]{1,0:T(1,128)S(1)} %bitcast.13), custom_call_target="tpu_custom_call" | custom-call | flops 2000000 | bytes 6000000 | tf_op jit(solution)/shard_map/pallas_call | solution.py:312
  11.3 0.0 copy-done.7
  11.3 0.0 copy-start.3
  11.3 1.1 %collective-permute-done.2.a_ref = f32[64,8,128]{2,1,0:T(8,128)S(1)} collective-permute-done((f32[64,8,128]{2,1,0:T(8,128)S(1)}, f32[64,8,128]{2,1,0:T(8,128)S(1)}, u32[]{:S(2)}, u32[]{:S(2)}) %collective-permute-start.2) | collective-permute-done | bytes 262176 | tf_op jit(solution)/shard_map/ppermute | solution.py:331
  12.4 3.2 %collective-permute-done.3.b_ref = f32[64,8,128]{2,1,0:T(8,128)S(1)} collective-permute-done((f32[64,8,128]{2,1,0:T(8,128)S(1)}, f32[64,8,128]{2,1,0:T(8,128)S(1)}, u32[]{:S(2)}, u32[]{:S(2)}) %collective-permute-start.3) | collective-permute-done | bytes 262176 | tf_op jit(solution)/shard_map/ppermute | solution.py:331
  15.6 0.0 copy-done.3
  15.6 0.7 %copy-done.5 = s32[128]{0:T(128)S(1)} copy-done((s32[128]{0:T(128)S(1)}, s32[128]{0:T(128)}, u32[]{:S(2)}) %copy-start.5) | copy-done | bytes 536
  16.2 3.2 %shard_map.97 = (f32[32,64,128]{2,1,0:T(8,128)S(1)}, f32[32,64,128]{2,1,0:T(8,128)S(1)}, f32[8,64,128]{2,1,0:T(8,128)}, f32[8,64,128]{2,1,0:T(8,128)S(1)}, f32[2,8,128]{2,1,0:T(8,128)S(1)}) custom-call(s32[1]{0:T(128)} %bitcast.odd_ref, f32[2048,128]{1,0:T(8,128)S(1)} %get-tuple-element.20.rd_ref, f32[64,8,128]{2,1,0:T(8,128)S(1)} %collective-permute-done.2.a_ref, ...), custom_call_target="tpu_custom_call" | custom-call | flops 2000000 | bytes 6000000 | tf_op jit(solution)/shard_map/pallas_call | solution.py:312
  19.4 0.0 collective-permute-done.a_ref
  19.4 0.6 %collective-permute-done.1.b_ref = f32[64,8,128]{2,1,0:T(8,128)S(1)} collective-permute-done((f32[64,8,128]{2,1,0:T(8,128)S(1)}, f32[64,8,128]{2,1,0:T(8,128)S(1)}, u32[]{:S(2)}, u32[]{:S(2)}) %collective-permute-start.1) | collective-permute-done | bytes 262176 | tf_op jit(solution)/shard_map/ppermute | solution.py:331
  20.0 3.2 %shard_map.98 = (f32[32,64,128]{2,1,0:T(8,128)S(1)}, f32[8,64,128]{2,1,0:T(8,128)}, f32[8,64,128]{2,1,0:T(8,128)}, f32[2,8,128]{2,1,0:T(8,128)S(1)}) custom-call(s32[1]{0:T(128)} %bitcast.odd_ref, f32[2048,128]{1,0:T(8,128)S(1)} %get-tuple-element.17.re_ref, f32[64,8,128]{2,1,0:T(8,128)S(1)} %collective-permute-done.a_ref, ...), custom_call_target="tpu_custom_call" | custom-call | flops 2000000 | bytes 6000000 | tf_op jit(solution)/shard_map/pallas_call | solution.py:312
  23.3 0.0 collective-permute-start.4
  23.3 3.6 %collective-permute-start.5 = (f32[8,64,128]{2,1,0:T(8,128)}, f32[8,64,128]{2,1,0:T(8,128)S(1)}, u32[]{:S(2)}, u32[]{:S(2)}) collective-permute-start(f32[8,64,128]{2,1,0:T(8,128)} %get-tuple-element.27), channel_id=1, source_target_pairs={{1,2},{2,1},{5,6},{6,5},{9,10},{10,9},{13,14},{14,13},{17,18},{18,... | collective-permute-start | bytes 786440 | tf_op jit(solution)/shard_map/ppermute | solution.py:331
  26.9 0.1 collective-permute-start.6
  27.0 2.7 %collective-permute-start.7 = (f32[8,64,128]{2,1,0:T(8,128)S(1)}, f32[8,64,128]{2,1,0:T(8,128)S(1)}, u32[]{:S(2)}, u32[]{:S(2)}) collective-permute-start(f32[8,64,128]{2,1,0:T(8,128)S(1)} %get-tuple-element.29), channel_id=1, source_target_pairs={{1,2},{2,1},{5,6},{6,5},{9,10},{10,9},{13,14},{14,13},{17,18},{18,... | collective-permute-start | bytes 786440 | tf_op jit(solution)/shard_map/ppermute | solution.py:331
  29.7 0.0 copy-start.6
  29.7 0.1 collective-permute-start.10
  29.8 3.2 %collective-permute-done.10.refs_3_ = f32[2,2,8,128]{3,2,1,0:T(8,128)S(1)} collective-permute-done((f32[2,2,8,128]{3,2,1,0:T(8,128)S(1)}, f32[2,2,8,128]{3,2,1,0:T(8,128)S(1)}, u32[]{:S(2)}, u32[]{:S(2)}) %collective-permute-start.10) | collective-permute-done | bytes 16416 | tf_op jit(solution)/shard_map/ppermute | solution.py:377
  32.9 0.0 collective-permute-start.8
  32.9 1.4 %collective-permute-done.8.refs_1_ = f32[2,2,8,128]{3,2,1,0:T(8,128)S(1)} collective-permute-done((f32[2,2,8,128]{3,2,1,0:T(8,128)S(1)}, f32[2,2,8,128]{3,2,1,0:T(8,128)S(1)}, u32[]{:S(2)}, u32[]{:S(2)}) %collective-permute-start.8) | collective-permute-done | bytes 16416 | tf_op jit(solution)/shard_map/ppermute | solution.py:377
  34.4 0.5 collective-permute-start.9
  34.9 0.0 copy-done.6
  34.9 0.7 %copy.11 = f32[64,32]{1,0:T(8,128)} copy(f32[64,32]{0,1:T(8,128)S(1)} %copy-done.6) | data formatting | bytes 16384 | tf_op args[7]
  35.6 0.8 %copy.12 = f32[2,8,4,32]{3,2,1,0:T(4,128)S(1)} copy(f32[2,8,4,32]{3,1,2,0:T(8,128)} %bitcast.20) | data formatting | bytes 16384 | tf_op jit(solution)/shard_map/transpose | solution.py:344
  36.4 0.1 reshape.12.weight_ref
  36.5 1.8 %collective-permute-done.9.refs_2_ = f32[2,2,8,128]{3,2,1,0:T(8,128)S(1)} collective-permute-done((f32[2,2,8,128]{3,2,1,0:T(8,128)S(1)}, f32[2,2,8,128]{3,2,1,0:T(8,128)S(1)}, u32[]{:S(2)}, u32[]{:S(2)}) %collective-permute-start.9) | collective-permute-done | bytes 16416 | tf_op jit(solution)/shard_map/ppermute | solution.py:377
  38.3 0.1 collective-permute-start.11
  38.3 3.7 %collective-permute-done.11.wa_ref = f32[2,2,8,128]{3,2,1,0:T(8,128)S(1)} collective-permute-done((f32[2,2,8,128]{3,2,1,0:T(8,128)S(1)}, f32[2,2,8,128]{3,2,1,0:T(8,128)S(1)}, u32[]{:S(2)}, u32[]{:S(2)}) %collective-permute-start.11) | collective-permute-done | bytes 16416 | tf_op jit(solution)/shard_map/ppermute | solution.py:331
  42.1 3.2 %collective-permute-start.12 = (f32[2,2,8,128]{3,2,1,0:T(8,128)S(1)}, f32[2,2,8,128]{3,2,1,0:T(8,128)S(1)}, u32[]{:S(2)}, u32[]{:S(2)}) collective-permute-start(f32[2,2,8,128]{3,2,1,0:T(8,128)S(1)} %shard_map.99.own_ref), channel_id=1, source_target_pairs={{1,2},{2,1},{5,6},{6,5},{9,10},{10,9},{13,14},{14,13},{17,18},{18,... | collective-permute-start | bytes 49160 | tf_op jit(solution)/shard_map/ppermute | solution.py:331
  45.2 2.5 %collective-permute-done.12.wb_ref = f32[2,2,8,128]{3,2,1,0:T(8,128)S(1)} collective-permute-done((f32[2,2,8,128]{3,2,1,0:T(8,128)S(1)}, f32[2,2,8,128]{3,2,1,0:T(8,128)S(1)}, u32[]{:S(2)}, u32[]{:S(2)}) %collective-permute-start.12) | collective-permute-done | bytes 16416 | tf_op jit(solution)/shard_map/ppermute | solution.py:331
  47.7 0.0 collective-permute-done.4.pa_ref
  47.7 0.0 collective-permute-done.5.pb_ref
  47.7 0.0 collective-permute-done.6.qa_ref
  47.7 0.0 collective-permute-done.7.qb_ref
  47.7 6.0 %shard_map.100 = (f32[64,32,128]{2,1,0:T(8,128)}, f32[64,32,128]{2,1,0:T(8,128)}) custom-call(s32[1]{0:T(128)} %bitcast.odd_ref, f32[32,64,128]{2,1,0:T(8,128)S(1)} %get-tuple-element.25.p_ref, f32[32,64,128]{2,1,0:T(8,128)S(1)} %get-tuple-element.23.q_ref, f32[8,64,128]{2,1,0:T(8,128)S(1)} %collective-permute-done.4.pa_ref, ...), custom_call_target="tpu_custom_call" | custom-call | flops 4000000 | bytes 12000000 | tf_op jit(solution)/shard_map/pallas_call | solution.py:312
  (5 shorter events, 0.0 us)
Async XLA Ops:
  0.6 1.2 %copy-start = (f32[64,32,128]{2,1,0:T(8,128)S(1)}, f32[64,32,128]{2,1,0:T(8,128)}, u32[]{:S(2)}) copy-start(f32[64,32,128]{2,1,0:T(8,128)} %d_ref.3) | copy-start | bytes 3145732
  1.9 1.2 %copy-start.1 = (f32[64,32,128]{2,1,0:T(8,128)S(1)}, f32[64,32,128]{2,1,0:T(8,128)}, u32[]{:S(2)}) copy-start(f32[64,32,128]{2,1,0:T(8,128)} %e_ref.3) | copy-start | bytes 3145732
  3.3 9.1 %collective-permute-start.2 = (f32[64,8,128]{2,1,0:T(8,128)S(1)}, f32[64,8,128]{2,1,0:T(8,128)S(1)}, u32[]{:S(2)}, u32[]{:S(2)}) collective-permute-start(f32[64,8,128]{2,1,0:T(8,128)S(1)} %get-tuple-element.21), channel_id=1, source_target_pairs={{0,1},{1,0},{2,3},{3,2},{4,5},{5,4},{6,7},{7,6},{8,9},{9,8},{10,11... | collective-permute-start | bytes 786440 | tf_op jit(solution)/shard_map/ppermute | solution.py:331
  3.8 11.8 %collective-permute-start.3 = (f32[64,8,128]{2,1,0:T(8,128)S(1)}, f32[64,8,128]{2,1,0:T(8,128)S(1)}, u32[]{:S(2)}, u32[]{:S(2)}) collective-permute-start(f32[64,8,128]{2,1,0:T(8,128)S(1)} %get-tuple-element.22), channel_id=1, source_target_pairs={{1,2},{2,1},{5,6},{6,5},{9,10},{10,9},{13,14},{14,13},{17,18},{18,... | collective-permute-start | bytes 786440 | tf_op jit(solution)/shard_map/ppermute | solution.py:331
  8.4 2.0 %copy-start.2 = (f32[4,128]{1,0:T(4,128)S(1)}, f32[4,128]{1,0:T(4,128)}, u32[]{:S(2)}) copy-start(f32[4,128]{1,0:T(4,128)} %row_taps_ref.5) | copy-start | bytes 6148
  8.4 11.0 %collective-permute-start = (f32[64,8,128]{2,1,0:T(8,128)S(1)}, f32[64,8,128]{2,1,0:T(8,128)S(1)}, u32[]{:S(2)}, u32[]{:S(2)}) collective-permute-start(f32[64,8,128]{2,1,0:T(8,128)S(1)} %get-tuple-element.18), channel_id=1, source_target_pairs={{0,1},{1,0},{2,3},{3,2},{4,5},{5,4},{6,7},{7,6},{8,9},{9,8},{10,11... | collective-permute-start | bytes 786440 | tf_op jit(solution)/shard_map/ppermute | solution.py:331
  8.5 2.0 %copy-start.4 = (s32[128]{0:T(128)S(1)}, s32[128]{0:T(128)}, u32[]{:S(2)}) copy-start(s32[128]{0:T(128)} %param.13) | copy-start | bytes 1540
  8.5 11.5 %collective-permute-start.1 = (f32[64,8,128]{2,1,0:T(8,128)S(1)}, f32[64,8,128]{2,1,0:T(8,128)S(1)}, u32[]{:S(2)}, u32[]{:S(2)}) collective-permute-start(f32[64,8,128]{2,1,0:T(8,128)S(1)} %get-tuple-element.19), channel_id=1, source_target_pairs={{1,2},{2,1},{5,6},{6,5},{9,10},{10,9},{13,14},{14,13},{17,18},{18,... | collective-permute-start | bytes 786440 | tf_op jit(solution)/shard_map/ppermute | solution.py:331
  10.5 0.8 %copy-start.7 = (f32[128]{0:T(128)S(1)}, f32[128]{0:T(128)}, u32[]{:S(2)}) copy-start(f32[128]{0:T(128)} %param.14) | copy-start | bytes 1540
  11.3 4.3 %copy-start.3 = (f32[4,128]{1,0:T(4,128)S(1)}, f32[4,128]{1,0:T(4,128)}, u32[]{:S(2)}) copy-start(f32[4,128]{1,0:T(4,128)} %taps_ref.7) | copy-start | bytes 6148
  15.6 0.7 %copy-start.5 = (s32[128]{0:T(128)S(1)}, s32[128]{0:T(128)}, u32[]{:S(2)}) copy-start(s32[128]{0:T(128)} %param.11) | copy-start | bytes 1540
  23.3 24.4 %collective-permute-start.4 = (f32[8,64,128]{2,1,0:T(8,128)}, f32[8,64,128]{2,1,0:T(8,128)S(1)}, u32[]{:S(2)}, u32[]{:S(2)}) collective-permute-start(f32[8,64,128]{2,1,0:T(8,128)} %get-tuple-element.26), channel_id=1, source_target_pairs={{0,1},{1,0},{2,3},{3,2},{4,5},{5,4},{6,7},{7,6},{8,9},{9,8},{10,11... | collective-permute-start | bytes 786440 | tf_op jit(solution)/shard_map/ppermute | solution.py:331
  23.3 24.4 %collective-permute-start.5 = (f32[8,64,128]{2,1,0:T(8,128)}, f32[8,64,128]{2,1,0:T(8,128)S(1)}, u32[]{:S(2)}, u32[]{:S(2)}) collective-permute-start(f32[8,64,128]{2,1,0:T(8,128)} %get-tuple-element.27), channel_id=1, source_target_pairs={{1,2},{2,1},{5,6},{6,5},{9,10},{10,9},{13,14},{14,13},{17,18},{18,... | collective-permute-start | bytes 786440 | tf_op jit(solution)/shard_map/ppermute | solution.py:331
  26.9 20.8 %collective-permute-start.6 = (f32[8,64,128]{2,1,0:T(8,128)}, f32[8,64,128]{2,1,0:T(8,128)S(1)}, u32[]{:S(2)}, u32[]{:S(2)}) collective-permute-start(f32[8,64,128]{2,1,0:T(8,128)} %get-tuple-element.28), channel_id=1, source_target_pairs={{0,1},{1,0},{2,3},{3,2},{4,5},{5,4},{6,7},{7,6},{8,9},{9,8},{10,11... | collective-permute-start | bytes 786440 | tf_op jit(solution)/shard_map/ppermute | solution.py:331
  27.0 20.7 %collective-permute-start.7 = (f32[8,64,128]{2,1,0:T(8,128)S(1)}, f32[8,64,128]{2,1,0:T(8,128)S(1)}, u32[]{:S(2)}, u32[]{:S(2)}) collective-permute-start(f32[8,64,128]{2,1,0:T(8,128)S(1)} %get-tuple-element.29), channel_id=1, source_target_pairs={{1,2},{2,1},{5,6},{6,5},{9,10},{10,9},{13,14},{14,13},{17,18},{18,... | collective-permute-start | bytes 786440 | tf_op jit(solution)/shard_map/ppermute | solution.py:331
  29.7 5.2 %copy-start.6 = (f32[64,32]{0,1:T(8,128)S(1)}, f32[64,32]{0,1:T(8,128)}, u32[]{:S(2)}) copy-start(f32[64,32]{0,1:T(8,128)} %param.15) | copy-start | bytes 24580
  29.7 3.2 %collective-permute-start.10 = (f32[2,2,8,128]{3,2,1,0:T(8,128)S(1)}, f32[2,2,8,128]{3,2,1,0:T(8,128)S(1)}, u32[]{:S(2)}, u32[]{:S(2)}) collective-permute-start(f32[2,2,8,128]{3,2,1,0:T(8,128)S(1)} %pad_maximum_fusion.refs_0_), channel_id=1, source_target_pairs={{12,0},{0,4},{4,8},{8,12},{13,1},{1,5},{5,9},{9,13},{14,2},{2,6},{... | collective-permute-start | bytes 49160 | tf_op jit(solution)/shard_map/ppermute | solution.py:377
  32.9 1.4 %collective-permute-start.8 = (f32[2,2,8,128]{3,2,1,0:T(8,128)S(1)}, f32[2,2,8,128]{3,2,1,0:T(8,128)S(1)}, u32[]{:S(2)}, u32[]{:S(2)}) collective-permute-start(f32[2,2,8,128]{3,2,1,0:T(8,128)S(1)} %pad_maximum_fusion.refs_0_), channel_id=1, source_target_pairs={{4,0},{8,4},{12,8},{0,12},{5,1},{9,5},{13,9},{1,13},{6,2},{10,6},{... | collective-permute-start | bytes 49160 | tf_op jit(solution)/shard_map/ppermute | solution.py:377
  34.4 3.9 %collective-permute-start.9 = (f32[2,2,8,128]{3,2,1,0:T(8,128)S(1)}, f32[2,2,8,128]{3,2,1,0:T(8,128)S(1)}, u32[]{:S(2)}, u32[]{:S(2)}) collective-permute-start(f32[2,2,8,128]{3,2,1,0:T(8,128)S(1)} %pad_maximum_fusion.refs_0_), channel_id=1, source_target_pairs={{8,0},{12,4},{0,8},{4,12},{9,1},{13,5},{1,9},{5,13},{10,2},{14,6},... | collective-permute-start | bytes 49160 | tf_op jit(solution)/shard_map/ppermute | solution.py:377
  38.3 3.8 %collective-permute-start.11 = (f32[2,2,8,128]{3,2,1,0:T(8,128)S(1)}, f32[2,2,8,128]{3,2,1,0:T(8,128)S(1)}, u32[]{:S(2)}, u32[]{:S(2)}) collective-permute-start(f32[2,2,8,128]{3,2,1,0:T(8,128)S(1)} %shard_map.99.own_ref), channel_id=1, source_target_pairs={{0,1},{1,0},{2,3},{3,2},{4,5},{5,4},{6,7},{7,6},{8,9},{9,8},{10,11... | collective-permute-start | bytes 49160 | tf_op jit(solution)/shard_map/ppermute | solution.py:331
  42.1 5.6 %collective-permute-start.12 = (f32[2,2,8,128]{3,2,1,0:T(8,128)S(1)}, f32[2,2,8,128]{3,2,1,0:T(8,128)S(1)}, u32[]{:S(2)}, u32[]{:S(2)}) collective-permute-start(f32[2,2,8,128]{3,2,1,0:T(8,128)S(1)} %shard_map.99.own_ref), channel_id=1, source_target_pairs={{1,2},{2,1},{5,6},{6,5},{9,10},{10,9},{13,14},{14,13},{17,18},{18,... | collective-permute-start | bytes 49160 | tf_op jit(solution)/shard_map/ppermute | solution.py:331

commit v2 on v1

v2 whole, which is shorter than its diff:
```python
import functools

import jax
import jax.numpy as jnp
from jax import lax
from jax.experimental import pallas as pl
from jax.experimental.pallas import tpu as pltpu
from jax.sharding import PartitionSpec as P

HALO = 8
REACH = 6
SUB = 8
F32 = jnp.float32
BF16 = jnp.bfloat16
VMEM_LIMIT = 48 * 1024 * 1024
UNROLL = 4


def pitch_of(columns):
    return columns + 1


def loop(count, body):
    def step(i, carry):
        body(i)
        return carry

    lax.fori_loop(0, count, step, 0, unroll=min(count, UNROLL))


def bits_of(shift):
    moved = jnp.broadcast_to(shift, (SUB, shift.shape[-1])) + REACH
    return {b: (moved & b) != 0 for b in (8, 4, 2, 1)}


def rows_of(taps):
    return [jnp.broadcast_to(taps[k : k + 1, :], (SUB, taps.shape[-1])) for k in range(4)]


def choose(mask, yes, no):
    if yes is None and no is None:
        return None
    if yes is None:
        return jnp.where(mask, 0.0, no)
    if no is None:
        return jnp.where(mask, yes, 0.0)
    return jnp.where(mask, yes, no)


def resample(get, bits, taps, count, flipped):
    way = -1 if flipped else 1
    memo = {}

    def stage(b, i):
        if b == 16:
            key = (b, i)
            if key not in memo:
                memo[key] = get(i)
            return memo[key]
        key = (b, i)
        if key not in memo:
            memo[key] = choose(bits[b], stage(2 * b, i + way * b), stage(2 * b, i))
        return memo[key]

    for i in range(count):
        total = None
        for k in range(4):
            v = stage(1, i + 7 - k if flipped else i - 7 + k)
            if v is not None:
                total = taps[k] * v if total is None else total + taps[k] * v
        yield i, total


def halves(x):
    hi = x.astype(BF16)
    lo = (x - hi.astype(F32)).astype(BF16)
    return jnp.concatenate([hi, lo], axis=1)


def scan_matrix(planes, before):
    a = lax.broadcasted_iota(jnp.int32, (2 * planes, 2 * planes), 0)
    b = lax.broadcasted_iota(jnp.int32, (2 * planes, 2 * planes), 1)
    a = jnp.where(a >= planes, a - planes, a)
    ordered = (a < b) if before else (a > b)
    return jnp.where((b >= planes) | ordered, 1.0, 0.0).astype(BF16)


def edge_kernel(odd_ref, field_ref, a_ref, b_ref, sems):
    columns = field_ref.shape[1]
    odd = odd_ref[0]
    first = pl.multiple_of(jnp.where(odd == 1, 0, columns - HALO), HALO)
    second = pl.multiple_of(jnp.where(odd == 1, columns - HALO, 0), HALO)
    copies = [
        pltpu.make_async_copy(field_ref.at[:, pl.ds(at, HALO), :], out, sems.at[n])
        for n, (at, out) in enumerate(((first, a_ref), (second, b_ref)))
    ]
    for c in copies:
        c.start()
    for c in copies:
        c.wait()


def row_kernel(d_ref, e_ref, taps_ref, shift_ref, weight_ref, rd_ref, re_ref):
    rows, columns, planes = d_ref.shape
    bits = bits_of(shift_ref[...])
    taps = rows_of(taps_ref[...])

    pitch = pitch_of(columns)

    def body(t):
        at = pl.multiple_of(t * SUB, SUB)
        for ref, out in ((d_ref, rd_ref), (e_ref, re_ref)):
            get = lambda y: ref[y, pl.ds(at, SUB), :] if 0 <= y < rows else None
            for y, v in resample(get, bits, taps, rows, False):
                out[pl.ds(y * pitch + at, SUB), :] = v

    loop(columns // SUB, body)


def row_halo(odd, a_ref, b_ref, halo_ref, bits, taps):
    rows = a_ref.shape[0]
    for side in range(2):
        use_a = odd == (1 - side)
        get = lambda y: jnp.where(use_a, a_ref[y], b_ref[y]) if 0 <= y < rows else None
        for y, v in resample(get, bits, taps, rows, False):
            halo_ref[pl.ds(y * pitch_of(2 * HALO) + side * HALO, SUB), :] = v


def column_get(r_ref, halo_ref, y0, columns):
    pitch, side_pitch = pitch_of(columns), pitch_of(2 * HALO)

    def get(x):
        if x < -HALO or x >= columns + HALO:
            return None
        if x < 0:
            return halo_ref[pl.ds(y0 * side_pitch + x + HALO, SUB, stride=side_pitch), :]
        if x >= columns:
            return halo_ref[pl.ds(y0 * side_pitch + HALO + x - columns, SUB, stride=side_pitch), :]
        return r_ref[pl.ds(y0 * pitch + x, SUB, stride=pitch), :]

    return get


def pack_totals(totals, dense_ref, group, columns):
    lane = lax.broadcasted_iota(jnp.int32, (SUB, 128), 1)
    per = 128 // columns
    packed = jnp.zeros((SUB, 128), F32)
    base = (group % per) * columns
    for x in range(columns):
        packed = jnp.where(lane == base + x, totals[x * SUB : (x + 1) * SUB, :], packed)
    dense_ref[group // per] += packed


def edges_out(odd, ref, a_ref, b_ref):
    columns = ref.shape[0]
    first = jnp.where(odd == 1, 0, columns - HALO)
    second = jnp.where(odd == 1, columns - HALO, 0)
    a_ref[...] = ref[pl.ds(first, HALO)]
    b_ref[...] = ref[pl.ds(second, HALO)]


def absorbed(optical):
    series = 1.0 - optical * (1 / 6)
    for k in (5, 4, 3, 2):
        series = 1.0 - optical * (1 / k) * series
    return jnp.where(optical < 0.25, optical * series, 1.0 - jnp.exp(-optical))


def density_kernel(
    odd_ref, rd_ref, a_ref, b_ref, row_taps_ref, row_shift_ref, taps_ref, shift_ref, scale_ref,
    q_ref, n_ref, qa_ref, qb_ref, dense_ref, halo_ref, optical_ref, split_ref, sums_ref,
):
    odd = odd_ref[0]
    columns, rows, planes = q_ref.shape
    row_halo(odd, a_ref, b_ref, halo_ref, bits_of(row_shift_ref[...]), rows_of(row_taps_ref[...]))
    bits = bits_of(shift_ref[...])
    taps = rows_of(taps_ref[...])
    scale = jnp.broadcast_to(scale_ref[...], (SUB, planes))
    matrix = scan_matrix(planes, True)
    dense_ref[...] = jnp.zeros_like(dense_ref)

    def body(group):
        y0 = group * SUB
        get = column_get(rd_ref, halo_ref, y0, columns)
        held = []
        for x, v in resample(get, bits, taps, columns, False):
            at = pl.multiple_of((group * columns + x) * SUB, SUB)
            v = scale * v
            optical_ref[pl.ds(at, SUB), :] = v
            held.append(v)
            if x % 2:
                at = pl.multiple_of((group * columns + x - 1) * SUB, 2 * SUB)
                split_ref[pl.ds(at, 2 * SUB), :] = halves(jnp.concatenate(held, axis=0))
                held = []

    loop(rows // SUB, body)
    sums_ref[...] = jnp.dot(split_ref[...], matrix, preferred_element_type=F32)

    def finish(group):
        to = pl.ds(pl.multiple_of(group * SUB, SUB), SUB)
        totals = []
        for x in range(columns):
            at = pl.ds(pl.multiple_of((group * columns + x) * SUB, SUB), SUB)
            optical = optical_ref[at, :]
            transmit = jnp.exp(-sums_ref[at, :planes])
            q = transmit * absorbed(optical)
            q_ref[x, to, :] = q
            n_ref[x, to, :] = transmit - q
            totals.append(sums_ref[at, planes:])
        pack_totals(jnp.concatenate(totals, axis=0), dense_ref, group, columns)

    loop(rows // SUB, finish)
    edges_out(odd, q_ref, qa_ref, qb_ref)


def emission_kernel(
    odd_ref, re_ref, a_ref, b_ref, q_ref, n_ref, row_taps_ref, row_shift_ref, taps_ref, shift_ref, scale_ref,
    p_ref, dense_ref, halo_ref,
):
    odd = odd_ref[0]
    columns, rows, planes = p_ref.shape
    row_halo(odd, a_ref, b_ref, halo_ref, bits_of(row_shift_ref[...]), rows_of(row_taps_ref[...]))
    bits = bits_of(shift_ref[...])
    taps = rows_of(taps_ref[...])
    scale = jnp.broadcast_to(scale_ref[...], (SUB, planes))
    matrix = scan_matrix(planes, False)
    dense_ref[...] = jnp.zeros_like(dense_ref)

    def body(group):
        y0 = group * SUB
        at = pl.multiple_of(y0, SUB)
        get = column_get(re_ref, halo_ref, y0, columns)
        pieces = [v for _, v in resample(get, bits, taps, columns, False)]
        light = jnp.concatenate([q_ref[x, pl.ds(at, SUB), :] * pieces[x] for x in range(columns)], axis=0)
        sums = jnp.dot(halves(light), matrix, preferred_element_type=F32)
        for x in range(columns):
            behind = sums[x * SUB : (x + 1) * SUB, :planes]
            p_ref[x, pl.ds(at, SUB), :] = scale * (n_ref[x, pl.ds(at, SUB), :] * pieces[x] - behind)
        pack_totals(sums[:, planes:], dense_ref, group, columns)

    loop(rows // SUB, body)


def join_kernel(count, odd_ref, mine_ref, weight_ref, p_ref, *refs):
    sums, (out_ref, a_ref, b_ref) = refs[:count], refs[count:]
    mine = mine_ref[0]
    weight = weight_ref[...]
    front = jnp.zeros_like(weight)
    for ahead in range(1, count):
        front += jnp.where(mine + ahead >= count, sums[ahead][0], 0.0)
    running = front + sums[0][0]
    back = jnp.zeros_like(weight)
    for ahead in range(1, count):
        there = mine + ahead < count
        back += jnp.where(there, jnp.exp(-running) * sums[ahead][1], 0.0)
        running += jnp.where(there, sums[ahead][0], 0.0)
    out_ref[0] = weight * jnp.exp(-front)
    out_ref[1] = weight * back
    columns = p_ref.shape[0]
    for ref, at in (
        (a_ref, jnp.where(odd_ref[0] == 1, 0, columns - HALO)),
        (b_ref, jnp.where(odd_ref[0] == 1, columns - HALO, 0)),
    ):
        rows = p_ref.shape[1]
        for x in range(HALO):
            ref[x * rows : (x + 1) * rows, :] = p_ref[at + x]
        for f in range(2):
            for c in range(weight.shape[0]):
                row = HALO * rows + (f * weight.shape[0] + c) * SUB
                ref[row : row + SUB, :] = out_ref[f, c]


def spread(pair, base, first, last):
    lane = lax.broadcasted_iota(jnp.int32, (SUB, 128), 1)
    masks = [lane == base + x for x in range(first, last)]
    rows = []
    for dense in pair:
        hi = dense.astype(BF16).astype(F32)
        stacks = [
            jnp.concatenate([jnp.where(m, part, 0.0) for m in masks], axis=0).astype(BF16)
            for part in (hi, dense - hi)
        ]
        rows.append(jnp.concatenate(stacks, axis=1))
    ones = jnp.ones((256, 128), BF16)
    return [jnp.dot(r, ones, preferred_element_type=F32) for r in rows]


def own_kernel(
    p_ref, q_ref, own_ref, row_taps_ref, row_shift_ref, taps_ref, shift_ref, scale_ref,
    gd_ref, ge_ref, td_ref, te_ref, cd_ref, ce_ref, out_ref, front_ref, back_ref, sems,
):
    columns, rows, planes = p_ref.shape
    per = 128 // columns
    inner = columns - 2 * HALO
    pitch, side_pitch = pitch_of(inner), pitch_of(2 * HALO)
    bits = bits_of(shift_ref[...])
    taps = rows_of(taps_ref[...])
    scale = jnp.broadcast_to(scale_ref[...], (SUB, planes))

    for group in range(rows // SUB):
        chunk = group // per
        front, back = spread((own_ref[0, chunk], own_ref[1, chunk]), group % per * columns, 0, columns)
        for x in range(columns):
            front_ref[x, group * SUB : (group + 1) * SUB, :] = front[x * SUB : (x + 1) * SUB]
            back_ref[x, group * SUB : (group + 1) * SUB, :] = back[x * SUB : (x + 1) * SUB] * scale

    def body(group):
        y0 = group * SUB
        at = pl.multiple_of(y0, SUB)

        def get_d(x):
            if not 0 <= x < columns:
                return None
            return front_ref[x, pl.ds(at, SUB), :] * p_ref[x, pl.ds(at, SUB), :] - back_ref[x, pl.ds(at, SUB), :]

        def get_e(x):
            if not 0 <= x < columns:
                return None
            return front_ref[x, pl.ds(at, SUB), :] * q_ref[x, pl.ds(at, SUB), :]

        for get, inside, outside in ((get_d, cd_ref, td_ref), (get_e, ce_ref, te_ref)):
            for x, v in resample(get, bits, taps, columns, True):
                if HALO <= x < columns - HALO:
                    inside[pl.ds(y0 * pitch + x - HALO, SUB, stride=pitch), :] = v
                else:
                    to = x if x < HALO else x - inner
                    outside[pl.ds(y0 * side_pitch + to, SUB, stride=side_pitch), :] = v

    loop(rows // SUB, body)
    row_bits = bits_of(row_shift_ref[...])
    row_taps = rows_of(row_taps_ref[...])
    copies = []
    for field, (ref, out) in enumerate(((cd_ref, gd_ref), (ce_ref, ge_ref))):
        def row_body(t):
            at = pl.multiple_of(t * SUB, SUB)
            get = lambda y: ref[pl.ds(y * pitch + at, SUB), :] if 0 <= y < rows else None
            for y, v in resample(get, row_bits, row_taps, rows, True):
                out_ref[field, y, pl.ds(at, SUB), :] = v

        loop(inner // SUB, row_body)
        copies.append(
            pltpu.make_async_copy(out_ref.at[field], out.at[:, pl.ds(HALO, inner), :], sems.at[field])
        )
        copies[-1].start()
    for c in copies:
        c.wait()


def outer_kernel(
    odd_ref, pa_ref, pb_ref, qa_ref, qb_ref, td_ref, te_ref,
    row_taps_ref, row_shift_ref, taps_ref, shift_ref, scale_ref, gd_in, ge_in,
    gd_ref, ge_ref, cd_ref, ce_ref, out_ref, front_ref, back_ref, sems,
):
    odd = odd_ref[0]
    rows, columns, planes = gd_ref.shape
    per = 128 // columns
    chunks = rows // SUB // per
    pitch = pitch_of(2 * HALO)
    bits = bits_of(shift_ref[...])
    taps = rows_of(taps_ref[...])
    scale = jnp.broadcast_to(scale_ref[...], (SUB, planes))
    use_a = (odd == 1, odd != 1)

    for side in range(2):
        first = columns - HALO if side == 0 else 0
        for group in range(rows // SUB):
            pair = []
            for f in range(2):
                row = HALO * rows + (f * chunks + group // per) * SUB
                pair.append(
                    jnp.where(use_a[side], pa_ref[row : row + SUB, :], pb_ref[row : row + SUB, :])
                )
            front, back = spread(pair, group % per * columns, first, first + HALO)
            for x in range(HALO):
                front_ref[side, x, group * SUB : (group + 1) * SUB, :] = front[x * SUB : (x + 1) * SUB]
                back_ref[side, x, group * SUB : (group + 1) * SUB, :] = back[x * SUB : (x + 1) * SUB] * scale

    def body(group):
        y0 = group * SUB
        at = pl.multiple_of(y0, SUB)
        for side in range(2):
            start = -HALO if side == 0 else HALO

            def get_d(x):
                i = x - start
                if not 0 <= i < HALO:
                    return None
                here = pl.ds(pl.multiple_of(i * rows + at, SUB), SUB)
                v = jnp.where(use_a[side], pa_ref[here, :], pb_ref[here, :])
                return front_ref[side, i, pl.ds(at, SUB), :] * v - back_ref[side, i, pl.ds(at, SUB), :]

            def get_e(x):
                i = x - start
                if not 0 <= i < HALO:
                    return None
                v = jnp.where(use_a[side], qa_ref[i, pl.ds(at, SUB), :], qb_ref[i, pl.ds(at, SUB), :])
                return front_ref[side, i, pl.ds(at, SUB), :] * v

            for get, ref, out in ((get_d, td_ref, cd_ref), (get_e, te_ref, ce_ref)):
                for x, v in resample(get, bits, taps, HALO, True):
                    where = pl.ds(y0 * pitch + side * HALO + x, SUB, stride=pitch)
                    out[where, :] = ref[where, :] if v is None else ref[where, :] + v

    loop(rows // SUB, body)
    row_bits = bits_of(row_shift_ref[...])
    row_taps = rows_of(row_taps_ref[...])
    copies = []
    for field, (ref, out) in enumerate(((cd_ref, gd_ref), (ce_ref, ge_ref))):
        for side in range(2):
            get = lambda y: ref[pl.ds(y * pitch + side * HALO, SUB), :] if 0 <= y < rows else None
            for y, v in resample(get, row_bits, row_taps, rows, True):
                out_ref[field, side, y] = v
            copies.append(
                pltpu.make_async_copy(
                    out_ref.at[field, side],
                    out.at[:, pl.ds(side * (columns - HALO), HALO), :],
                    sems.at[2 * field + side],
                )
            )
            copies[-1].start()
    for c in copies:
        c.wait()


def call(kernel, outs, scalars, vmem, scratch=(), hbm_in=(), hbm_out=0, aliases=None, micros=2.0, limit=VMEM_LIMIT):
    whole, far = pl.BlockSpec(memory_space=pltpu.VMEM), pl.BlockSpec(memory_space=pl.ANY)
    return pl.pallas_call(
        kernel,
        out_shape=[jax.ShapeDtypeStruct(s, F32) for s in outs],
        in_specs=[pl.BlockSpec(memory_space=pltpu.SMEM)] * len(scalars)
        + [whole] * len(vmem)
        + [far] * len(hbm_in),
        out_specs=[far] * hbm_out + [whole] * (len(outs) - hbm_out),
        scratch_shapes=list(scratch),
        input_output_aliases=aliases or {},
        compiler_params=pltpu.CompilerParams(vmem_limit_bytes=limit),
        cost_estimate=pl.CostEstimate(
            flops=int(micros * 1e6), bytes_accessed=int(micros * 3.0e6), transcendentals=0
        ),
    )(*scalars, *vmem, *hbm_in)


def swap(value, axis, parity):
    count = lax.axis_size(axis)
    pairs = []
    for i in range(parity, count - 1, 2):
        pairs += [(i, i + 1), (i + 1, i)]
    return lax.ppermute(value, axis, pairs)


def on_device(density, emission, taps, shift, row_taps, row_shift, step_length, cotangent):
    rows, columns, planes = density.shape
    slabs = lax.axis_size("depth")
    all_planes = planes * slabs
    per = 128 // columns
    chunks = rows // SUB // per
    shift, row_shift = shift[None, :], row_shift[None, :]
    scale = step_length[None, :] / all_planes
    odd = (lax.axis_index("screen") % 2).astype(jnp.int32)[None]
    mine = lax.axis_index("depth").astype(jnp.int32)[None]
    weight = cotangent.reshape(chunks, per, SUB, columns).transpose(0, 2, 1, 3).reshape(chunks, SUB, 128)

    edge = (rows, HALO, planes)
    sides = []
    for field in (density, emission):
        a, b = call(
            edge_kernel,
            [edge] * 2,
            [odd],
            [],
            [pltpu.SemaphoreType.DMA((2,))],
            hbm_in=[field],
            hbm_out=2,
            micros=0.2,
        )
        sides.append((swap(a, "screen", 0), swap(b, "screen", 1)))
    (da, db), (ea, eb) = sides
    flat = (rows * pitch_of(columns), planes)
    rd, re = call(row_kernel, [flat, flat], [], [density, emission, row_taps, row_shift, weight])

    cells = (columns, rows, planes)
    side = (HALO, rows, planes)
    dense = (chunks, SUB, 128)
    outer = (rows * pitch_of(2 * HALO), planes)
    q, n, qa, qb, slab_optical = call(
        density_kernel,
        [cells, cells, side, side, dense],
        [odd],
        [rd, da, db, row_taps, row_shift, taps, shift, scale],
        [
            pltpu.VMEM(outer, F32),
            pltpu.VMEM((rows * columns, planes), F32),
            pltpu.VMEM((rows * columns, 2 * planes), BF16),
            pltpu.VMEM((rows * columns, 2 * planes), F32),
        ],
    )
    qa, qb = swap(qa, "screen", 0), swap(qb, "screen", 1)
    p, slab_light = call(
        emission_kernel,
        [cells, dense],
        [odd],
        [re, ea, eb, q, n, row_taps, row_shift, taps, shift, scale],
        [pltpu.VMEM(outer, F32)],
        micros=6.0,
    )
    sums = jnp.stack([slab_optical, slab_light])
    ahead = [sums] + [
        lax.ppermute(sums, "depth", [((i + e) % slabs, i) for i in range(slabs)]) for e in range(1, slabs)
    ]
    message = (HALO * rows + 2 * chunks * SUB, planes)
    own, pa, pb = call(
        functools.partial(join_kernel, slabs),
        [(2,) + dense, message, message],
        [odd, mine],
        [weight, p] + ahead,
        micros=0.3,
    )
    pa, pb, qa, qb = lax.optimization_barrier((pa, pb, qa, qb))
    pa, pb = swap(pa, "screen", 0), swap(pb, "screen", 1)
    inner = (rows * pitch_of(columns - 2 * HALO), planes)
    gd, ge, td, te = call(
        own_kernel,
        [density.shape, density.shape, outer, outer],
        [],
        [p, q, own, row_taps, row_shift, taps, shift, scale],
        [
            pltpu.VMEM(inner, F32),
            pltpu.VMEM(inner, F32),
            pltpu.VMEM((2, rows, columns - 2 * HALO, planes), F32),
            pltpu.VMEM(cells, F32),
            pltpu.VMEM(cells, F32),
            pltpu.SemaphoreType.DMA((2,)),
        ],
        hbm_out=2,
        micros=6.0,
    )
    gd, ge = call(
        outer_kernel,
        [density.shape, density.shape],
        [odd],
        [pa, pb, qa, qb, td, te, row_taps, row_shift, taps, shift, scale],
        [
            pltpu.VMEM(outer, F32),
            pltpu.VMEM(outer, F32),
            pltpu.VMEM((2, 2, rows, HALO, planes), F32),
            pltpu.VMEM((2,) + side, F32),
            pltpu.VMEM((2,) + side, F32),
            pltpu.SemaphoreType.DMA((4,)),
        ],
        hbm_in=[gd, ge],
        hbm_out=2,
        aliases={12: 0, 13: 1},
    )
    return gd, ge


def solution(mesh):
    in_specs = (
        P("groups", "screen", "depth"),
        P("groups", "screen", "depth"),
        P("groups", "depth"),
        P(("groups", "depth")),
        P("groups", "depth"),
        P(("groups", "depth")),
        P(("groups", "depth")),
        P("groups", "screen"),
    )
    out_specs = (P("groups", "screen", "depth"), P("groups", "screen", "depth"))
    return jax.shard_map(
        on_device, mesh=mesh, in_specs=in_specs, out_specs=out_specs, check_vma=False
    )
```

time: 54.1 us -> 41 us (0.76)
  waiting for transfers between devices: 17.4 us -> 8.39 us
  local copies, waits for them, and re-layouts: 4.66 us -> 2.65 us
  Pallas kernels: 13.5 us -> 11.7 us
  starting transfers between devices: 17.3 us -> 16.6 us
    ppermute x3, waiting for transfers between devices: 6.38 us -> 1.82 us  [on_device(): lax.ppermute(sums, 'depth', [((i + e) % slabs, i) for i in range(slabs)])]
    ppermute x10 -> x8, waiting for transfers between devices: 11.1 us -> 6.57 us  [swap(): return lax.ppermute(value, axis, pairs)]
    ppermute x10 -> x8, starting transfers between devices: 16.7 us -> 14.6 us  [swap(): return lax.ppermute(value, axis, pairs)]
    pallas_call x6 -> x8, Pallas kernels: 13.5 us -> 11.7 us  [call(): pl.pallas_call(kernel, out_shape=[jax.ShapeDtypeStruct(s, F32) for s in o...]
    ppermute x3, starting transfers between devices: 0.6 us -> 2.05 us  [on_device(): lax.ppermute(sums, 'depth', [((i + e) % slabs, i) for i in range(slabs)])]
    unnamed x17 -> x21, local copies, waits for them, and re-layouts: 3.81 us -> 2.56 us
    transpose x1, local copies, waits for them, and re-layouts: 0.77 us -> 0.01 us  [on_device(): cotangent.reshape(chunks, per, SUB, columns).transpose(0, 2, 1, 3)]
  transfers between devices with their start and end apart: 13 -> 11, of which waited for: 8 -> 5; matrix products, arithmetic and copies ran while one was open for 3% -> 0% of each run, Pallas kernels for 7% -> 22%
where the time goes in v2:
time: 41 us; the launch traced here: 40.3 us
  starting transfers between devices  16.6 us (40%)
  Pallas kernels  11.7 us (29%)
  waiting for transfers between devices  8.39 us (20%)
  local copies, waits for them, and re-layouts  2.65 us (6%)
  between operations  0.88 us (2%)
    ppermute x8, starting transfers between devices, swap(): return lax.ppermute(value, axis, pairs)  14.6 us
    pallas_call x8, Pallas kernels, call(): pl.pallas_call(kernel, out_shape=[jax.ShapeDtypeStruct(s, F32) for s in o...  11.7 us
    ppermute x8, waiting for transfers between devices, swap(): return lax.ppermute(value, axis, pairs)  6.57 us
    unnamed x21, local copies, waits for them, and re-layouts  2.56 us
    ppermute x3, starting transfers between devices, on_device(): lax.ppermute(sums, 'depth', [((i + e) % slabs, i) for i in range(slabs)])  2.05 us
    ppermute x3, waiting for transfers between devices, on_device(): lax.ppermute(sums, 'depth', [((i + e) % slabs, i) for i in range(slabs)])  1.82 us
  transfers between devices with their start and end apart: 11, of which 5 were waited for; matrix products, arithmetic and copies ran while one was open for 0% of the time, Pallas kernels for 22%

profile of v2, /device:TPU:14, one launch (start us, length us, event | category | flops | bytes accessed | tf_op | source)
XLA Modules:
  0.0 40.3 jit_solution(6082301831849640292)
XLA Ops:
  0.6 0.0 copy-start.8
  0.7 0.0 copy-start
  0.7 1.2 %copy-done = f32[64,32,128]{2,1,0:T(8,128)S(1)} copy-done((f32[64,32,128]{2,1,0:T(8,128)S(1)}, f32[64,32,128]{2,1,0:T(8,128)}, u32[]{:S(2)}) %copy-start) | copy-done | bytes 1048600
  1.9 0.0 copy-start.1
  1.9 0.7 %shard_map.97 = (f32[64,8,128]{2,1,0:T(8,128)}, f32[64,8,128]{2,1,0:T(8,128)S(1)}) custom-call(s32[1]{0:T(128)} %bitcast.odd_ref, f32[64,32,128]{2,1,0:T(8,128)S(1)} %copy-done), custom_call_target="tpu_custom_call" | custom-call | flops 200000 | bytes 600000 | tf_op jit(solution)/shard_map/pallas_call | solution.py:427
  2.6 0.5 %collective-permute-start.2 = (f32[64,8,128]{2,1,0:T(8,128)}, f32[64,8,128]{2,1,0:T(8,128)S(1)}, u32[]{:S(2)}, u32[]{:S(2)}) collective-permute-start(f32[64,8,128]{2,1,0:T(8,128)} %get-tuple-element.30), channel_id=1, source_target_pairs={{0,1},{1,0},{2,3},{3,2},{4,5},{5,4},{6,7},{7,6},{8,9},{9,8},{10,11... | collective-permute-start | bytes 786440 | tf_op jit(solution)/shard_map/ppermute | solution.py:448
  3.1 4.6 %collective-permute-start.3 = (f32[64,8,128]{2,1,0:T(8,128)S(1)}, f32[64,8,128]{2,1,0:T(8,128)S(1)}, u32[]{:S(2)}, u32[]{:S(2)}) collective-permute-start(f32[64,8,128]{2,1,0:T(8,128)S(1)} %get-tuple-element.31), channel_id=1, source_target_pairs={{1,2},{2,1},{5,6},{6,5},{9,10},{10,9},{13,14},{14,13},{17,18},{18,... | collective-permute-start | bytes 786440 | tf_op jit(solution)/shard_map/ppermute | solution.py:448
  7.7 0.0 copy-start.2
  7.7 1.2 %copy-done.2 = f32[64,32,128]{2,1,0:T(8,128)S(1)} copy-done((f32[64,32,128]{2,1,0:T(8,128)S(1)}, f32[64,32,128]{2,1,0:T(8,128)}, u32[]{:S(2)}) %copy-start.2) | copy-done | bytes 1048600
  9.0 0.8 %shard_map.96 = (f32[64,8,128]{2,1,0:T(8,128)}, f32[64,8,128]{2,1,0:T(8,128)}) custom-call(s32[1]{0:T(128)} %bitcast.odd_ref, f32[64,32,128]{2,1,0:T(8,128)S(1)} %copy-done.2), custom_call_target="tpu_custom_call" | custom-call | flops 200000 | bytes 600000 | tf_op jit(solution)/shard_map/pallas_call | solution.py:427
  9.8 0.1 collective-permute-start
  9.8 1.9 %collective-permute-start.1 = (f32[64,8,128]{2,1,0:T(8,128)}, f32[64,8,128]{2,1,0:T(8,128)S(1)}, u32[]{:S(2)}, u32[]{:S(2)}) collective-permute-start(f32[64,8,128]{2,1,0:T(8,128)} %get-tuple-element.28), channel_id=1, source_target_pairs={{1,2},{2,1},{5,6},{6,5},{9,10},{10,9},{13,14},{14,13},{17,18},{18,... | collective-permute-start | bytes 786440 | tf_op jit(solution)/shard_map/ppermute | solution.py:448
  11.8 0.0 copy-done.8
  11.8 0.1 copy.13
  11.9 0.0 copy-start.9
  11.9 0.0 copy-start.5
  11.9 0.0 copy-start.7
  11.9 0.1 reshape.12.weight_ref
  12.0 0.0 copy-done.1
  12.0 0.0 copy-done.4
  12.0 0.0 copy-done.6
  12.0 0.0 copy-done.3
  12.0 0.8 %shard_map.95 = (f32[2112,128]{1,0:T(8,128)S(1)}, f32[2112,128]{1,0:T(8,128)S(1)}) custom-call(f32[64,32,128]{2,1,0:T(8,128)S(1)} %copy-done.1, f32[64,32,128]{2,1,0:T(8,128)S(1)} %copy-done.3, f32[4,128]{1,0:T(4,128)S(1)} %copy-done.4, s32[1,128]{1,0:T(1,128)S(1)} %bitcast.11, f32[2,8,128]{2,1,0:T(8,128)S(1)} %reshape.12.weight_ref), custom_call_target="tpu_custom_call" | custom-call | flops 2000000 | bytes 6000000 | tf_op jit(solution)/shard_map/pallas_call | solution.py:427
  12.8 0.0 copy-done.9
  12.8 0.0 collective-permute-done.2.a_ref
  12.8 1.4 %collective-permute-done.3.b_ref = f32[64,8,128]{2,1,0:T(8,128)S(1)} collective-permute-done((f32[64,8,128]{2,1,0:T(8,128)S(1)}, f32[64,8,128]{2,1,0:T(8,128)S(1)}, u32[]{:S(2)}, u32[]{:S(2)}) %collective-permute-start.3) | collective-permute-done | bytes 262176 | tf_op jit(solution)/shard_map/ppermute | solution.py:448
  14.3 0.0 copy-done.5
  14.3 0.0 copy-done.7
  14.3 3.1 %shard_map.98 = (f32[32,64,128]{2,1,0:T(8,128)S(1)}, f32[32,64,128]{2,1,0:T(8,128)S(1)}, f32[8,64,128]{2,1,0:T(8,128)}, f32[8,64,128]{2,1,0:T(8,128)S(1)}, f32[2,8,128]{2,1,0:T(8,128)S(1)}) custom-call(s32[1]{0:T(128)} %bitcast.odd_ref, f32[2112,128]{1,0:T(8,128)S(1)} %get-tuple-element.29.rd_ref, f32[64,8,128]{2,1,0:T(8,128)S(1)} %collective-permute-done.2.a_ref, ...), custom_call_target="tpu_custom_call" | custom-call | flops 2000000 | bytes 6000000 | tf_op jit(solution)/shard_map/pallas_call | solution.py:427
  17.3 0.0 collective-permute-start.7
  17.3 4.4 %collective-permute-start.8 = (f32[8,64,128]{2,1,0:T(8,128)S(1)}, f32[8,64,128]{2,1,0:T(8,128)S(1)}, u32[]{:S(2)}, u32[]{:S(2)}) collective-permute-start(f32[8,64,128]{2,1,0:T(8,128)S(1)} %get-tuple-element.40), channel_id=1, source_target_pairs={{1,2},{2,1},{5,6},{6,5},{9,10},{10,9},{13,14},{14,13},{17,18},{18,... | collective-permute-start | bytes 786440 | tf_op jit(solution)/shard_map/ppermute | solution.py:448
  21.7 0.0 collective-permute-done.a_ref
  21.7 0.0 collective-permute-done.1.b_ref
  21.8 1.2 %shard_map.99 = (f32[32,64,128]{2,1,0:T(8,128)S(1)}, f32[2,8,128]{2,1,0:T(8,128)S(1)}) custom-call(s32[1]{0:T(128)} %bitcast.odd_ref, f32[2112,128]{1,0:T(8,128)S(1)} %get-tuple-element.26.re_ref, f32[64,8,128]{2,1,0:T(8,128)S(1)} %collective-permute-done.a_ref, f32[64,8,128]{2,1,0:T(8,128)S(1)} %collective-permute-done.1.b_ref, ...), custom_call_target="tpu_custom_call" | custom-call | flops 6000000 | bytes 18000000 | tf_op jit(solution)/shard_map/pallas_call | solution.py:427
  22.9 0.1 collective-permute-start.6
  23.0 0.6 %collective-permute-start.5 = (f32[2,2,8,128]{3,2,1,0:T(8,128)S(1)}, f32[2,2,8,128]{3,2,1,0:T(8,128)S(1)}, u32[]{:S(2)}, u32[]{:S(2)}) collective-permute-start(f32[2,2,8,128]{3,2,1,0:T(8,128)S(1)} %pad_maximum_fusion.refs_0_), channel_id=1, source_target_pairs={{8,0},{12,4},{0,8},{4,12},{9,1},{13,5},{1,9},{5,13},{10,2},{14,6},... | collective-permute-start | bytes 49160 | tf_op jit(solution)/shard_map/ppermute | solution.py:508
  23.6 1.4 %collective-permute-start.4 = (f32[2,2,8,128]{3,2,1,0:T(8,128)S(1)}, f32[2,2,8,128]{3,2,1,0:T(8,128)S(1)}, u32[]{:S(2)}, u32[]{:S(2)}) collective-permute-start(f32[2,2,8,128]{3,2,1,0:T(8,128)S(1)} %pad_maximum_fusion.refs_0_), channel_id=1, source_target_pairs={{4,0},{8,4},{12,8},{0,12},{5,1},{9,5},{13,9},{1,13},{6,2},{10,6},{... | collective-permute-start | bytes 49160 | tf_op jit(solution)/shard_map/ppermute | solution.py:508
  25.0 1.2 %collective-permute-done.6.refs_3_ = f32[2,2,8,128]{3,2,1,0:T(8,128)S(1)} collective-permute-done((f32[2,2,8,128]{3,2,1,0:T(8,128)S(1)}, f32[2,2,8,128]{3,2,1,0:T(8,128)S(1)}, u32[]{:S(2)}, u32[]{:S(2)}) %collective-permute-start.6) | collective-permute-done | bytes 16416 | tf_op jit(solution)/shard_map/ppermute | solution.py:508
  26.2 0.7 %collective-permute-done.5.refs_2_ = f32[2,2,8,128]{3,2,1,0:T(8,128)S(1)} collective-permute-done((f32[2,2,8,128]{3,2,1,0:T(8,128)S(1)}, f32[2,2,8,128]{3,2,1,0:T(8,128)S(1)}, u32[]{:S(2)}, u32[]{:S(2)}) %collective-permute-start.5) | collective-permute-done | bytes 16416 | tf_op jit(solution)/shard_map/ppermute | solution.py:508
  26.8 0.0 collective-permute-done.4.refs_1_
  26.9 0.0 collective-permute-done.7.qa_ref
  26.9 0.0 collective-permute-done.8.qb_ref
  26.9 0.1 collective-permute-start.9
  27.0 3.0 %collective-permute-start.10 = (f32[544,128]{1,0:T(8,128)S(1)}, f32[544,128]{1,0:T(8,128)S(1)}, u32[]{:S(2)}, u32[]{:S(2)}) collective-permute-start(f32[544,128]{1,0:T(8,128)S(1)} %get-tuple-element.42), channel_id=1, source_target_pairs={{1,2},{2,1},{5,6},{6,5},{9,10},{10,9},{13,14},{14,13},{17,18},{18,... | collective-permute-start | bytes 835592 | tf_op jit(solution)/shard_map/ppermute | solution.py:448
  30.0 3.0 %shard_map.101 = (f32[64,32,128]{2,1,0:T(8,128)}, f32[64,32,128]{2,1,0:T(8,128)}, f32[1088,128]{1,0:T(8,128)S(1)}, f32[1088,128]{1,0:T(8,128)S(1)}) custom-call(f32[32,64,128]{2,1,0:T(8,128)S(1)} %get-tuple-element.34.p_ref, f32[32,64,128]{2,1,0:T(8,128)S(1)} %get-tuple-element.32.q_ref, f32[2,2,8,128]{3,2,1,0:T(8,128)S(1)} %get-tuple-element.45.own_ref, ...), custom_call_target="tpu_custom_call" | custom-call | flops 6000000 | bytes 18000000 | tf_op jit(solution)/shard_map/pallas_call | solution.py:427
  33.0 3.2 %collective-permute-done.9.pa_ref = f32[544,128]{1,0:T(8,128)S(1)} collective-permute-done((f32[544,128]{1,0:T(8,128)S(1)}, f32[544,128]{1,0:T(8,128)S(1)}, u32[]{:S(2)}, u32[]{:S(2)}) %collective-permute-start.9) | collective-permute-done | bytes 278560 | tf_op jit(solution)/shard_map/ppermute | solution.py:448
  36.2 1.9 %collective-permute-done.10.pb_ref = f32[544,128]{1,0:T(8,128)S(1)} collective-permute-done((f32[544,128]{1,0:T(8,128)S(1)}, f32[544,128]{1,0:T(8,128)S(1)}, u32[]{:S(2)}, u32[]{:S(2)}) %collective-permute-start.10) | collective-permute-done | bytes 278560 | tf_op jit(solution)/shard_map/ppermute | solution.py:448
  38.2 2.1 %shard_map.102 = (f32[64,32,128]{2,1,0:T(8,128)}, f32[64,32,128]{2,1,0:T(8,128)}) custom-call(s32[1]{0:T(128)} %bitcast.odd_ref, f32[544,128]{1,0:T(8,128)S(1)} %collective-permute-done.9.pa_ref, f32[544,128]{1,0:T(8,128)S(1)} %collective-permute-done.10.pb_ref, ...), custom_call_target="tpu_custom_call", output_to_operand_aliasing={{0}: (12, {}), {1}: (13, {})} | custom-call | flops 2000000 | bytes 6000000 | tf_op jit(solution)/shard_map/pallas_call | solution.py:427
  (7 shorter events, 0.1 us)
Async XLA Ops:
  0.6 11.1 %copy-start.8 = (f32[64,32]{0,1:T(8,128)S(1)}, f32[64,32]{0,1:T(8,128)}, u32[]{:S(2)}) copy-start(f32[64,32]{0,1:T(8,128)} %param.15) | copy-start | bytes 24580
  0.7 1.2 %copy-start = (f32[64,32,128]{2,1,0:T(8,128)S(1)}, f32[64,32,128]{2,1,0:T(8,128)}, u32[]{:S(2)}) copy-start(f32[64,32,128]{2,1,0:T(8,128)} %field_ref.3) | copy-start | bytes 3145732
  1.9 10.1 %copy-start.1 = (f32[64,32,128]{2,1,0:T(8,128)S(1)}, f32[64,32,128]{2,1,0:T(8,128)}, u32[]{:S(2)}) copy-start(f32[64,32,128]{2,1,0:T(8,128)} %field_ref.3) | copy-start | bytes 3145732
  1.9 10.1 %copy-start.4 = (f32[4,128]{1,0:T(4,128)S(1)}, f32[4,128]{1,0:T(4,128)}, u32[]{:S(2)}) copy-start(f32[4,128]{1,0:T(4,128)} %row_taps_ref.7) | copy-start | bytes 6148
  1.9 10.1 %copy-start.6 = (s32[128]{0:T(128)S(1)}, s32[128]{0:T(128)}, u32[]{:S(2)}) copy-start(s32[128]{0:T(128)} %param.13) | copy-start | bytes 1540
  2.6 10.2 %collective-permute-start.2 = (f32[64,8,128]{2,1,0:T(8,128)}, f32[64,8,128]{2,1,0:T(8,128)S(1)}, u32[]{:S(2)}, u32[]{:S(2)}) collective-permute-start(f32[64,8,128]{2,1,0:T(8,128)} %get-tuple-element.30), channel_id=1, source_target_pairs={{0,1},{1,0},{2,3},{3,2},{4,5},{5,4},{6,7},{7,6},{8,9},{9,8},{10,11... | collective-permute-start | bytes 786440 | tf_op jit(solution)/shard_map/ppermute | solution.py:448
  3.1 11.2 %collective-permute-start.3 = (f32[64,8,128]{2,1,0:T(8,128)S(1)}, f32[64,8,128]{2,1,0:T(8,128)S(1)}, u32[]{:S(2)}, u32[]{:S(2)}) collective-permute-start(f32[64,8,128]{2,1,0:T(8,128)S(1)} %get-tuple-element.31), channel_id=1, source_target_pairs={{1,2},{2,1},{5,6},{6,5},{9,10},{10,9},{13,14},{14,13},{17,18},{18,... | collective-permute-start | bytes 786440 | tf_op jit(solution)/shard_map/ppermute | solution.py:448
  7.7 1.2 %copy-start.2 = (f32[64,32,128]{2,1,0:T(8,128)S(1)}, f32[64,32,128]{2,1,0:T(8,128)}, u32[]{:S(2)}) copy-start(f32[64,32,128]{2,1,0:T(8,128)} %field_ref.2) | copy-start | bytes 3145732
  9.0 3.1 %copy-start.3 = (f32[64,32,128]{2,1,0:T(8,128)S(1)}, f32[64,32,128]{2,1,0:T(8,128)}, u32[]{:S(2)}) copy-start(f32[64,32,128]{2,1,0:T(8,128)} %field_ref.2) | copy-start | bytes 3145732
  9.8 12.0 %collective-permute-start = (f32[64,8,128]{2,1,0:T(8,128)}, f32[64,8,128]{2,1,0:T(8,128)S(1)}, u32[]{:S(2)}, u32[]{:S(2)}) collective-permute-start(f32[64,8,128]{2,1,0:T(8,128)} %get-tuple-element.27), channel_id=1, source_target_pairs={{0,1},{1,0},{2,3},{3,2},{4,5},{5,4},{6,7},{7,6},{8,9},{9,8},{10,11... | collective-permute-start | bytes 786440 | tf_op jit(solution)/shard_map/ppermute | solution.py:448
  9.8 11.9 %collective-permute-start.1 = (f32[64,8,128]{2,1,0:T(8,128)}, f32[64,8,128]{2,1,0:T(8,128)S(1)}, u32[]{:S(2)}, u32[]{:S(2)}) collective-permute-start(f32[64,8,128]{2,1,0:T(8,128)} %get-tuple-element.28), channel_id=1, source_target_pairs={{1,2},{2,1},{5,6},{6,5},{9,10},{10,9},{13,14},{14,13},{17,18},{18,... | collective-permute-start | bytes 786440 | tf_op jit(solution)/shard_map/ppermute | solution.py:448
  11.9 0.9 %copy-start.9 = (f32[128]{0:T(128)S(1)}, f32[128]{0:T(128)}, u32[]{:S(2)}) copy-start(f32[128]{0:T(128)} %param.14) | copy-start | bytes 1540
  11.9 2.4 %copy-start.5 = (f32[4,128]{1,0:T(4,128)S(1)}, f32[4,128]{1,0:T(4,128)}, u32[]{:S(2)}) copy-start(f32[4,128]{1,0:T(4,128)} %taps_ref.9) | copy-start | bytes 6148
  11.9 2.4 %copy-start.7 = (s32[128]{0:T(128)S(1)}, s32[128]{0:T(128)}, u32[]{:S(2)}) copy-start(s32[128]{0:T(128)} %param.11) | copy-start | bytes 1540
  17.3 9.5 %collective-permute-start.7 = (f32[8,64,128]{2,1,0:T(8,128)}, f32[8,64,128]{2,1,0:T(8,128)S(1)}, u32[]{:S(2)}, u32[]{:S(2)}) collective-permute-start(f32[8,64,128]{2,1,0:T(8,128)} %get-tuple-element.39), channel_id=1, source_target_pairs={{0,1},{1,0},{2,3},{3,2},{4,5},{5,4},{6,7},{7,6},{8,9},{9,8},{10,11... | collective-permute-start | bytes 786440 | tf_op jit(solution)/shard_map/ppermute | solution.py:448
  17.3 9.5 %collective-permute-start.8 = (f32[8,64,128]{2,1,0:T(8,128)S(1)}, f32[8,64,128]{2,1,0:T(8,128)S(1)}, u32[]{:S(2)}, u32[]{:S(2)}) collective-permute-start(f32[8,64,128]{2,1,0:T(8,128)S(1)} %get-tuple-element.40), channel_id=1, source_target_pairs={{1,2},{2,1},{5,6},{6,5},{9,10},{10,9},{13,14},{14,13},{17,18},{18,... | collective-permute-start | bytes 786440 | tf_op jit(solution)/shard_map/ppermute | solution.py:448
  22.9 3.2 %collective-permute-start.6 = (f32[2,2,8,128]{3,2,1,0:T(8,128)S(1)}, f32[2,2,8,128]{3,2,1,0:T(8,128)S(1)}, u32[]{:S(2)}, u32[]{:S(2)}) collective-permute-start(f32[2,2,8,128]{3,2,1,0:T(8,128)S(1)} %pad_maximum_fusion.refs_0_), channel_id=1, source_target_pairs={{12,0},{0,4},{4,8},{8,12},{13,1},{1,5},{5,9},{9,13},{14,2},{2,6},{... | collective-permute-start | bytes 49160 | tf_op jit(solution)/shard_map/ppermute | solution.py:508
  23.0 3.8 %collective-permute-start.5 = (f32[2,2,8,128]{3,2,1,0:T(8,128)S(1)}, f32[2,2,8,128]{3,2,1,0:T(8,128)S(1)}, u32[]{:S(2)}, u32[]{:S(2)}) collective-permute-start(f32[2,2,8,128]{3,2,1,0:T(8,128)S(1)} %pad_maximum_fusion.refs_0_), channel_id=1, source_target_pairs={{8,0},{12,4},{0,8},{4,12},{9,1},{13,5},{1,9},{5,13},{10,2},{14,6},... | collective-permute-start | bytes 49160 | tf_op jit(solution)/shard_map/ppermute | solution.py:508
  23.6 3.2 %collective-permute-start.4 = (f32[2,2,8,128]{3,2,1,0:T(8,128)S(1)}, f32[2,2,8,128]{3,2,1,0:T(8,128)S(1)}, u32[]{:S(2)}, u32[]{:S(2)}) collective-permute-start(f32[2,2,8,128]{3,2,1,0:T(8,128)S(1)} %pad_maximum_fusion.refs_0_), channel_id=1, source_target_pairs={{4,0},{8,4},{12,8},{0,12},{5,1},{9,5},{13,9},{1,13},{6,2},{10,6},{... | collective-permute-start | bytes 49160 | tf_op jit(solution)/shard_map/ppermute | solution.py:508
  26.9 9.4 %collective-permute-start.9 = (f32[544,128]{1,0:T(8,128)S(1)}, f32[544,128]{1,0:T(8,128)S(1)}, u32[]{:S(2)}, u32[]{:S(2)}) collective-permute-start(f32[544,128]{1,0:T(8,128)S(1)} %get-tuple-element.41), channel_id=1, source_target_pairs={{0,1},{1,0},{2,3},{3,2},{4,5},{5,4},{6,7},{7,6},{8,9},{9,8},{10,11... | collective-permute-start | bytes 835592 | tf_op jit(solution)/shard_map/ppermute | solution.py:448
  27.0 11.2 %collective-permute-start.10 = (f32[544,128]{1,0:T(8,128)S(1)}, f32[544,128]{1,0:T(8,128)S(1)}, u32[]{:S(2)}, u32[]{:S(2)}) collective-permute-start(f32[544,128]{1,0:T(8,128)S(1)} %get-tuple-element.42), channel_id=1, source_target_pairs={{1,2},{2,1},{5,6},{6,5},{9,10},{10,9},{13,14},{14,13},{17,18},{18,... | collective-permute-start | bytes 835592 | tf_op jit(solution)/shard_map/ppermute | solution.py:448

commit v3 on v2

v3 whole, which is shorter than its diff:
```python
import functools

import jax
import jax.numpy as jnp
from jax import lax
from jax.experimental import pallas as pl
from jax.experimental.pallas import tpu as pltpu
from jax.sharding import PartitionSpec as P

HALO = 8
REACH = 6
SUB = 8
F32 = jnp.float32
BF16 = jnp.bfloat16
VMEM_LIMIT = 24 * 1024 * 1024
EDGE_LIMIT = int(24 * 1024 * 1024)
UNROLL = 4
LARGEST = 64.0


def pitch_of(columns):
    return columns + 1


def loop(count, body):
    def step(i, carry):
        body(i)
        return carry

    lax.fori_loop(0, count, step, 0, unroll=min(count, UNROLL))


def bits_of(shift):
    moved = jnp.broadcast_to(shift, (SUB, shift.shape[-1])) + REACH
    return {b: (moved & b) != 0 for b in (8, 4, 2, 1)}


def rows_of(taps):
    return [jnp.broadcast_to(taps[k : k + 1, :], (SUB, taps.shape[-1])) for k in range(4)]


def choose(mask, yes, no):
    if yes is None and no is None:
        return None
    if yes is None:
        return jnp.where(mask, 0.0, no)
    if no is None:
        return jnp.where(mask, yes, 0.0)
    return jnp.where(mask, yes, no)


def resample(get, bits, taps, indices, flipped):
    way = -1 if flipped else 1
    memo = {}

    def stage(b, i):
        if b == 16:
            key = (b, i)
            if key not in memo:
                memo[key] = get(i)
            return memo[key]
        key = (b, i)
        if key not in memo:
            memo[key] = choose(bits[b], stage(2 * b, i + way * b), stage(2 * b, i))
        return memo[key]

    for i in indices:
        total = None
        for k in range(4):
            v = stage(1, i + 7 - k if flipped else i - 7 + k)
            if v is not None:
                total = taps[k] * v if total is None else total + taps[k] * v
        yield i, total


def halves(x):
    hi = x.astype(BF16)
    lo = (x - hi.astype(F32)).astype(BF16)
    return jnp.concatenate([hi, lo], axis=1)


def scan_matrix(planes, before):
    a = lax.broadcasted_iota(jnp.int32, (2 * planes, 2 * planes), 0)
    b = lax.broadcasted_iota(jnp.int32, (2 * planes, 2 * planes), 1)
    a = jnp.where(a >= planes, a - planes, a)
    ordered = (a < b) if before else (a > b)
    return jnp.where((b >= planes) | ordered, 1.0, 0.0).astype(BF16)


def edge_kernel(where_ref, field_ref, a_ref, b_ref, left_ref, right_ref, sems):
    rows, columns, _ = field_ref.shape
    copies = [
        pltpu.make_async_copy(field_ref.at[:, pl.ds(at, HALO), :], held, sems.at[n])
        for n, (at, held) in enumerate(((0, left_ref), (columns - HALO, right_ref)))
    ]
    for c in copies:
        c.start()
    odd = where_ref[0] == 1
    for c in copies:
        c.wait()

    def body(y):
        left, right = left_ref[y], right_ref[y]
        a_ref[y] = jnp.where(odd, left, right)
        b_ref[y] = jnp.where(odd, right, left)

    loop(rows, body)


def absorbed(optical, bound):
    series = 1 / 120
    for k in (-1 / 24, 1 / 6, -1 / 2, 1.0):
        series = series * optical + k
    series = series * optical
    return series if bound <= 0.125 else jnp.where(optical < 0.125, series, 1.0 - jnp.exp(-optical))


def march(optical, matrix, bound):
    planes = optical.shape[1]
    sums = jnp.dot(halves(optical), matrix, preferred_element_type=F32)
    transmit = jnp.exp(-sums[:, :planes])
    q = transmit * absorbed(optical, bound)
    return q, transmit - q, sums[:, planes:]


def inner_kernel(
    all_planes, d_ref, e_ref, row_taps_ref, row_shift_ref, taps_ref, shift_ref, scale_ref, cotangent_ref,
    rd_ref, re_ref, q_ref, p_ref, dense_ref, weight_ref,
):
    rows, columns, planes = d_ref.shape
    row_bits = bits_of(row_shift_ref[...])
    row_taps = rows_of(row_taps_ref[...])
    pitch = pitch_of(columns)
    per = 128 // columns
    cotangent = jnp.transpose(cotangent_ref[...])
    for group in range(rows // SUB):
        at = group % per * columns
        weight_ref[group // per, :, at : at + columns] = cotangent[group * SUB : (group + 1) * SUB, :]

    def row_body(t):
        at = pl.multiple_of(t * SUB, SUB)
        for ref, out in ((d_ref, rd_ref), (e_ref, re_ref)):
            get = lambda y: ref[y, pl.ds(at, SUB), :] if 0 <= y < rows else None
            for y, v in resample(get, row_bits, row_taps, range(rows), False):
                out[pl.ds(y * pitch + at, SUB), :] = v

    loop(columns // SUB, row_body)
    bits = bits_of(shift_ref[...])
    taps = rows_of(taps_ref[...])
    scale = jnp.broadcast_to(scale_ref[...] / all_planes, (SUB, planes))
    before, after = scan_matrix(planes, True), scan_matrix(planes, False)
    dense_ref[...] = jnp.zeros_like(dense_ref)
    inside = range(HALO, columns - HALO)

    def body(group):
        y0 = group * SUB
        at = pl.multiple_of(y0, SUB)
        get = column_get(rd_ref, None, y0, columns)
        optical = jnp.concatenate([scale * v for _, v in resample(get, bits, taps, inside, False)], axis=0)
        q, n, totals = march(optical, before, LARGEST / all_planes)
        pack_totals(totals, dense_ref.at[0], group, columns, inside)
        get = column_get(re_ref, None, y0, columns)
        emission = jnp.concatenate([v for _, v in resample(get, bits, taps, inside, False)], axis=0)
        sums = jnp.dot(halves(q * emission), after, preferred_element_type=F32)
        pack_totals(sums[:, planes:], dense_ref.at[1], group, columns, inside)
        p = n * emission - sums[:, :planes]
        for i in range(len(inside)):
            q_ref[i, pl.ds(at, SUB), :] = q[i * SUB : (i + 1) * SUB]
            p_ref[i, pl.ds(at, SUB), :] = scale * p[i * SUB : (i + 1) * SUB]

    loop(rows // SUB, body)


def row_halo(odd, a_ref, b_ref, halo_ref, bits, taps):
    rows = a_ref.shape[0]
    for side in range(2):
        use_a = odd == (1 - side)
        get = lambda y: jnp.where(use_a, a_ref[y], b_ref[y]) if 0 <= y < rows else None
        for y, v in resample(get, bits, taps, range(rows), False):
            halo_ref[pl.ds(y * pitch_of(2 * HALO) + side * HALO, SUB), :] = v


def column_get(r_ref, halo_ref, y0, columns):
    pitch, side_pitch = pitch_of(columns), pitch_of(2 * HALO)

    def get(x):
        reach = 0 if halo_ref is None else HALO
        if x < -reach or x >= columns + reach:
            return None
        if x < 0:
            return halo_ref[pl.ds(y0 * side_pitch + x + HALO, SUB, stride=side_pitch), :]
        if x >= columns:
            return halo_ref[pl.ds(y0 * side_pitch + HALO + x - columns, SUB, stride=side_pitch), :]
        return r_ref[pl.ds(y0 * pitch + x, SUB, stride=pitch), :]

    return get


def pack_totals(totals, dense_ref, group, columns, inside):
    lane = lax.broadcasted_iota(jnp.int32, (SUB, 128), 1)
    per = 128 // columns
    packed = jnp.zeros((SUB, 128), F32)
    base = (group % per) * columns
    for i, x in enumerate(inside):
        packed = jnp.where(lane == base + x, totals[i * SUB : (i + 1) * SUB, :], packed)
    dense_ref[group // per] += packed


def outside_of(columns):
    return [*range(HALO), *range(columns - HALO, columns)]


def density_kernel(
    all_planes, odd_ref, rd_ref, a_ref, b_ref, inner_ref, row_taps_ref, row_shift_ref, taps_ref, shift_ref, scale_ref,
    q_ref, n_ref, qa_ref, qb_ref, dense_ref, halo_ref,
):
    odd = odd_ref[0]
    rows, planes = q_ref.shape[1:]
    columns = rd_ref.shape[0] // rows - 1
    row_halo(odd, a_ref, b_ref, halo_ref, bits_of(row_shift_ref[...]), rows_of(row_taps_ref[...]))
    bits = bits_of(shift_ref[...])
    taps = rows_of(taps_ref[...])
    scale = jnp.broadcast_to(scale_ref[...] / all_planes, (SUB, planes))
    matrix = scan_matrix(planes, True)
    dense_ref[...] = inner_ref[0]
    outside = outside_of(columns)

    def body(group):
        y0 = group * SUB
        at = pl.multiple_of(y0, SUB)
        get = column_get(rd_ref, halo_ref, y0, columns)
        optical = jnp.concatenate([scale * v for _, v in resample(get, bits, taps, outside, False)], axis=0)
        q, n, totals = march(optical, matrix, LARGEST / all_planes)
        for i in range(len(outside)):
            q_ref[i, pl.ds(at, SUB), :] = q[i * SUB : (i + 1) * SUB]
            n_ref[i, pl.ds(at, SUB), :] = n[i * SUB : (i + 1) * SUB]
        pack_totals(totals, dense_ref, group, columns, outside)

    loop(rows // SUB, body)
    for ref, at in ((qa_ref, jnp.where(odd == 1, 0, HALO)), (qb_ref, jnp.where(odd == 1, HALO, 0))):
        ref[...] = q_ref[pl.ds(at, HALO)]


def emission_kernel(
    all_planes, odd_ref, re_ref, a_ref, b_ref, q_ref, n_ref, inner_ref, optical_ref, row_taps_ref, row_shift_ref, taps_ref, shift_ref, scale_ref,
    p_ref, pa_ref, pb_ref, dense_ref, halo_ref,
):
    odd = odd_ref[0]
    rows, planes = p_ref.shape[1:]
    columns = re_ref.shape[0] // rows - 1
    row_halo(odd, a_ref, b_ref, halo_ref, bits_of(row_shift_ref[...]), rows_of(row_taps_ref[...]))
    bits = bits_of(shift_ref[...])
    taps = rows_of(taps_ref[...])
    scale = jnp.broadcast_to(scale_ref[...] / all_planes, (SUB, planes))
    matrix = scan_matrix(planes, False)
    dense_ref[0] = optical_ref[...]
    dense_ref[1] = inner_ref[1]
    outside = outside_of(columns)

    def body(group):
        y0 = group * SUB
        at = pl.multiple_of(y0, SUB)
        get = column_get(re_ref, halo_ref, y0, columns)
        pieces = [v for _, v in resample(get, bits, taps, outside, False)]
        light = jnp.concatenate([q_ref[i, pl.ds(at, SUB), :] * v for i, v in enumerate(pieces)], axis=0)
        sums = jnp.dot(halves(light), matrix, preferred_element_type=F32)
        for i, v in enumerate(pieces):
            behind = sums[i * SUB : (i + 1) * SUB, :planes]
            p_ref[i, pl.ds(at, SUB), :] = scale * (n_ref[i, pl.ds(at, SUB), :] * v - behind)
        pack_totals(sums[:, planes:], dense_ref.at[1], group, columns, outside)

    loop(rows // SUB, body)
    for ref, at in ((pa_ref, jnp.where(odd == 1, 0, HALO)), (pb_ref, jnp.where(odd == 1, HALO, 0))):
        ref[...] = p_ref[pl.ds(at, HALO)]


def merge(later, mine, other, front, back):
    (depth, light), (depth_2, light_2) = mine, other
    dim = jnp.exp(-jnp.where(later, depth_2, depth))
    joined = (depth + depth_2, jnp.where(later, light_2 + dim * light, light + dim * light_2))
    return joined, jnp.where(later, front + depth_2, front), jnp.where(later, back * dim, back + dim * light_2)


def merge_kernel(step, last, where_ref, weight_ref, mine_ref, other_ref, *refs):
    later = (where_ref[1] & (1 << step)) != 0
    outs = refs if step == 0 else refs[1:]
    for c in range(weight_ref.shape[0]):
        zero = jnp.zeros_like(weight_ref[c])
        front, back = (zero, zero) if step == 0 else (refs[0][0, c], refs[0][1, c])
        joined, front, back = merge(
            later, (mine_ref[0, c], mine_ref[1, c]), (other_ref[0, c], other_ref[1, c]), front, back
        )
        if last:
            outs[0][0, c] = weight_ref[c] * jnp.exp(-front)
            outs[0][1, c] = weight_ref[c] * back
        else:
            outs[0][0, c], outs[0][1, c] = joined
            outs[1][0, c], outs[1][1, c] = front, back


def lay(split_ref, row, dense, base, first, count):
    lane = lax.broadcasted_iota(jnp.int32, (SUB, 128), 1)
    masks = [lane == base + first + x for x in range(count)]
    hi = dense.astype(BF16).astype(F32)
    stacks = [
        jnp.concatenate([jnp.where(m, part, 0.0) for m in masks], axis=0).astype(BF16) for part in (hi, dense - hi)
    ]
    split_ref[row : row + count * SUB, :] = jnp.concatenate(stacks, axis=1)


def spread(split_ref, out_ref):
    out_ref[...] = jnp.dot(split_ref[...], jnp.ones((256, 128), BF16), preferred_element_type=F32)


def finish_rows(ref, pitch, at, bits, taps, held, out, sems):
    rows = held.shape[0]
    half = rows // 2
    copies = []
    get = lambda y: ref[pl.ds(y * pitch + at, SUB), :] if 0 <= y < rows else None
    for y, v in resample(get, bits, taps, range(rows), True):
        held[y] = v
        if y % half == half - 1:
            part = pl.ds(y + 1 - half, half)
            copies.append(pltpu.make_async_copy(held.at[part], out.at[part], sems.at[y // half]))
            copies[-1].start()
    return copies


def own_kernel(
    all_planes, p_in, q_in, p_out, q_out, own_ref, row_taps_ref, row_shift_ref, taps_ref, shift_ref, scale_ref,
    gd_ref, ge_ref, td_ref, te_ref, cd_ref, ce_ref, held_ref, split_ref, weight_ref, sems,
):
    inner, rows, planes = p_in.shape
    columns = inner + 2 * HALO
    per = 128 // columns
    groups = rows // SUB
    pitch, side_pitch = pitch_of(inner), pitch_of(2 * HALO)
    bits = bits_of(shift_ref[...])
    taps = rows_of(taps_ref[...])
    scale = jnp.broadcast_to(scale_ref[...] / all_planes, (SUB, planes))

    for group in range(groups):
        lay(split_ref, group * columns * SUB, own_ref[0, group // per], group % per * columns, 0, columns)
    spread(split_ref, weight_ref)

    for group in range(groups):
        y0 = group * SUB
        back = own_ref[1, group // per]

        def front_at(x):
            row = (group * columns + x) * SUB
            return weight_ref[row : row + SUB, :]

        def back_at(x):
            lane = group % per * columns + x
            return jnp.broadcast_to(back[:, lane : lane + 1], (SUB, 128)) * scale

        def local(inside, outside, x):
            if HALO <= x < columns - HALO:
                return inside[x - HALO, y0 : y0 + SUB, :]
            return outside[x if x < HALO else x - inner, y0 : y0 + SUB, :]

        def get_d(x):
            if not 0 <= x < columns:
                return None
            return front_at(x) * local(p_in, p_out, x) - back_at(x)

        def get_e(x):
            if not 0 <= x < columns:
                return None
            return front_at(x) * local(q_in, q_out, x)

        for get, inside, outside in ((get_d, cd_ref, td_ref), (get_e, ce_ref, te_ref)):
            for x, v in resample(get, bits, taps, range(columns), True):
                if HALO <= x < columns - HALO:
                    inside[pl.ds(y0 * pitch + x - HALO, SUB, stride=pitch), :] = v
                else:
                    to = x if x < HALO else x - inner
                    outside[pl.ds(y0 * side_pitch + to, SUB, stride=side_pitch), :] = v

    row_bits = bits_of(row_shift_ref[...])
    row_taps = rows_of(row_taps_ref[...])
    copies = []
    for f, (ref, out) in enumerate(((cd_ref, gd_ref), (ce_ref, ge_ref))):
        for t in range(inner // SUB):
            copies += finish_rows(
                ref, pitch, t * SUB, row_bits, row_taps, held_ref.at[f, t],
                out.at[:, pl.ds(HALO + t * SUB, SUB), :], sems.at[f, t],
            )
    for c in copies:
        c.wait()


def outer_kernel(
    all_planes, odd_ref, pa_ref, pb_ref, qa_ref, qb_ref, wa_ref, wb_ref, td_ref, te_ref,
    row_taps_ref, row_shift_ref, taps_ref, shift_ref, scale_ref, gd_in, ge_in,
    gd_ref, ge_ref, cd_ref, ce_ref, held_ref, split_ref, weight_ref, sems,
):
    odd = odd_ref[0]
    rows, columns, planes = gd_ref.shape
    per = 128 // columns
    groups = rows // SUB
    pitch = pitch_of(2 * HALO)
    bits = bits_of(shift_ref[...])
    taps = rows_of(taps_ref[...])
    scale = jnp.broadcast_to(scale_ref[...] / all_planes, (SUB, planes))
    use_a = (odd == 1, odd != 1)

    for side in range(2):
        for group in range(groups):
            row = (side * groups + group) * HALO * SUB
            dense = jnp.where(use_a[side], wa_ref[0, group // per], wb_ref[0, group // per])
            lay(split_ref, row, dense, group % per * columns, columns - HALO if side == 0 else 0, HALO)
    spread(split_ref, weight_ref)

    for group in range(groups):
        y0 = group * SUB
        for side in range(2):
            start = -HALO if side == 0 else HALO
            back = jnp.where(use_a[side], wa_ref[1, group // per], wb_ref[1, group // per])

            def front_at(i):
                row = ((side * groups + group) * HALO + i) * SUB
                return weight_ref[row : row + SUB, :]

            def back_at(i):
                lane = group % per * columns + i + (columns - HALO if side == 0 else 0)
                return jnp.broadcast_to(back[:, lane : lane + 1], (SUB, 128)) * scale

            def get_d(x):
                i = x - start
                if not 0 <= i < HALO:
                    return None
                v = jnp.where(use_a[side], pa_ref[i, y0 : y0 + SUB, :], pb_ref[i, y0 : y0 + SUB, :])
                return front_at(i) * v - back_at(i)

            def get_e(x):
                i = x - start
                if not 0 <= i < HALO:
                    return None
                v = jnp.where(use_a[side], qa_ref[i, y0 : y0 + SUB, :], qb_ref[i, y0 : y0 + SUB, :])
                return front_at(i) * v

            for get, ref, out in ((get_d, td_ref, cd_ref), (get_e, te_ref, ce_ref)):
                for x, v in resample(get, bits, taps, range(HALO), True):
                    at = pl.ds(y0 * pitch + side * HALO + x, SUB, stride=pitch)
                    out[at, :] = ref[at, :] if v is None else ref[at, :] + v

    row_bits = bits_of(row_shift_ref[...])
    row_taps = rows_of(row_taps_ref[...])
    copies = []
    for f, (ref, out) in enumerate(((cd_ref, gd_ref), (ce_ref, ge_ref))):
        for side in range(2):
            copies += finish_rows(
                ref, pitch, side * HALO, row_bits, row_taps, held_ref.at[f, side],
                out.at[:, pl.ds(side * (columns - HALO), HALO), :], sems.at[f, side],
            )
    for c in copies:
        c.wait()


def near(value):
    big = value.size >= 1 << 16
    return pltpu.with_memory_space_constraint(value, pltpu.VMEM) if big else value


def call(kernel, outs, scalars, vmem, scratch=(), hbm_in=(), hbm_out=0, aliases=None, micros=2.0, limit=VMEM_LIMIT):
    whole, far = pl.BlockSpec(memory_space=pltpu.VMEM), pl.BlockSpec(memory_space=pl.ANY)
    return pl.pallas_call(
        kernel,
        out_shape=[jax.ShapeDtypeStruct(s, F32) if i < hbm_out else pltpu.VMEM(s, F32) for i, s in enumerate(outs)],
        in_specs=[pl.BlockSpec(memory_space=pltpu.SMEM)] * len(scalars)
        + [whole] * len(vmem)
        + [far] * len(hbm_in),
        out_specs=[far] * hbm_out + [whole] * (len(outs) - hbm_out),
        scratch_shapes=list(scratch),
        input_output_aliases=aliases or {},
        compiler_params=pltpu.CompilerParams(vmem_limit_bytes=limit),
        cost_estimate=pl.CostEstimate(
            flops=int(micros * 1e6), bytes_accessed=int(micros * 3.0e6), transcendentals=0
        ),
    )(*scalars, *[near(v) for v in vmem], *[pltpu.with_memory_space_constraint(v, pltpu.HBM) for v in hbm_in])


def swap(value, axis, parity):
    count = lax.axis_size(axis)
    pairs = []
    for i in range(parity, count - 1, 2):
        pairs += [(i, i + 1), (i + 1, i)]
    return lax.ppermute(value, axis, pairs)


def on_device(density, emission, taps, shift, row_taps, row_shift, step_length, cotangent):
    rows, columns, planes = density.shape
    slabs = lax.axis_size("depth")
    all_planes = planes * slabs
    per = 128 // columns
    chunks = rows // SUB // per
    shift, row_shift = shift[None, :], row_shift[None, :]
    scale = step_length[None, :]
    place = jnp.stack([lax.axis_index("screen") % 2, lax.axis_index("depth")]).astype(jnp.int32)
    where = jnp.broadcast_to(place[:, None, None], (2, SUB, 128))
    edge = (rows, HALO, planes)
    sides = []
    for field in (density, emission):
        a, b = call(
            edge_kernel,
            [edge] * 2,
            [],
            [where],
            [pltpu.VMEM(edge, F32), pltpu.VMEM(edge, F32), pltpu.SemaphoreType.DMA((2,))],
            hbm_in=[field],
            micros=0.2,
        )
        sides.append((swap(a, "screen", 0), swap(b, "screen", 1)))
    (da, db), (ea, eb) = sides
    flat = (rows * pitch_of(columns), planes)
    inside = (columns - 2 * HALO, rows, planes)
    outside = (2 * HALO, rows, planes)
    side = (HALO, rows, planes)
    dense = (chunks, SUB, 128)
    rd, re, q_in, p_in, inner_sums, weight = call(
        functools.partial(inner_kernel, all_planes),
        [flat, flat, inside, inside, (2,) + dense, dense],
        [],
        [density, emission, row_taps, row_shift, taps, shift, scale, cotangent.T],
        micros=3.0,
    )
    outer = (rows * pitch_of(2 * HALO), planes)
    q_out, n_out, qa, qb, slab_optical = call(
        functools.partial(density_kernel, all_planes),
        [outside, outside, side, side, dense],
        [place],
        [rd, da, db, inner_sums, row_taps, row_shift, taps, shift, scale],
        [pltpu.VMEM(outer, F32)],
    )
    qa, qb = swap(qa, "screen", 0), swap(qb, "screen", 1)
    p_out, pa, pb, state = call(
        functools.partial(emission_kernel, all_planes),
        [outside, side, side, (2,) + dense],
        [place],
        [re, ea, eb, q_out, n_out, inner_sums, slab_optical, row_taps, row_shift, taps, shift, scale],
        [pltpu.VMEM(outer, F32)],
        micros=6.0,
    )
    rounds = slabs.bit_length() - 1
    assert slabs == 1 << rounds and rounds
    sums = (2,) + dense
    around = []
    for step in range(rounds):
        last = step == rounds - 1
        if last:
            pa, pb = swap(pa, "screen", 0), swap(pb, "screen", 1)
        other = lax.ppermute(state, "depth", [(i, i ^ (1 << step)) for i in range(slabs)])
        state, *around = call(
            functools.partial(merge_kernel, step, last),
            [sums] * (1 if last else 2),
            [],
            [where, weight, state, other] + around,
            micros=0.1,
        )
    own, qa, qb = lax.optimization_barrier((state, qa, qb))
    wa, wb = swap(own, "screen", 0), swap(own, "screen", 1)
    inner = (rows * pitch_of(columns - 2 * HALO), planes)
    halves_of = rows * columns
    gd, ge, td, te = call(
        functools.partial(own_kernel, all_planes),
        [density.shape, density.shape, outer, outer],
        [],
        [p_in, q_in, p_out, q_out, own, row_taps, row_shift, taps, shift, scale],
        [
            pltpu.VMEM(inner, F32),
            pltpu.VMEM(inner, F32),
            pltpu.VMEM((2, (columns - 2 * HALO) // SUB, rows, SUB, planes), F32),
            pltpu.VMEM((halves_of, 256), BF16),
            pltpu.VMEM((halves_of, planes), F32),
            pltpu.SemaphoreType.DMA((2, (columns - 2 * HALO) // SUB, 2)),
        ],
        hbm_out=2,
        micros=6.0,
    )
    halves_of = rows * HALO * 2
    gd, ge = call(
        functools.partial(outer_kernel, all_planes),
        [density.shape, density.shape],
        [place],
        [pa, pb, qa, qb, wa, wb, td, te, row_taps, row_shift, taps, shift, scale],
        [
            pltpu.VMEM(outer, F32),
            pltpu.VMEM(outer, F32),
            pltpu.VMEM((2, 2, rows, HALO, planes), F32),
            pltpu.VMEM((halves_of, 256), BF16),
            pltpu.VMEM((halves_of, planes), F32),
            pltpu.SemaphoreType.DMA((2, 2, 2)),
        ],
        hbm_in=[gd, ge],
        hbm_out=2,
        aliases={14: 0, 15: 1},
    )
    return gd, ge


def solution(mesh):
    in_specs = (
        P("groups", "screen", "depth"),
        P("groups", "screen", "depth"),
        P("groups", "depth"),
        P(("groups", "depth")),
        P("groups", "depth"),
        P(("groups", "depth")),
        P(("groups", "depth")),
        P("groups", "screen"),
    )
    out_specs = (P("groups", "screen", "depth"), P("groups", "screen", "depth"))
    return jax.shard_map(
        on_device, mesh=mesh, in_specs=in_specs, out_specs=out_specs, check_vma=False
    )
```

time: 41 us -> 39.4 us (0.961)
  the two profiles are of different devices: /device:TPU:14 before, /device:TPU:0 now
where the time goes in v3:
time: 39.4 us; the launch traced here: 39.1 us
  starting transfers between devices  21.5 us (55%)
  Pallas kernels  13 us (33%)
  waiting for transfers between devices  3.44 us (9%)
  between operations  0.94 us (2%)
    ppermute x10, starting transfers between devices, swap(): return lax.ppermute(value, axis, pairs)  19.9 us
    pallas_call x9, Pallas kernels, call(): pl.pallas_call(kernel, out_shape=[jax.ShapeDtypeStruct(s, F32) if i < hbm...  13 us
    ppermute x2, waiting for transfers between devices, on_device(): lax.ppermute(state, 'depth', [(i, i ^ 1 << step) for i in range(slabs)])  3.42 us
    ppermute x2, starting transfers between devices, on_device(): lax.ppermute(state, 'depth', [(i, i ^ 1 << step) for i in range(slabs)])  1.63 us
  transfers between devices with their start and end apart: 12, of which 2 were waited for; matrix products, arithmetic and copies ran while one was open for 0% of the time, Pallas kernels for 23%

profile of v3, /device:TPU:0, one launch (start us, length us, event | category | flops | bytes accessed | tf_op | source)
XLA Modules:
  0.0 39.1 jit_solution(4664755421129162920)
XLA Ops:
  0.6 0.0 copy-start
  0.6 0.0 copy-start.1
  0.7 0.0 copy-start.2
  0.7 0.0 copy-start.3
  0.7 0.0 copy-start.4
  0.7 0.0 copy-start.5
  0.7 0.0 copy-start.6
  0.7 0.0 copy-start.7
  0.7 0.1 pad_add_fusion.odd_ref
  0.8 0.1 broadcast_in_dim.18.where_ref
  0.9 1.3 %shard_map.97 = (f32[64,8,128]{2,1,0:T(8,128)S(1)}, f32[64,8,128]{2,1,0:T(8,128)S(1)}) custom-call(s32[2,8,128]{2,1,0:T(8,128)S(1)} %broadcast_in_dim.18.where_ref, f32[64,32,128]{2,1,0:T(8,128)} %field_ref.3), custom_call_target="tpu_custom_call" | custom-call | flops 200000 | bytes 600000 | tf_op jit(solution)/shard_map/pallas_call | solution.py:469
  2.1 3.1 %collective-permute-start.2 = (f32[64,8,128]{2,1,0:T(8,128)S(1)}, f32[64,8,128]{2,1,0:T(8,128)S(1)}, u32[]{:S(2)}, u32[]{:S(2)}) collective-permute-start(f32[64,8,128]{2,1,0:T(8,128)S(1)} %get-tuple-element.34), channel_id=1, source_target_pairs={{0,1},{1,0},{2,3},{3,2},{4,5},{5,4},{6,7},{7,6},{8,9},{9,8},{10,11... | collective-permute-start | bytes 786440 | tf_op jit(solution)/shard_map/ppermute | solution.py:490
  5.2 0.7 %collective-permute-start.3 = (f32[64,8,128]{2,1,0:T(8,128)S(1)}, f32[64,8,128]{2,1,0:T(8,128)S(1)}, u32[]{:S(2)}, u32[]{:S(2)}) collective-permute-start(f32[64,8,128]{2,1,0:T(8,128)S(1)} %get-tuple-element.35), channel_id=1, source_target_pairs={{1,2},{2,1},{5,6},{6,5},{9,10},{10,9},{13,14},{14,13},{17,18},{18,... | collective-permute-start | bytes 786440 | tf_op jit(solution)/shard_map/ppermute | solution.py:490
  5.9 1.1 %shard_map.96 = (f32[64,8,128]{2,1,0:T(8,128)S(1)}, f32[64,8,128]{2,1,0:T(8,128)S(1)}) custom-call(s32[2,8,128]{2,1,0:T(8,128)S(1)} %broadcast_in_dim.18.where_ref, f32[64,32,128]{2,1,0:T(8,128)} %field_ref.2), custom_call_target="tpu_custom_call" | custom-call | flops 200000 | bytes 600000 | tf_op jit(solution)/shard_map/pallas_call | solution.py:469
  7.1 4.4 %collective-permute-start = (f32[64,8,128]{2,1,0:T(8,128)S(1)}, f32[64,8,128]{2,1,0:T(8,128)S(1)}, u32[]{:S(2)}, u32[]{:S(2)}) collective-permute-start(f32[64,8,128]{2,1,0:T(8,128)S(1)} %get-tuple-element.31), channel_id=1, source_target_pairs={{0,1},{1,0},{2,3},{3,2},{4,5},{5,4},{6,7},{7,6},{8,9},{9,8},{10,11... | collective-permute-start | bytes 786440 | tf_op jit(solution)/shard_map/ppermute | solution.py:490
  11.5 0.7 %collective-permute-start.1 = (f32[64,8,128]{2,1,0:T(8,128)S(1)}, f32[64,8,128]{2,1,0:T(8,128)S(1)}, u32[]{:S(2)}, u32[]{:S(2)}) collective-permute-start(f32[64,8,128]{2,1,0:T(8,128)S(1)} %get-tuple-element.32), channel_id=1, source_target_pairs={{1,2},{2,1},{5,6},{6,5},{9,10},{10,9},{13,14},{14,13},{17,18},{18,... | collective-permute-start | bytes 786440 | tf_op jit(solution)/shard_map/ppermute | solution.py:490
  12.2 0.0 copy-done
  12.2 0.0 copy-done.1
  12.2 0.0 copy-done.2
  12.2 0.0 copy-done.3
  12.2 0.0 copy-done.4
  12.2 0.0 copy-done.5
  12.2 0.0 copy-done.6
  12.3 2.1 %shard_map.95 = (f32[2112,128]{1,0:T(8,128)S(1)}, f32[2112,128]{1,0:T(8,128)S(1)}, f32[16,64,128]{2,1,0:T(8,128)S(1)}, f32[16,64,128]{2,1,0:T(8,128)S(1)}, f32[2...) custom-call(f32[64,32,128]{2,1,0:T(8,128)S(1)} %copy-done, f32[64,32,128]{2,1,0:T(8,128)S(1)} %copy-done.1, ...), custom_call_target="tpu_custom_call" | custom-call | flops 3000000 | bytes 9000000 | tf_op jit(solution)/shard_map/pallas_call | solution.py:469
  14.4 0.0 collective-permute-done.2.a_ref
  14.4 0.0 collective-permute-done.3.b_ref
  14.4 1.6 %shard_map.98 = (f32[16,64,128]{2,1,0:T(8,128)S(1)}, f32[16,64,128]{2,1,0:T(8,128)S(1)}, f32[8,64,128]{2,1,0:T(8,128)S(1)}, f32[8,64,128]{2,1,0:T(8,128)S(1)}, f32[2,8,128]{2,1,0:T(8,128)S(1)}) custom-call(s32[2]{0:T(128)S(1)} %pad_add_fusion.odd_ref, f32[2112,128]{1,0:T(8,128)S(1)} %get-tuple-element.33.rd_ref, ...), custom_call_target="tpu_custom_call" | custom-call | flops 2000000 | bytes 6000000 | tf_op jit(solution)/shard_map/pallas_call | solution.py:469
  16.0 2.9 %collective-permute-start.8 = (f32[8,64,128]{2,1,0:T(8,128)S(1)}, f32[8,64,128]{2,1,0:T(8,128)S(1)}, u32[]{:S(2)}, u32[]{:S(2)}) collective-permute-start(f32[8,64,128]{2,1,0:T(8,128)S(1)} %get-tuple-element.46), channel_id=1, source_target_pairs={{0,1},{1,0},{2,3},{3,2},{4,5},{5,4},{6,7},{7,6},{8,9},{9,8},{10,11... | collective-permute-start | bytes 786440 | tf_op jit(solution)/shard_map/ppermute | solution.py:490
  18.9 0.7 %collective-permute-start.9 = (f32[8,64,128]{2,1,0:T(8,128)S(1)}, f32[8,64,128]{2,1,0:T(8,128)S(1)}, u32[]{:S(2)}, u32[]{:S(2)}) collective-permute-start(f32[8,64,128]{2,1,0:T(8,128)S(1)} %get-tuple-element.47), channel_id=1, source_target_pairs={{1,2},{2,1},{5,6},{6,5},{9,10},{10,9},{13,14},{14,13},{17,18},{18,... | collective-permute-start | bytes 786440 | tf_op jit(solution)/shard_map/ppermute | solution.py:490
  19.6 0.0 collective-permute-done.a_ref
  19.6 0.0 collective-permute-done.1.b_ref
  19.6 1.5 %shard_map.99 = (f32[16,64,128]{2,1,0:T(8,128)S(1)}, f32[8,64,128]{2,1,0:T(8,128)S(1)}, f32[8,64,128]{2,1,0:T(8,128)S(1)}, f32[2,2,8,128]{3,2,1,0:T(8,128)S(1)}) custom-call(s32[2]{0:T(128)S(1)} %pad_add_fusion.odd_ref, f32[2112,128]{1,0:T(8,128)S(1)} %get-tuple-element.30.re_ref, f32[64,8,128]{2,1,0:T(8,128)S(1)} %collective-permute-done.a_ref, ...), custom_call_target="tpu_custom_call" | custom-call | flops 6000000 | bytes 18000000 | tf_op jit(solution)/shard_map/pallas_call | solution.py:469
  21.2 3.6 %collective-permute-start.4 = (f32[8,64,128]{2,1,0:T(8,128)S(1)}, f32[8,64,128]{2,1,0:T(8,128)S(1)}, u32[]{:S(2)}, u32[]{:S(2)}) collective-permute-start(f32[8,64,128]{2,1,0:T(8,128)S(1)} %get-tuple-element.40), channel_id=1, source_target_pairs={{0,1},{1,0},{2,3},{3,2},{4,5},{5,4},{6,7},{7,6},{8,9},{9,8},{10,11... | collective-permute-start | bytes 786440 | tf_op jit(solution)/shard_map/ppermute | solution.py:490
  24.7 0.7 %collective-permute-start.5 = (f32[8,64,128]{2,1,0:T(8,128)S(1)}, f32[8,64,128]{2,1,0:T(8,128)S(1)}, u32[]{:S(2)}, u32[]{:S(2)}) collective-permute-start(f32[8,64,128]{2,1,0:T(8,128)S(1)} %get-tuple-element.41), channel_id=1, source_target_pairs={{1,2},{2,1},{5,6},{6,5},{9,10},{10,9},{13,14},{14,13},{17,18},{18,... | collective-permute-start | bytes 786440 | tf_op jit(solution)/shard_map/ppermute | solution.py:490
  25.4 0.1 collective-permute-start.6
  25.5 1.2 %collective-permute-done.6.other_ref = f32[2,2,8,128]{3,2,1,0:T(8,128)S(1)} collective-permute-done((f32[2,2,8,128]{3,2,1,0:T(8,128)S(1)}, f32[2,2,8,128]{3,2,1,0:T(8,128)S(1)}, u32[]{:S(2)}, u32[]{:S(2)}) %collective-permute-start.6) | collective-permute-done | bytes 16416 | tf_op jit(solution)/shard_map/ppermute | solution.py:554
  26.7 1.6 %collective-permute-start.7 = (f32[2,2,8,128]{3,2,1,0:T(8,128)S(1)}, f32[2,2,8,128]{3,2,1,0:T(8,128)S(1)}, u32[]{:S(2)}, u32[]{:S(2)}) collective-permute-start(f32[2,2,8,128]{3,2,1,0:T(8,128)S(1)} %get-tuple-element.44.mine_ref), channel_id=1, source_target_pairs={{0,8},{4,12},{8,0},{12,4},{1,9},{5,13},{9,1},{13,5},{2,10},{6,14},... | collective-permute-start | bytes 49160 | tf_op jit(solution)/shard_map/ppermute | solution.py:554
  28.2 2.2 %collective-permute-done.7.other_ref = f32[2,2,8,128]{3,2,1,0:T(8,128)S(1)} collective-permute-done((f32[2,2,8,128]{3,2,1,0:T(8,128)S(1)}, f32[2,2,8,128]{3,2,1,0:T(8,128)S(1)}, u32[]{:S(2)}, u32[]{:S(2)}) %collective-permute-start.7) | collective-permute-done | bytes 16416 | tf_op jit(solution)/shard_map/ppermute | solution.py:554
  30.5 0.0 collective-permute-done.8.qa_ref
  30.5 0.0 collective-permute-done.9.qb_ref
  30.5 2.6 %collective-permute-start.10 = (f32[2,2,8,128]{3,2,1,0:T(8,128)S(1)}, f32[2,2,8,128]{3,2,1,0:T(8,128)S(1)}, u32[]{:S(2)}, u32[]{:S(2)}) collective-permute-start(f32[2,2,8,128]{3,2,1,0:T(8,128)S(1)} %shard_map.101.own_ref), channel_id=1, source_target_pairs={{0,1},{1,0},{2,3},{3,2},{4,5},{5,4},{6,7},{7,6},{8,9},{9,8},{10,11... | collective-permute-start | bytes 49160 | tf_op jit(solution)/shard_map/ppermute | solution.py:490
  33.1 0.7 %collective-permute-start.11 = (f32[2,2,8,128]{3,2,1,0:T(8,128)S(1)}, f32[2,2,8,128]{3,2,1,0:T(8,128)S(1)}, u32[]{:S(2)}, u32[]{:S(2)}) collective-permute-start(f32[2,2,8,128]{3,2,1,0:T(8,128)S(1)} %shard_map.101.own_ref), channel_id=1, source_target_pairs={{1,2},{2,1},{5,6},{6,5},{9,10},{10,9},{13,14},{14,13},{17,18},{18,... | collective-permute-start | bytes 49160 | tf_op jit(solution)/shard_map/ppermute | solution.py:490
  33.7 2.7 %shard_map.102 = (f32[64,32,128]{2,1,0:T(8,128)}, f32[64,32,128]{2,1,0:T(8,128)}, f32[1088,128]{1,0:T(8,128)S(1)}, f32[1088,128]{1,0:T(8,128)S(1)}) custom-call(f32[16,64,128]{2,1,0:T(8,128)S(1)} %get-tuple-element.51.p_in, f32[16,64,128]{2,1,0:T(8,128)S(1)} %get-tuple-element.52.q_in, f32[16,64,128]{2,1,0:T(8,128)S(1)} %get-tuple-element.53.p_out, ...), custom_call_target="tpu_custom_call" | custom-call | flops 6000000 | bytes 18000000 | tf_op jit(solution)/shard_map/pallas_call | solution.py:469
  36.5 0.0 collective-permute-done.4.pa_ref
  36.5 0.0 collective-permute-done.5.pb_ref
  36.5 0.0 collective-permute-done.10.wa_ref
  36.5 0.0 collective-permute-done.11.wb_ref
  36.5 2.6 %shard_map.103 = (f32[64,32,128]{2,1,0:T(8,128)}, f32[64,32,128]{2,1,0:T(8,128)}) custom-call(s32[2]{0:T(128)S(1)} %pad_add_fusion.odd_ref, f32[8,64,128]{2,1,0:T(8,128)S(1)} %collective-permute-done.4.pa_ref, f32[8,64,128]{2,1,0:T(8,128)S(1)} %collective-permute-done.5.pb_ref, ...), custom_call_target="tpu_custom_call", output_to_operand_aliasing={{0}: (14, {}), {1}: (15, {})} | custom-call | flops 2000000 | bytes 6000000 | tf_op jit(solution)/shard_map/pallas_call | solution.py:469
  (3 shorter events, 0.0 us)
Async XLA Ops:
  0.6 11.5 %copy-start = (f32[64,32,128]{2,1,0:T(8,128)S(1)}, f32[64,32,128]{2,1,0:T(8,128)}, u32[]{:S(2)}) copy-start(f32[64,32,128]{2,1,0:T(8,128)} %field_ref.3) | copy-start | bytes 3145732
  0.6 11.5 %copy-start.1 = (f32[64,32,128]{2,1,0:T(8,128)S(1)}, f32[64,32,128]{2,1,0:T(8,128)}, u32[]{:S(2)}) copy-start(f32[64,32,128]{2,1,0:T(8,128)} %field_ref.2) | copy-start | bytes 3145732
  0.7 11.5 %copy-start.2 = (f32[4,128]{1,0:T(4,128)S(1)}, f32[4,128]{1,0:T(4,128)}, u32[]{:S(2)}) copy-start(f32[4,128]{1,0:T(4,128)} %row_taps_ref.9) | copy-start | bytes 6148
  0.7 11.5 %copy-start.3 = (f32[4,128]{1,0:T(4,128)S(1)}, f32[4,128]{1,0:T(4,128)}, u32[]{:S(2)}) copy-start(f32[4,128]{1,0:T(4,128)} %taps_ref.9) | copy-start | bytes 6148
  0.7 11.5 %copy-start.4 = (f32[64,32]{0,1:T(8,128)S(1)}, f32[64,32]{0,1:T(8,128)}, u32[]{:S(2)}) copy-start(f32[64,32]{0,1:T(8,128)} %param.15) | copy-start | bytes 24580
  0.7 11.5 %copy-start.5 = (s32[128]{0:T(128)S(1)}, s32[128]{0:T(128)}, u32[]{:S(2)}) copy-start(s32[128]{0:T(128)} %param.13) | copy-start | bytes 1540
  0.7 11.5 %copy-start.6 = (s32[128]{0:T(128)S(1)}, s32[128]{0:T(128)}, u32[]{:S(2)}) copy-start(s32[128]{0:T(128)} %param.11) | copy-start | bytes 1540
  0.7 11.5 %copy-start.7 = (f32[128]{0:T(128)S(1)}, f32[128]{0:T(128)}, u32[]{:S(2)}) copy-start(f32[128]{0:T(128)} %param.14) | copy-start | bytes 1540
  2.1 12.3 %collective-permute-start.2 = (f32[64,8,128]{2,1,0:T(8,128)S(1)}, f32[64,8,128]{2,1,0:T(8,128)S(1)}, u32[]{:S(2)}, u32[]{:S(2)}) collective-permute-start(f32[64,8,128]{2,1,0:T(8,128)S(1)} %get-tuple-element.34), channel_id=1, source_target_pairs={{0,1},{1,0},{2,3},{3,2},{4,5},{5,4},{6,7},{7,6},{8,9},{9,8},{10,11... | collective-permute-start | bytes 786440 | tf_op jit(solution)/shard_map/ppermute | solution.py:490
  5.2 9.2 %collective-permute-start.3 = (f32[64,8,128]{2,1,0:T(8,128)S(1)}, f32[64,8,128]{2,1,0:T(8,128)S(1)}, u32[]{:S(2)}, u32[]{:S(2)}) collective-permute-start(f32[64,8,128]{2,1,0:T(8,128)S(1)} %get-tuple-element.35), channel_id=1, source_target_pairs={{1,2},{2,1},{5,6},{6,5},{9,10},{10,9},{13,14},{14,13},{17,18},{18,... | collective-permute-start | bytes 786440 | tf_op jit(solution)/shard_map/ppermute | solution.py:490
  7.1 12.5 %collective-permute-start = (f32[64,8,128]{2,1,0:T(8,128)S(1)}, f32[64,8,128]{2,1,0:T(8,128)S(1)}, u32[]{:S(2)}, u32[]{:S(2)}) collective-permute-start(f32[64,8,128]{2,1,0:T(8,128)S(1)} %get-tuple-element.31), channel_id=1, source_target_pairs={{0,1},{1,0},{2,3},{3,2},{4,5},{5,4},{6,7},{7,6},{8,9},{9,8},{10,11... | collective-permute-start | bytes 786440 | tf_op jit(solution)/shard_map/ppermute | solution.py:490
  11.5 8.1 %collective-permute-start.1 = (f32[64,8,128]{2,1,0:T(8,128)S(1)}, f32[64,8,128]{2,1,0:T(8,128)S(1)}, u32[]{:S(2)}, u32[]{:S(2)}) collective-permute-start(f32[64,8,128]{2,1,0:T(8,128)S(1)} %get-tuple-element.32), channel_id=1, source_target_pairs={{1,2},{2,1},{5,6},{6,5},{9,10},{10,9},{13,14},{14,13},{17,18},{18,... | collective-permute-start | bytes 786440 | tf_op jit(solution)/shard_map/ppermute | solution.py:490
  16.0 14.5 %collective-permute-start.8 = (f32[8,64,128]{2,1,0:T(8,128)S(1)}, f32[8,64,128]{2,1,0:T(8,128)S(1)}, u32[]{:S(2)}, u32[]{:S(2)}) collective-permute-start(f32[8,64,128]{2,1,0:T(8,128)S(1)} %get-tuple-element.46), channel_id=1, source_target_pairs={{0,1},{1,0},{2,3},{3,2},{4,5},{5,4},{6,7},{7,6},{8,9},{9,8},{10,11... | collective-permute-start | bytes 786440 | tf_op jit(solution)/shard_map/ppermute | solution.py:490
  18.9 11.6 %collective-permute-start.9 = (f32[8,64,128]{2,1,0:T(8,128)S(1)}, f32[8,64,128]{2,1,0:T(8,128)S(1)}, u32[]{:S(2)}, u32[]{:S(2)}) collective-permute-start(f32[8,64,128]{2,1,0:T(8,128)S(1)} %get-tuple-element.47), channel_id=1, source_target_pairs={{1,2},{2,1},{5,6},{6,5},{9,10},{10,9},{13,14},{14,13},{17,18},{18,... | collective-permute-start | bytes 786440 | tf_op jit(solution)/shard_map/ppermute | solution.py:490
  21.2 15.3 %collective-permute-start.4 = (f32[8,64,128]{2,1,0:T(8,128)S(1)}, f32[8,64,128]{2,1,0:T(8,128)S(1)}, u32[]{:S(2)}, u32[]{:S(2)}) collective-permute-start(f32[8,64,128]{2,1,0:T(8,128)S(1)} %get-tuple-element.40), channel_id=1, source_target_pairs={{0,1},{1,0},{2,3},{3,2},{4,5},{5,4},{6,7},{7,6},{8,9},{9,8},{10,11... | collective-permute-start | bytes 786440 | tf_op jit(solution)/shard_map/ppermute | solution.py:490
  24.7 11.8 %collective-permute-start.5 = (f32[8,64,128]{2,1,0:T(8,128)S(1)}, f32[8,64,128]{2,1,0:T(8,128)S(1)}, u32[]{:S(2)}, u32[]{:S(2)}) collective-permute-start(f32[8,64,128]{2,1,0:T(8,128)S(1)} %get-tuple-element.41), channel_id=1, source_target_pairs={{1,2},{2,1},{5,6},{6,5},{9,10},{10,9},{13,14},{14,13},{17,18},{18,... | collective-permute-start | bytes 786440 | tf_op jit(solution)/shard_map/ppermute | solution.py:490
  25.4 1.2 %collective-permute-start.6 = (f32[2,2,8,128]{3,2,1,0:T(8,128)S(1)}, f32[2,2,8,128]{3,2,1,0:T(8,128)S(1)}, u32[]{:S(2)}, u32[]{:S(2)}) collective-permute-start(f32[2,2,8,128]{3,2,1,0:T(8,128)S(1)} %get-tuple-element.43.mine_ref), channel_id=1, source_target_pairs={{0,4},{4,0},{8,12},{12,8},{1,5},{5,1},{9,13},{13,9},{2,6},{6,2},{1... | collective-permute-start | bytes 49160 | tf_op jit(solution)/shard_map/ppermute | solution.py:554
  26.7 3.8 %collective-permute-start.7 = (f32[2,2,8,128]{3,2,1,0:T(8,128)S(1)}, f32[2,2,8,128]{3,2,1,0:T(8,128)S(1)}, u32[]{:S(2)}, u32[]{:S(2)}) collective-permute-start(f32[2,2,8,128]{3,2,1,0:T(8,128)S(1)} %get-tuple-element.44.mine_ref), channel_id=1, source_target_pairs={{0,8},{4,12},{8,0},{12,4},{1,9},{5,13},{9,1},{13,5},{2,10},{6,14},... | collective-permute-start | bytes 49160 | tf_op jit(solution)/shard_map/ppermute | solution.py:554
  30.5 6.0 %collective-permute-start.10 = (f32[2,2,8,128]{3,2,1,0:T(8,128)S(1)}, f32[2,2,8,128]{3,2,1,0:T(8,128)S(1)}, u32[]{:S(2)}, u32[]{:S(2)}) collective-permute-start(f32[2,2,8,128]{3,2,1,0:T(8,128)S(1)} %shard_map.101.own_ref), channel_id=1, source_target_pairs={{0,1},{1,0},{2,3},{3,2},{4,5},{5,4},{6,7},{7,6},{8,9},{9,8},{10,11... | collective-permute-start | bytes 49160 | tf_op jit(solution)/shard_map/ppermute | solution.py:490
  33.1 3.4 %collective-permute-start.11 = (f32[2,2,8,128]{3,2,1,0:T(8,128)S(1)}, f32[2,2,8,128]{3,2,1,0:T(8,128)S(1)}, u32[]{:S(2)}, u32[]{:S(2)}) collective-permute-start(f32[2,2,8,128]{3,2,1,0:T(8,128)S(1)} %shard_map.101.own_ref), channel_id=1, source_target_pairs={{1,2},{2,1},{5,6},{6,5},{9,10},{10,9},{13,14},{14,13},{17,18},{18,... | collective-permute-start | bytes 49160 | tf_op jit(solution)/shard_map/ppermute | solution.py:490

commit v4 on v3

--- a/solution.py
+++ b/solution.py
@@ -174,7 +174,7 @@
 def row_halo(odd, a_ref, b_ref, halo_ref, bits, taps):
     rows = a_ref.shape[0]
     for side in range(2):
-        use_a = odd == (1 - side)
+        use_a = odd if side == 0 else ~odd
         get = lambda y: jnp.where(use_a, a_ref[y], b_ref[y]) if 0 <= y < rows else None
         for y, v in resample(get, bits, taps, range(rows), False):
             halo_ref[pl.ds(y * pitch_of(2 * HALO) + side * HALO, SUB), :] = v
@@ -210,11 +210,25 @@
     return [*range(HALO), *range(columns - HALO, columns)]
 
 
+def split_edges(odd, refs, a_ref, b_ref):
+    rows = refs[0].shape[1]
+
+    def body(group):
+        at = pl.ds(pl.multiple_of(group * SUB, SUB), SUB)
+        for n, ref in enumerate(refs):
+            for i in range(HALO):
+                left, right = ref[i, at, :], ref[HALO + i, at, :]
+                a_ref[n * HALO + i, at, :] = jnp.where(odd, left, right)
+                b_ref[n * HALO + i, at, :] = jnp.where(odd, right, left)
+
+    loop(rows // SUB, body)
+
+
 def density_kernel(
     all_planes, odd_ref, rd_ref, a_ref, b_ref, inner_ref, row_taps_ref, row_shift_ref, taps_ref, shift_ref, scale_ref,
-    q_ref, n_ref, qa_ref, qb_ref, dense_ref, halo_ref,
+    q_ref, n_ref, dense_ref, halo_ref,
 ):
-    odd = odd_ref[0]
+    odd = odd_ref[0] == 1
     rows, planes = q_ref.shape[1:]
     columns = rd_ref.shape[0] // rows - 1
     row_halo(odd, a_ref, b_ref, halo_ref, bits_of(row_shift_ref[...]), rows_of(row_taps_ref[...]))
@@ -237,15 +251,13 @@
         pack_totals(totals, dense_ref, group, columns, outside)
 
     loop(rows // SUB, body)
-    for ref, at in ((qa_ref, jnp.where(odd == 1, 0, HALO)), (qb_ref, jnp.where(odd == 1, HALO, 0))):
-        ref[...] = q_ref[pl.ds(at, HALO)]
 
 
 def emission_kernel(
     all_planes, odd_ref, re_ref, a_ref, b_ref, q_ref, n_ref, inner_ref, optical_ref, row_taps_ref, row_shift_ref, taps_ref, shift_ref, scale_ref,
     p_ref, pa_ref, pb_ref, dense_ref, halo_ref,
 ):
-    odd = odd_ref[0]
+    odd = odd_ref[0] == 1
     rows, planes = p_ref.shape[1:]
     columns = re_ref.shape[0] // rows - 1
     row_halo(odd, a_ref, b_ref, halo_ref, bits_of(row_shift_ref[...]), rows_of(row_taps_ref[...]))
@@ -270,32 +282,24 @@
         pack_totals(sums[:, planes:], dense_ref.at[1], group, columns, outside)
 
     loop(rows // SUB, body)
-    for ref, at in ((pa_ref, jnp.where(odd == 1, 0, HALO)), (pb_ref, jnp.where(odd == 1, HALO, 0))):
-        ref[...] = p_ref[pl.ds(at, HALO)]
-
-
-def merge(later, mine, other, front, back):
-    (depth, light), (depth_2, light_2) = mine, other
-    dim = jnp.exp(-jnp.where(later, depth_2, depth))
-    joined = (depth + depth_2, jnp.where(later, light_2 + dim * light, light + dim * light_2))
-    return joined, jnp.where(later, front + depth_2, front), jnp.where(later, back * dim, back + dim * light_2)
-
-
-def merge_kernel(step, last, where_ref, weight_ref, mine_ref, other_ref, *refs):
-    later = (where_ref[1] & (1 << step)) != 0
-    outs = refs if step == 0 else refs[1:]
+    split_edges(odd, (p_ref, q_ref), pa_ref, pb_ref)
+
+
+def join_kernel(count, where_ref, weight_ref, *refs):
+    sums, out_ref = refs[:count], refs[count]
+    mine = where_ref[1]
     for c in range(weight_ref.shape[0]):
-        zero = jnp.zeros_like(weight_ref[c])
-        front, back = (zero, zero) if step == 0 else (refs[0][0, c], refs[0][1, c])
-        joined, front, back = merge(
-            later, (mine_ref[0, c], mine_ref[1, c]), (other_ref[0, c], other_ref[1, c]), front, back
-        )
-        if last:
-            outs[0][0, c] = weight_ref[c] * jnp.exp(-front)
-            outs[0][1, c] = weight_ref[c] * back
-        else:
-            outs[0][0, c], outs[0][1, c] = joined
-            outs[1][0, c], outs[1][1, c] = front, back
+        front = jnp.zeros_like(weight_ref[c])
+        for ahead in range(1, count):
+            front += jnp.where(mine + ahead >= count, sums[ahead][0, c], 0.0)
+        running = front + sums[0][0, c]
+        back = jnp.zeros_like(front)
+        for ahead in range(1, count):
+            there = mine + ahead < count
+            back += jnp.where(there, jnp.exp(-running) * sums[ahead][1, c], 0.0)
+            running += jnp.where(there, sums[ahead][0, c], 0.0)
+        out_ref[0, c] = weight_ref[c] * jnp.exp(-front)
+        out_ref[1, c] = weight_ref[c] * back
 
 
 def lay(split_ref, row, dense, base, first, count):
@@ -392,11 +396,11 @@
 
 
 def outer_kernel(
-    all_planes, odd_ref, pa_ref, pb_ref, qa_ref, qb_ref, wa_ref, wb_ref, td_ref, te_ref,
+    all_planes, odd_ref, pa_ref, pb_ref, wb_ref, wa_ref, td_ref, te_ref,
     row_taps_ref, row_shift_ref, taps_ref, shift_ref, scale_ref, gd_in, ge_in,
     gd_ref, ge_ref, cd_ref, ce_ref, held_ref, split_ref, weight_ref, sems,
 ):
-    odd = odd_ref[0]
+    odd = odd_ref[0] == 1
     rows, columns, planes = gd_ref.shape
     per = 128 // columns
     groups = rows // SUB
@@ -404,7 +408,7 @@
     bits = bits_of(shift_ref[...])
     taps = rows_of(taps_ref[...])
     scale = jnp.broadcast_to(scale_ref[...] / all_planes, (SUB, planes))
-    use_a = (odd == 1, odd != 1)
+    use_a = (odd, ~odd)
 
     for side in range(2):
         for group in range(groups):
@@ -438,7 +442,7 @@
                 i = x - start
                 if not 0 <= i < HALO:
                     return None
-                v = jnp.where(use_a[side], qa_ref[i, y0 : y0 + SUB, :], qb_ref[i, y0 : y0 + SUB, :])
+                v = jnp.where(use_a[side], pa_ref[HALO + i, y0 : y0 + SUB, :], pb_ref[HALO + i, y0 : y0 + SUB, :])
                 return front_at(i) * v
 
             for get, ref, out in ((get_d, td_ref, cd_ref), (get_e, te_ref, ce_ref)):
@@ -527,39 +531,28 @@
         micros=3.0,
     )
     outer = (rows * pitch_of(2 * HALO), planes)
-    q_out, n_out, qa, qb, slab_optical = call(
+    q_out, n_out, slab_optical = call(
         functools.partial(density_kernel, all_planes),
-        [outside, outside, side, side, dense],
-        [place],
-        [rd, da, db, inner_sums, row_taps, row_shift, taps, shift, scale],
+        [outside, outside, dense],
+        [],
+        [where, rd, da, db, inner_sums, row_taps, row_shift, taps, shift, scale],
         [pltpu.VMEM(outer, F32)],
     )
-    qa, qb = swap(qa, "screen", 0), swap(qb, "screen", 1)
     p_out, pa, pb, state = call(
         functools.partial(emission_kernel, all_planes),
-        [outside, side, side, (2,) + dense],
-        [place],
-        [re, ea, eb, q_out, n_out, inner_sums, slab_optical, row_taps, row_shift, taps, shift, scale],
+        [outside, outside, outside, (2,) + dense],
+        [],
+        [where, re, ea, eb, q_out, n_out, inner_sums, slab_optical, row_taps, row_shift, taps, shift, scale],
         [pltpu.VMEM(outer, F32)],
         micros=6.0,
     )
-    rounds = slabs.bit_length() - 1
-    assert slabs == 1 << rounds and rounds
-    sums = (2,) + dense
-    around = []
-    for step in range(rounds):
-        last = step == rounds - 1
-        if last:
-            pa, pb = swap(pa, "screen", 0), swap(pb, "screen", 1)
-        other = lax.ppermute(state, "depth", [(i, i ^ (1 << step)) for i in range(slabs)])
-        state, *around = call(
-            functools.partial(merge_kernel, step, last),
-            [sums] * (1 if last else 2),
-            [],
-            [where, weight, state, other] + around,
-            micros=0.1,
-        )
-    own, qa, qb = lax.optimization_barrier((state, qa, qb))
+    pa, pb = swap(pa, "screen", 0), swap(pb, "screen", 1)
+    ahead = [state] + [
+        lax.ppermute(state, "depth", [((i + e) % slabs, i) for i in range(slabs)]) for e in range(1, slabs)
+    ]
+    (own,) = call(
+        functools.partial(join_kernel, slabs), [(2,) + dense], [], [where, weight] + ahead, micros=0.1
+    )
     wa, wb = swap(own, "screen", 0), swap(own, "screen", 1)
     inner = (rows * pitch_of(columns - 2 * HALO), planes)
     halves_of = rows * columns
@@ -583,8 +576,8 @@
     gd, ge = call(
         functools.partial(outer_kernel, all_planes),
         [density.shape, density.shape],
-        [place],
-        [pa, pb, qa, qb, wa, wb, td, te, row_taps, row_shift, taps, shift, scale],
+        [],
+        [where, pa, pb, wb, wa, td, te, row_taps, row_shift, taps, shift, scale],
         [
             pltpu.VMEM(outer, F32),
             pltpu.VMEM(outer, F32),
@@ -595,7 +588,7 @@
         ],
         hbm_in=[gd, ge],
         hbm_out=2,
-        aliases={14: 0, 15: 1},
+        aliases={12: 0, 13: 1},
     )
     return gd, ge
 

time: 39.4 us -> 37.7 us (0.957)
  the two profiles are of different devices: /device:TPU:0 before, /device:TPU:14 now
where the time goes in v4:
time: 37.7 us; the launch traced here: 37.5 us
  starting transfers between devices  14.4 us (38%)
  Pallas kernels  11.5 us (31%)
  waiting for transfers between devices  10.5 us (28%)
  between operations  0.88 us (2%)
    ppermute x8, starting transfers between devices, swap(): return lax.ppermute(value, axis, pairs)  13.6 us
    pallas_call x8, Pallas kernels, call(): pl.pallas_call(kernel, out_shape=[jax.ShapeDtypeStruct(s, F32) if i < hbm...  11.5 us
    ppermute x8, waiting for transfers between devices, swap(): return lax.ppermute(value, axis, pairs)  7.3 us
    ppermute x3, waiting for transfers between devices, on_device(): lax.ppermute(state, 'depth', [((i + e) % slabs, i) for i in range(slabs)])  3.18 us
    ppermute x3, starting transfers between devices, on_device(): lax.ppermute(state, 'depth', [((i + e) % slabs, i) for i in range(slabs)])  0.82 us
  transfers between devices with their start and end apart: 11, of which 7 were waited for; matrix products, arithmetic and copies ran while one was open for 0% of the time, Pallas kernels for 19%

profile of v4, /device:TPU:14, one launch (start us, length us, event | category | flops | bytes accessed | tf_op | source)
XLA Modules:
  0.0 37.5 jit_solution(3152195575786698494)
XLA Ops:
  0.6 0.0 copy-start
  0.6 0.0 copy-start.1
  0.7 0.0 copy-start.2
  0.7 0.0 copy-start.3
  0.7 0.0 copy-start.4
  0.7 0.0 copy-start.5
  0.7 0.0 copy-start.6
  0.7 0.0 copy-start.7
  0.7 0.1 pad_add_fusion
  0.8 0.1 broadcast_in_dim.15.where_ref.odd_ref
  0.9 1.3 %shard_map.97 = (f32[64,8,128]{2,1,0:T(8,128)S(1)}, f32[64,8,128]{2,1,0:T(8,128)S(1)}) custom-call(s32[2,8,128]{2,1,0:T(8,128)S(1)} %broadcast_in_dim.15.where_ref.odd_ref, f32[64,32,128]{2,1,0:T(8,128)} %field_ref.3), custom_call_target="tpu_custom_call" | custom-call | flops 200000 | bytes 600000 | tf_op jit(solution)/shard_map/pallas_call | solution.py:473
  2.1 0.5 %collective-permute-start.2 = (f32[64,8,128]{2,1,0:T(8,128)S(1)}, f32[64,8,128]{2,1,0:T(8,128)S(1)}, u32[]{:S(2)}, u32[]{:S(2)}) collective-permute-start(f32[64,8,128]{2,1,0:T(8,128)S(1)} %get-tuple-element.27), channel_id=1, source_target_pairs={{0,1},{1,0},{2,3},{3,2},{4,5},{5,4},{6,7},{7,6},{8,9},{9,8},{10,11... | collective-permute-start | bytes 786440 | tf_op jit(solution)/shard_map/ppermute | solution.py:494
  2.7 4.6 %collective-permute-start.3 = (f32[64,8,128]{2,1,0:T(8,128)S(1)}, f32[64,8,128]{2,1,0:T(8,128)S(1)}, u32[]{:S(2)}, u32[]{:S(2)}) collective-permute-start(f32[64,8,128]{2,1,0:T(8,128)S(1)} %get-tuple-element.28), channel_id=1, source_target_pairs={{1,2},{2,1},{5,6},{6,5},{9,10},{10,9},{13,14},{14,13},{17,18},{18,... | collective-permute-start | bytes 786440 | tf_op jit(solution)/shard_map/ppermute | solution.py:494
  7.3 1.1 %shard_map.96 = (f32[64,8,128]{2,1,0:T(8,128)S(1)}, f32[64,8,128]{2,1,0:T(8,128)S(1)}) custom-call(s32[2,8,128]{2,1,0:T(8,128)S(1)} %broadcast_in_dim.15.where_ref.odd_ref, f32[64,32,128]{2,1,0:T(8,128)} %field_ref.2), custom_call_target="tpu_custom_call" | custom-call | flops 200000 | bytes 600000 | tf_op jit(solution)/shard_map/pallas_call | solution.py:473
  8.4 0.1 collective-permute-start
  8.5 1.9 %collective-permute-start.1 = (f32[64,8,128]{2,1,0:T(8,128)S(1)}, f32[64,8,128]{2,1,0:T(8,128)S(1)}, u32[]{:S(2)}, u32[]{:S(2)}) collective-permute-start(f32[64,8,128]{2,1,0:T(8,128)S(1)} %get-tuple-element.25), channel_id=1, source_target_pairs={{1,2},{2,1},{5,6},{6,5},{9,10},{10,9},{13,14},{14,13},{17,18},{18,... | collective-permute-start | bytes 786440 | tf_op jit(solution)/shard_map/ppermute | solution.py:494
  10.4 0.0 copy-done
  10.4 0.0 copy-done.1
  10.4 0.0 copy-done.2
  10.5 0.0 copy-done.3
  10.5 0.0 copy-done.4
  10.5 0.0 copy-done.5
  10.5 0.0 copy-done.6
  10.5 0.0 copy-done.7
  10.5 2.1 %shard_map.95 = (f32[2112,128]{1,0:T(8,128)S(1)}, f32[2112,128]{1,0:T(8,128)S(1)}, f32[16,64,128]{2,1,0:T(8,128)S(1)}, f32[16,64,128]{2,1,0:T(8,128)S(1)}, f32[2...) custom-call(f32[64,32,128]{2,1,0:T(8,128)S(1)} %copy-done, f32[64,32,128]{2,1,0:T(8,128)S(1)} %copy-done.1, ...), custom_call_target="tpu_custom_call" | custom-call | flops 3000000 | bytes 9000000 | tf_op jit(solution)/shard_map/pallas_call | solution.py:473
  12.7 0.0 collective-permute-done.2.a_ref
  12.7 1.6 %collective-permute-done.3.b_ref = f32[64,8,128]{2,1,0:T(8,128)S(1)} collective-permute-done((f32[64,8,128]{2,1,0:T(8,128)S(1)}, f32[64,8,128]{2,1,0:T(8,128)S(1)}, u32[]{:S(2)}, u32[]{:S(2)}) %collective-permute-start.3) | collective-permute-done | bytes 262176 | tf_op jit(solution)/shard_map/ppermute | solution.py:494
  14.2 1.0 %shard_map.98 = (f32[16,64,128]{2,1,0:T(8,128)S(1)}, f32[16,64,128]{2,1,0:T(8,128)S(1)}, f32[2,8,128]{2,1,0:T(8,128)S(1)}) custom-call(s32[2,8,128]{2,1,0:T(8,128)S(1)} %broadcast_in_dim.15.where_ref.odd_ref, f32[2112,128]{1,0:T(8,128)S(1)} %get-tuple-element.26.rd_ref, f32[64,8,128]{2,1,0:T(8,128)S(1)} %collective-permute-done.2.a_ref, ...), custom_call_target="tpu_custom_call" | custom-call | flops 2000000 | bytes 6000000 | tf_op jit(solution)/shard_map/pallas_call | solution.py:473
  15.2 0.7 %collective-permute-done.a_ref = f32[64,8,128]{2,1,0:T(8,128)S(1)} collective-permute-done((f32[64,8,128]{2,1,0:T(8,128)S(1)}, f32[64,8,128]{2,1,0:T(8,128)S(1)}, u32[]{:S(2)}, u32[]{:S(2)}) %collective-permute-start) | collective-permute-done | bytes 262176 | tf_op jit(solution)/shard_map/ppermute | solution.py:494
  16.0 2.9 %collective-permute-done.1.b_ref = f32[64,8,128]{2,1,0:T(8,128)S(1)} collective-permute-done((f32[64,8,128]{2,1,0:T(8,128)S(1)}, f32[64,8,128]{2,1,0:T(8,128)S(1)}, u32[]{:S(2)}, u32[]{:S(2)}) %collective-permute-start.1) | collective-permute-done | bytes 262176 | tf_op jit(solution)/shard_map/ppermute | solution.py:494
  18.9 1.1 %shard_map.99 = (f32[16,64,128]{2,1,0:T(8,128)S(1)}, f32[16,64,128]{2,1,0:T(8,128)S(1)}, f32[16,64,128]{2,1,0:T(8,128)S(1)}, f32[2,2,8,128]{3,2,1,0:T(8,128)S(1)}) custom-call(s32[2,8,128]{2,1,0:T(8,128)S(1)} %broadcast_in_dim.15.where_ref.odd_ref, f32[2112,128]{1,0:T(8,128)S(1)} %get-tuple-element.23.re_ref, f32[64,8,128]{2,1,0:T(8,128)S(1)} %collective-permute-done.a_ref, ...), custom_call_target="tpu_custom_call" | custom-call | flops 6000000 | bytes 18000000 | tf_op jit(solution)/shard_map/pallas_call | solution.py:473
  20.0 0.1 collective-permute-start.4
  20.1 3.6 %collective-permute-start.5 = (f32[16,64,128]{2,1,0:T(8,128)S(1)}, f32[16,64,128]{2,1,0:T(8,128)S(1)}, u32[]{:S(2)}, u32[]{:S(2)}) collective-permute-start(f32[16,64,128]{2,1,0:T(8,128)S(1)} %get-tuple-element.34), channel_id=1, source_target_pairs={{1,2},{2,1},{5,6},{6,5},{9,10},{10,9},{13,14},{14,13},{17,18},{18,... | collective-permute-start | bytes 1572872 | tf_op jit(solution)/shard_map/ppermute | solution.py:494
  23.7 0.1 collective-permute-start.6
  23.8 0.6 %collective-permute-start.7 = (f32[2,2,8,128]{3,2,1,0:T(8,128)S(1)}, f32[2,2,8,128]{3,2,1,0:T(8,128)S(1)}, u32[]{:S(2)}, u32[]{:S(2)}) collective-permute-start(f32[2,2,8,128]{3,2,1,0:T(8,128)S(1)} %get-tuple-element.36.refs_0_), channel_id=1, source_target_pairs={{8,0},{12,4},{0,8},{4,12},{9,1},{13,5},{1,9},{5,13},{10,2},{14,6},... | collective-permute-start | bytes 49160 | tf_op jit(solution)/shard_map/ppermute | solution.py:551
  24.4 0.2 collective-permute-start.8
  24.6 0.7 %collective-permute-done.6.refs_1_ = f32[2,2,8,128]{3,2,1,0:T(8,128)S(1)} collective-permute-done((f32[2,2,8,128]{3,2,1,0:T(8,128)S(1)}, f32[2,2,8,128]{3,2,1,0:T(8,128)S(1)}, u32[]{:S(2)}, u32[]{:S(2)}) %collective-permute-start.6) | collective-permute-done | bytes 16416 | tf_op jit(solution)/shard_map/ppermute | solution.py:551
  25.2 2.5 %collective-permute-done.7.refs_2_ = f32[2,2,8,128]{3,2,1,0:T(8,128)S(1)} collective-permute-done((f32[2,2,8,128]{3,2,1,0:T(8,128)S(1)}, f32[2,2,8,128]{3,2,1,0:T(8,128)S(1)}, u32[]{:S(2)}, u32[]{:S(2)}) %collective-permute-start.7) | collective-permute-done | bytes 16416 | tf_op jit(solution)/shard_map/ppermute | solution.py:551
  27.8 0.0 collective-permute-done.8.refs_3_
  27.8 0.1 collective-permute-start.10
  27.9 2.7 %collective-permute-start.9 = (f32[2,2,8,128]{3,2,1,0:T(8,128)S(1)}, f32[2,2,8,128]{3,2,1,0:T(8,128)S(1)}, u32[]{:S(2)}, u32[]{:S(2)}) collective-permute-start(f32[2,2,8,128]{3,2,1,0:T(8,128)S(1)} %shard_map.100.own_ref), channel_id=1, source_target_pairs={{1,2},{2,1},{5,6},{6,5},{9,10},{10,9},{13,14},{14,13},{17,18},{18,... | collective-permute-start | bytes 49160 | tf_op jit(solution)/shard_map/ppermute | solution.py:494
  30.5 2.7 %shard_map.101 = (f32[64,32,128]{2,1,0:T(8,128)}, f32[64,32,128]{2,1,0:T(8,128)}, f32[1088,128]{1,0:T(8,128)S(1)}, f32[1088,128]{1,0:T(8,128)S(1)}) custom-call(f32[16,64,128]{2,1,0:T(8,128)S(1)} %get-tuple-element.37.p_in, f32[16,64,128]{2,1,0:T(8,128)S(1)} %get-tuple-element.38.q_in, f32[16,64,128]{2,1,0:T(8,128)S(1)} %get-tuple-element.39.p_out, ...), custom_call_target="tpu_custom_call" | custom-call | flops 6000000 | bytes 18000000 | tf_op jit(solution)/shard_map/pallas_call | solution.py:473
  33.3 0.1 collective-permute-done.10.wa_ref
  33.4 1.9 %collective-permute-done.9.wb_ref = f32[2,2,8,128]{3,2,1,0:T(8,128)S(1)} collective-permute-done((f32[2,2,8,128]{3,2,1,0:T(8,128)S(1)}, f32[2,2,8,128]{3,2,1,0:T(8,128)S(1)}, u32[]{:S(2)}, u32[]{:S(2)}) %collective-permute-start.9) | collective-permute-done | bytes 16416 | tf_op jit(solution)/shard_map/ppermute | solution.py:494
  35.3 0.0 collective-permute-done.4.pa_ref
  35.3 0.0 collective-permute-done.5.pb_ref
  35.3 2.1 %shard_map.102 = (f32[64,32,128]{2,1,0:T(8,128)}, f32[64,32,128]{2,1,0:T(8,128)}) custom-call(s32[2,8,128]{2,1,0:T(8,128)S(1)} %broadcast_in_dim.15.where_ref.odd_ref, f32[16,64,128]{2,1,0:T(8,128)S(1)} %collective-permute-done.4.pa_ref, f32[16,64,128]{2,1,0:T(8,128)S(1)} %collective-permute-done.5.pb_ref, ...), custom_call_target="tpu_custom_call", output_to_operand_aliasing={{0}: (12, {}), {1}: (13, {})} | custom-call | flops 2000000 | bytes 6000000 | tf_op jit(solution)/shard_map/pallas_call | solution.py:473
  (1 shorter events, 0.0 us)
Async XLA Ops:
  0.6 9.8 %copy-start = (f32[64,32,128]{2,1,0:T(8,128)S(1)}, f32[64,32,128]{2,1,0:T(8,128)}, u32[]{:S(2)}) copy-start(f32[64,32,128]{2,1,0:T(8,128)} %field_ref.3) | copy-start | bytes 3145732
  0.6 9.8 %copy-start.1 = (f32[64,32,128]{2,1,0:T(8,128)S(1)}, f32[64,32,128]{2,1,0:T(8,128)}, u32[]{:S(2)}) copy-start(f32[64,32,128]{2,1,0:T(8,128)} %field_ref.2) | copy-start | bytes 3145732
  0.7 9.8 %copy-start.2 = (f32[4,128]{1,0:T(4,128)S(1)}, f32[4,128]{1,0:T(4,128)}, u32[]{:S(2)}) copy-start(f32[4,128]{1,0:T(4,128)} %row_taps_ref.9) | copy-start | bytes 6148
  0.7 9.8 %copy-start.3 = (f32[4,128]{1,0:T(4,128)S(1)}, f32[4,128]{1,0:T(4,128)}, u32[]{:S(2)}) copy-start(f32[4,128]{1,0:T(4,128)} %taps_ref.9) | copy-start | bytes 6148
  0.7 9.8 %copy-start.4 = (f32[64,32]{0,1:T(8,128)S(1)}, f32[64,32]{0,1:T(8,128)}, u32[]{:S(2)}) copy-start(f32[64,32]{0,1:T(8,128)} %param.15) | copy-start | bytes 24580
  0.7 9.8 %copy-start.5 = (s32[128]{0:T(128)S(1)}, s32[128]{0:T(128)}, u32[]{:S(2)}) copy-start(s32[128]{0:T(128)} %param.13) | copy-start | bytes 1540
  0.7 9.8 %copy-start.6 = (s32[128]{0:T(128)S(1)}, s32[128]{0:T(128)}, u32[]{:S(2)}) copy-start(s32[128]{0:T(128)} %param.11) | copy-start | bytes 1540
  0.7 9.8 %copy-start.7 = (f32[128]{0:T(128)S(1)}, f32[128]{0:T(128)}, u32[]{:S(2)}) copy-start(f32[128]{0:T(128)} %param.14) | copy-start | bytes 1540
  2.1 10.5 %collective-permute-start.2 = (f32[64,8,128]{2,1,0:T(8,128)S(1)}, f32[64,8,128]{2,1,0:T(8,128)S(1)}, u32[]{:S(2)}, u32[]{:S(2)}) collective-permute-start(f32[64,8,128]{2,1,0:T(8,128)S(1)} %get-tuple-element.27), channel_id=1, source_target_pairs={{0,1},{1,0},{2,3},{3,2},{4,5},{5,4},{6,7},{7,6},{8,9},{9,8},{10,11... | collective-permute-start | bytes 786440 | tf_op jit(solution)/shard_map/ppermute | solution.py:494
  2.7 11.6 %collective-permute-start.3 = (f32[64,8,128]{2,1,0:T(8,128)S(1)}, f32[64,8,128]{2,1,0:T(8,128)S(1)}, u32[]{:S(2)}, u32[]{:S(2)}) collective-permute-start(f32[64,8,128]{2,1,0:T(8,128)S(1)} %get-tuple-element.28), channel_id=1, source_target_pairs={{1,2},{2,1},{5,6},{6,5},{9,10},{10,9},{13,14},{14,13},{17,18},{18,... | collective-permute-start | bytes 786440 | tf_op jit(solution)/shard_map/ppermute | solution.py:494
  8.4 7.6 %collective-permute-start = (f32[64,8,128]{2,1,0:T(8,128)S(1)}, f32[64,8,128]{2,1,0:T(8,128)S(1)}, u32[]{:S(2)}, u32[]{:S(2)}) collective-permute-start(f32[64,8,128]{2,1,0:T(8,128)S(1)} %get-tuple-element.24), channel_id=1, source_target_pairs={{0,1},{1,0},{2,3},{3,2},{4,5},{5,4},{6,7},{7,6},{8,9},{9,8},{10,11... | collective-permute-start | bytes 786440 | tf_op jit(solution)/shard_map/ppermute | solution.py:494
  8.5 10.4 %collective-permute-start.1 = (f32[64,8,128]{2,1,0:T(8,128)S(1)}, f32[64,8,128]{2,1,0:T(8,128)S(1)}, u32[]{:S(2)}, u32[]{:S(2)}) collective-permute-start(f32[64,8,128]{2,1,0:T(8,128)S(1)} %get-tuple-element.25), channel_id=1, source_target_pairs={{1,2},{2,1},{5,6},{6,5},{9,10},{10,9},{13,14},{14,13},{17,18},{18,... | collective-permute-start | bytes 786440 | tf_op jit(solution)/shard_map/ppermute | solution.py:494
  20.0 15.3 %collective-permute-start.4 = (f32[16,64,128]{2,1,0:T(8,128)S(1)}, f32[16,64,128]{2,1,0:T(8,128)S(1)}, u32[]{:S(2)}, u32[]{:S(2)}) collective-permute-start(f32[16,64,128]{2,1,0:T(8,128)S(1)} %get-tuple-element.33), channel_id=1, source_target_pairs={{0,1},{1,0},{2,3},{3,2},{4,5},{5,4},{6,7},{7,6},{8,9},{9,8},{10,11... | collective-permute-start | bytes 1572872 | tf_op jit(solution)/shard_map/ppermute | solution.py:494
  20.1 15.2 %collective-permute-start.5 = (f32[16,64,128]{2,1,0:T(8,128)S(1)}, f32[16,64,128]{2,1,0:T(8,128)S(1)}, u32[]{:S(2)}, u32[]{:S(2)}) collective-permute-start(f32[16,64,128]{2,1,0:T(8,128)S(1)} %get-tuple-element.34), channel_id=1, source_target_pairs={{1,2},{2,1},{5,6},{6,5},{9,10},{10,9},{13,14},{14,13},{17,18},{18,... | collective-permute-start | bytes 1572872 | tf_op jit(solution)/shard_map/ppermute | solution.py:494
  23.7 1.5 %collective-permute-start.6 = (f32[2,2,8,128]{3,2,1,0:T(8,128)S(1)}, f32[2,2,8,128]{3,2,1,0:T(8,128)S(1)}, u32[]{:S(2)}, u32[]{:S(2)}) collective-permute-start(f32[2,2,8,128]{3,2,1,0:T(8,128)S(1)} %get-tuple-element.36.refs_0_), channel_id=1, source_target_pairs={{4,0},{8,4},{12,8},{0,12},{5,1},{9,5},{13,9},{1,13},{6,2},{10,6},{... | collective-permute-start | bytes 49160 | tf_op jit(solution)/shard_map/ppermute | solution.py:551
  23.8 3.9 %collective-permute-start.7 = (f32[2,2,8,128]{3,2,1,0:T(8,128)S(1)}, f32[2,2,8,128]{3,2,1,0:T(8,128)S(1)}, u32[]{:S(2)}, u32[]{:S(2)}) collective-permute-start(f32[2,2,8,128]{3,2,1,0:T(8,128)S(1)} %get-tuple-element.36.refs_0_), channel_id=1, source_target_pairs={{8,0},{12,4},{0,8},{4,12},{9,1},{13,5},{1,9},{5,13},{10,2},{14,6},... | collective-permute-start | bytes 49160 | tf_op jit(solution)/shard_map/ppermute | solution.py:551
  24.4 3.3 %collective-permute-start.8 = (f32[2,2,8,128]{3,2,1,0:T(8,128)S(1)}, f32[2,2,8,128]{3,2,1,0:T(8,128)S(1)}, u32[]{:S(2)}, u32[]{:S(2)}) collective-permute-start(f32[2,2,8,128]{3,2,1,0:T(8,128)S(1)} %get-tuple-element.36.refs_0_), channel_id=1, source_target_pairs={{12,0},{0,4},{4,8},{8,12},{13,1},{1,5},{5,9},{9,13},{14,2},{2,6},{... | collective-permute-start | bytes 49160 | tf_op jit(solution)/shard_map/ppermute | solution.py:551
  27.8 5.6 %collective-permute-start.10 = (f32[2,2,8,128]{3,2,1,0:T(8,128)S(1)}, f32[2,2,8,128]{3,2,1,0:T(8,128)S(1)}, u32[]{:S(2)}, u32[]{:S(2)}) collective-permute-start(f32[2,2,8,128]{3,2,1,0:T(8,128)S(1)} %shard_map.100.own_ref), channel_id=1, source_target_pairs={{0,1},{1,0},{2,3},{3,2},{4,5},{5,4},{6,7},{7,6},{8,9},{9,8},{10,11... | collective-permute-start | bytes 49160 | tf_op jit(solution)/shard_map/ppermute | solution.py:494
  27.9 7.5 %collective-permute-start.9 = (f32[2,2,8,128]{3,2,1,0:T(8,128)S(1)}, f32[2,2,8,128]{3,2,1,0:T(8,128)S(1)}, u32[]{:S(2)}, u32[]{:S(2)}) collective-permute-start(f32[2,2,8,128]{3,2,1,0:T(8,128)S(1)} %shard_map.100.own_ref), channel_id=1, source_target_pairs={{1,2},{2,1},{5,6},{6,5},{9,10},{10,9},{13,14},{14,13},{17,18},{18,... | collective-permute-start | bytes 49160 | tf_op jit(solution)/shard_map/ppermute | solution.py:494

commit v5 on v4

--- a/solution.py
+++ b/solution.py
@@ -14,7 +14,7 @@
 BF16 = jnp.bfloat16
 VMEM_LIMIT = 24 * 1024 * 1024
 EDGE_LIMIT = int(24 * 1024 * 1024)
-UNROLL = 4
+UNROLL = 8
 LARGEST = 64.0
 
 
@@ -225,7 +225,7 @@
 
 
 def density_kernel(
-    all_planes, odd_ref, rd_ref, a_ref, b_ref, inner_ref, row_taps_ref, row_shift_ref, taps_ref, shift_ref, scale_ref,
+    all_planes, odd_ref, rd_ref, b_ref, a_ref, inner_ref, row_taps_ref, row_shift_ref, taps_ref, shift_ref, scale_ref,
     q_ref, n_ref, dense_ref, halo_ref,
 ):
     odd = odd_ref[0] == 1
@@ -254,7 +254,7 @@
 
 
 def emission_kernel(
-    all_planes, odd_ref, re_ref, a_ref, b_ref, q_ref, n_ref, inner_ref, optical_ref, row_taps_ref, row_shift_ref, taps_ref, shift_ref, scale_ref,
+    all_planes, odd_ref, re_ref, b_ref, a_ref, q_ref, n_ref, inner_ref, optical_ref, row_taps_ref, row_shift_ref, taps_ref, shift_ref, scale_ref,
     p_ref, pa_ref, pb_ref, dense_ref, halo_ref,
 ):
     odd = odd_ref[0] == 1
@@ -535,14 +535,14 @@
         functools.partial(density_kernel, all_planes),
         [outside, outside, dense],
         [],
-        [where, rd, da, db, inner_sums, row_taps, row_shift, taps, shift, scale],
+        [where, rd, db, da, inner_sums, row_taps, row_shift, taps, shift, scale],
         [pltpu.VMEM(outer, F32)],
     )
     p_out, pa, pb, state = call(
         functools.partial(emission_kernel, all_planes),
         [outside, outside, outside, (2,) + dense],
         [],
-        [where, re, ea, eb, q_out, n_out, inner_sums, slab_optical, row_taps, row_shift, taps, shift, scale],
+        [where, re, eb, ea, q_out, n_out, inner_sums, slab_optical, row_taps, row_shift, taps, shift, scale],
         [pltpu.VMEM(outer, F32)],
         micros=6.0,
     )

time: 37.7 us -> 37.5 us (level)
  starting transfers between devices: 14.4 us -> 13.4 us
  waiting for transfers between devices: 10.5 us -> 11.4 us
    ppermute x8, starting transfers between devices: 13.6 us -> 12.6 us  [swap(): return lax.ppermute(value, axis, pairs)]
    ppermute x8, waiting for transfers between devices: 7.3 us -> 8.24 us  [swap(): return lax.ppermute(value, axis, pairs)]
where the time goes in v5:
time: 37.5 us; the launch traced here: 37.3 us
  starting transfers between devices  13.4 us (36%)
  Pallas kernels  11.4 us (30%)
  waiting for transfers between devices  11.4 us (30%)
  between operations  0.85 us (2%)
    ppermute x8, starting transfers between devices, swap(): return lax.ppermute(value, axis, pairs)  12.6 us
    pallas_call x8, Pallas kernels, call(): pl.pallas_call(kernel, out_shape=[jax.ShapeDtypeStruct(s, F32) if i < hbm...  11.4 us
    ppermute x8, waiting for transfers between devices, swap(): return lax.ppermute(value, axis, pairs)  8.24 us
    ppermute x3, waiting for transfers between devices, on_device(): lax.ppermute(state, 'depth', [((i + e) % slabs, i) for i in range(slabs)])  3.18 us
    ppermute x3, starting transfers between devices, on_device(): lax.ppermute(state, 'depth', [((i + e) % slabs, i) for i in range(slabs)])  0.82 us
  transfers between devices with their start and end apart: 11, of which 7 were waited for; matrix products, arithmetic and copies ran while one was open for 0% of the time, Pallas kernels for 19%

profile of v5, /device:TPU:14, one launch (start us, length us, event | category | flops | bytes accessed | tf_op | source)
XLA Modules:
  0.0 37.3 jit_solution(3437064372467221885)
XLA Ops:
  0.6 0.0 copy-start
  0.6 0.0 copy-start.1
  0.7 0.0 copy-start.2
  0.7 0.0 copy-start.3
  0.7 0.0 copy-start.4
  0.7 0.0 copy-start.5
  0.7 0.0 copy-start.6
  0.7 0.0 copy-start.7
  0.7 0.1 pad_add_fusion
  0.8 0.1 broadcast_in_dim.15.where_ref.odd_ref
  0.9 1.2 %shard_map.97 = (f32[64,8,128]{2,1,0:T(8,128)S(1)}, f32[64,8,128]{2,1,0:T(8,128)S(1)}) custom-call(s32[2,8,128]{2,1,0:T(8,128)S(1)} %broadcast_in_dim.15.where_ref.odd_ref, f32[64,32,128]{2,1,0:T(8,128)} %field_ref.3), custom_call_target="tpu_custom_call" | custom-call | flops 200000 | bytes 600000 | tf_op jit(solution)/shard_map/pallas_call | solution.py:473
  2.1 3.5 %collective-permute-start.2 = (f32[64,8,128]{2,1,0:T(8,128)S(1)}, f32[64,8,128]{2,1,0:T(8,128)S(1)}, u32[]{:S(2)}, u32[]{:S(2)}) collective-permute-start(f32[64,8,128]{2,1,0:T(8,128)S(1)} %get-tuple-element.27), channel_id=1, source_target_pairs={{1,2},{2,1},{5,6},{6,5},{9,10},{10,9},{13,14},{14,13},{17,18},{18,... | collective-permute-start | bytes 786440 | tf_op jit(solution)/shard_map/ppermute | solution.py:494
  5.6 0.1 collective-permute-start.3
  5.7 1.1 %shard_map.96 = (f32[64,8,128]{2,1,0:T(8,128)S(1)}, f32[64,8,128]{2,1,0:T(8,128)S(1)}) custom-call(s32[2,8,128]{2,1,0:T(8,128)S(1)} %broadcast_in_dim.15.where_ref.odd_ref, f32[64,32,128]{2,1,0:T(8,128)} %field_ref.2), custom_call_target="tpu_custom_call" | custom-call | flops 200000 | bytes 600000 | tf_op jit(solution)/shard_map/pallas_call | solution.py:473
  6.8 2.4 %collective-permute-start = (f32[64,8,128]{2,1,0:T(8,128)S(1)}, f32[64,8,128]{2,1,0:T(8,128)S(1)}, u32[]{:S(2)}, u32[]{:S(2)}) collective-permute-start(f32[64,8,128]{2,1,0:T(8,128)S(1)} %get-tuple-element.24), channel_id=1, source_target_pairs={{1,2},{2,1},{5,6},{6,5},{9,10},{10,9},{13,14},{14,13},{17,18},{18,... | collective-permute-start | bytes 786440 | tf_op jit(solution)/shard_map/ppermute | solution.py:494
  9.2 0.4 %collective-permute-start.1 = (f32[64,8,128]{2,1,0:T(8,128)S(1)}, f32[64,8,128]{2,1,0:T(8,128)S(1)}, u32[]{:S(2)}, u32[]{:S(2)}) collective-permute-start(f32[64,8,128]{2,1,0:T(8,128)S(1)} %get-tuple-element.25), channel_id=1, source_target_pairs={{0,1},{1,0},{2,3},{3,2},{4,5},{5,4},{6,7},{7,6},{8,9},{9,8},{10,11... | collective-permute-start | bytes 786440 | tf_op jit(solution)/shard_map/ppermute | solution.py:494
  9.5 0.0 copy-done
  9.5 0.0 copy-done.1
  9.6 0.0 copy-done.2
  9.6 0.0 copy-done.3
  9.6 0.0 copy-done.4
  9.6 0.0 copy-done.5
  9.6 0.0 copy-done.6
  9.6 0.0 copy-done.7
  9.6 2.2 %shard_map.95 = (f32[2112,128]{1,0:T(8,128)S(1)}, f32[2112,128]{1,0:T(8,128)S(1)}, f32[16,64,128]{2,1,0:T(8,128)S(1)}, f32[16,64,128]{2,1,0:T(8,128)S(1)}, f32[2...) custom-call(f32[64,32,128]{2,1,0:T(8,128)S(1)} %copy-done, f32[64,32,128]{2,1,0:T(8,128)S(1)} %copy-done.1, ...), custom_call_target="tpu_custom_call" | custom-call | flops 3000000 | bytes 9000000 | tf_op jit(solution)/shard_map/pallas_call | solution.py:473
  11.8 1.4 %collective-permute-done.2.b_ref = f32[64,8,128]{2,1,0:T(8,128)S(1)} collective-permute-done((f32[64,8,128]{2,1,0:T(8,128)S(1)}, f32[64,8,128]{2,1,0:T(8,128)S(1)}, u32[]{:S(2)}, u32[]{:S(2)}) %collective-permute-start.2) | collective-permute-done | bytes 262176 | tf_op jit(solution)/shard_map/ppermute | solution.py:494
  13.2 1.7 %collective-permute-done.3.a_ref = f32[64,8,128]{2,1,0:T(8,128)S(1)} collective-permute-done((f32[64,8,128]{2,1,0:T(8,128)S(1)}, f32[64,8,128]{2,1,0:T(8,128)S(1)}, u32[]{:S(2)}, u32[]{:S(2)}) %collective-permute-start.3) | collective-permute-done | bytes 262176 | tf_op jit(solution)/shard_map/ppermute | solution.py:494
  14.9 1.0 %shard_map.98 = (f32[16,64,128]{2,1,0:T(8,128)S(1)}, f32[16,64,128]{2,1,0:T(8,128)S(1)}, f32[2,8,128]{2,1,0:T(8,128)S(1)}) custom-call(s32[2,8,128]{2,1,0:T(8,128)S(1)} %broadcast_in_dim.15.where_ref.odd_ref, f32[2112,128]{1,0:T(8,128)S(1)} %get-tuple-element.26.rd_ref, f32[64,8,128]{2,1,0:T(8,128)S(1)} %collective-permute-done.2.b_ref, ...), custom_call_target="tpu_custom_call" | custom-call | flops 2000000 | bytes 6000000 | tf_op jit(solution)/shard_map/pallas_call | solution.py:473
  15.9 1.7 %collective-permute-done.b_ref = f32[64,8,128]{2,1,0:T(8,128)S(1)} collective-permute-done((f32[64,8,128]{2,1,0:T(8,128)S(1)}, f32[64,8,128]{2,1,0:T(8,128)S(1)}, u32[]{:S(2)}, u32[]{:S(2)}) %collective-permute-start) | collective-permute-done | bytes 262176 | tf_op jit(solution)/shard_map/ppermute | solution.py:494
  17.7 1.4 %collective-permute-done.1.a_ref = f32[64,8,128]{2,1,0:T(8,128)S(1)} collective-permute-done((f32[64,8,128]{2,1,0:T(8,128)S(1)}, f32[64,8,128]{2,1,0:T(8,128)S(1)}, u32[]{:S(2)}, u32[]{:S(2)}) %collective-permute-start.1) | collective-permute-done | bytes 262176 | tf_op jit(solution)/shard_map/ppermute | solution.py:494
  19.0 1.0 %shard_map.99 = (f32[16,64,128]{2,1,0:T(8,128)S(1)}, f32[16,64,128]{2,1,0:T(8,128)S(1)}, f32[16,64,128]{2,1,0:T(8,128)S(1)}, f32[2,2,8,128]{3,2,1,0:T(8,128)S(1)}) custom-call(s32[2,8,128]{2,1,0:T(8,128)S(1)} %broadcast_in_dim.15.where_ref.odd_ref, f32[2112,128]{1,0:T(8,128)S(1)} %get-tuple-element.23.re_ref, f32[64,8,128]{2,1,0:T(8,128)S(1)} %collective-permute-done.b_ref, ...), custom_call_target="tpu_custom_call" | custom-call | flops 6000000 | bytes 18000000 | tf_op jit(solution)/shard_map/pallas_call | solution.py:473
  20.0 0.4 collective-permute-start.4
  20.4 2.3 %collective-permute-start.5 = (f32[16,64,128]{2,1,0:T(8,128)S(1)}, f32[16,64,128]{2,1,0:T(8,128)S(1)}, u32[]{:S(2)}, u32[]{:S(2)}) collective-permute-start(f32[16,64,128]{2,1,0:T(8,128)S(1)} %get-tuple-element.34), channel_id=1, source_target_pairs={{1,2},{2,1},{5,6},{6,5},{9,10},{10,9},{13,14},{14,13},{17,18},{18,... | collective-permute-start | bytes 1572872 | tf_op jit(solution)/shard_map/ppermute | solution.py:494
  22.8 0.1 collective-permute-start.6
  22.8 0.6 %collective-permute-start.7 = (f32[2,2,8,128]{3,2,1,0:T(8,128)S(1)}, f32[2,2,8,128]{3,2,1,0:T(8,128)S(1)}, u32[]{:S(2)}, u32[]{:S(2)}) collective-permute-start(f32[2,2,8,128]{3,2,1,0:T(8,128)S(1)} %get-tuple-element.36.refs_0_), channel_id=1, source_target_pairs={{8,0},{12,4},{0,8},{4,12},{9,1},{13,5},{1,9},{5,13},{10,2},{14,6},... | collective-permute-start | bytes 49160 | tf_op jit(solution)/shard_map/ppermute | solution.py:551
  23.4 0.2 collective-permute-start.8
  23.6 0.7 %collective-permute-done.6.refs_1_ = f32[2,2,8,128]{3,2,1,0:T(8,128)S(1)} collective-permute-done((f32[2,2,8,128]{3,2,1,0:T(8,128)S(1)}, f32[2,2,8,128]{3,2,1,0:T(8,128)S(1)}, u32[]{:S(2)}, u32[]{:S(2)}) %collective-permute-start.6) | collective-permute-done | bytes 16416 | tf_op jit(solution)/shard_map/ppermute | solution.py:551
  24.3 2.5 %collective-permute-done.7.refs_2_ = f32[2,2,8,128]{3,2,1,0:T(8,128)S(1)} collective-permute-done((f32[2,2,8,128]{3,2,1,0:T(8,128)S(1)}, f32[2,2,8,128]{3,2,1,0:T(8,128)S(1)}, u32[]{:S(2)}, u32[]{:S(2)}) %collective-permute-start.7) | collective-permute-done | bytes 16416 | tf_op jit(solution)/shard_map/ppermute | solution.py:551
  26.8 0.0 collective-permute-done.8.refs_3_
  26.8 0.1 collective-permute-start.10
  26.9 3.4 %collective-permute-start.9 = (f32[2,2,8,128]{3,2,1,0:T(8,128)S(1)}, f32[2,2,8,128]{3,2,1,0:T(8,128)S(1)}, u32[]{:S(2)}, u32[]{:S(2)}) collective-permute-start(f32[2,2,8,128]{3,2,1,0:T(8,128)S(1)} %shard_map.100.own_ref), channel_id=1, source_target_pairs={{1,2},{2,1},{5,6},{6,5},{9,10},{10,9},{13,14},{14,13},{17,18},{18,... | collective-permute-start | bytes 49160 | tf_op jit(solution)/shard_map/ppermute | solution.py:494
  30.4 2.7 %shard_map.101 = (f32[64,32,128]{2,1,0:T(8,128)}, f32[64,32,128]{2,1,0:T(8,128)}, f32[1088,128]{1,0:T(8,128)S(1)}, f32[1088,128]{1,0:T(8,128)S(1)}) custom-call(f32[16,64,128]{2,1,0:T(8,128)S(1)} %get-tuple-element.37.p_in, f32[16,64,128]{2,1,0:T(8,128)S(1)} %get-tuple-element.38.q_in, f32[16,64,128]{2,1,0:T(8,128)S(1)} %get-tuple-element.39.p_out, ...), custom_call_target="tpu_custom_call" | custom-call | flops 6000000 | bytes 18000000 | tf_op jit(solution)/shard_map/pallas_call | solution.py:473
  33.1 0.0 collective-permute-done.10.wa_ref
  33.1 2.0 %collective-permute-done.9.wb_ref = f32[2,2,8,128]{3,2,1,0:T(8,128)S(1)} collective-permute-done((f32[2,2,8,128]{3,2,1,0:T(8,128)S(1)}, f32[2,2,8,128]{3,2,1,0:T(8,128)S(1)}, u32[]{:S(2)}, u32[]{:S(2)}) %collective-permute-start.9) | collective-permute-done | bytes 16416 | tf_op jit(solution)/shard_map/ppermute | solution.py:494
  35.1 0.0 collective-permute-done.4.pa_ref
  35.1 0.0 collective-permute-done.5.pb_ref
  35.1 2.1 %shard_map.102 = (f32[64,32,128]{2,1,0:T(8,128)}, f32[64,32,128]{2,1,0:T(8,128)}) custom-call(s32[2,8,128]{2,1,0:T(8,128)S(1)} %broadcast_in_dim.15.where_ref.odd_ref, f32[16,64,128]{2,1,0:T(8,128)S(1)} %collective-permute-done.4.pa_ref, f32[16,64,128]{2,1,0:T(8,128)S(1)} %collective-permute-done.5.pb_ref, ...), custom_call_target="tpu_custom_call", output_to_operand_aliasing={{0}: (12, {}), {1}: (13, {})} | custom-call | flops 2000000 | bytes 6000000 | tf_op jit(solution)/shard_map/pallas_call | solution.py:473
  (1 shorter events, 0.0 us)
Async XLA Ops:
  0.6 8.9 %copy-start = (f32[64,32,128]{2,1,0:T(8,128)S(1)}, f32[64,32,128]{2,1,0:T(8,128)}, u32[]{:S(2)}) copy-start(f32[64,32,128]{2,1,0:T(8,128)} %field_ref.3) | copy-start | bytes 3145732
  0.6 8.9 %copy-start.1 = (f32[64,32,128]{2,1,0:T(8,128)S(1)}, f32[64,32,128]{2,1,0:T(8,128)}, u32[]{:S(2)}) copy-start(f32[64,32,128]{2,1,0:T(8,128)} %field_ref.2) | copy-start | bytes 3145732
  0.7 8.9 %copy-start.2 = (f32[4,128]{1,0:T(4,128)S(1)}, f32[4,128]{1,0:T(4,128)}, u32[]{:S(2)}) copy-start(f32[4,128]{1,0:T(4,128)} %row_taps_ref.9) | copy-start | bytes 6148
  0.7 8.9 %copy-start.3 = (f32[4,128]{1,0:T(4,128)S(1)}, f32[4,128]{1,0:T(4,128)}, u32[]{:S(2)}) copy-start(f32[4,128]{1,0:T(4,128)} %taps_ref.9) | copy-start | bytes 6148
  0.7 8.9 %copy-start.4 = (f32[64,32]{0,1:T(8,128)S(1)}, f32[64,32]{0,1:T(8,128)}, u32[]{:S(2)}) copy-start(f32[64,32]{0,1:T(8,128)} %param.15) | copy-start | bytes 24580
  0.7 8.9 %copy-start.5 = (s32[128]{0:T(128)S(1)}, s32[128]{0:T(128)}, u32[]{:S(2)}) copy-start(s32[128]{0:T(128)} %param.13) | copy-start | bytes 1540
  0.7 8.9 %copy-start.6 = (s32[128]{0:T(128)S(1)}, s32[128]{0:T(128)}, u32[]{:S(2)}) copy-start(s32[128]{0:T(128)} %param.11) | copy-start | bytes 1540
  0.7 8.9 %copy-start.7 = (f32[128]{0:T(128)S(1)}, f32[128]{0:T(128)}, u32[]{:S(2)}) copy-start(f32[128]{0:T(128)} %param.14) | copy-start | bytes 1540
  2.1 11.1 %collective-permute-start.2 = (f32[64,8,128]{2,1,0:T(8,128)S(1)}, f32[64,8,128]{2,1,0:T(8,128)S(1)}, u32[]{:S(2)}, u32[]{:S(2)}) collective-permute-start(f32[64,8,128]{2,1,0:T(8,128)S(1)} %get-tuple-element.27), channel_id=1, source_target_pairs={{1,2},{2,1},{5,6},{6,5},{9,10},{10,9},{13,14},{14,13},{17,18},{18,... | collective-permute-start | bytes 786440 | tf_op jit(solution)/shard_map/ppermute | solution.py:494
  5.6 9.3 %collective-permute-start.3 = (f32[64,8,128]{2,1,0:T(8,128)S(1)}, f32[64,8,128]{2,1,0:T(8,128)S(1)}, u32[]{:S(2)}, u32[]{:S(2)}) collective-permute-start(f32[64,8,128]{2,1,0:T(8,128)S(1)} %get-tuple-element.28), channel_id=1, source_target_pairs={{0,1},{1,0},{2,3},{3,2},{4,5},{5,4},{6,7},{7,6},{8,9},{9,8},{10,11... | collective-permute-start | bytes 786440 | tf_op jit(solution)/shard_map/ppermute | solution.py:494
  6.8 10.9 %collective-permute-start = (f32[64,8,128]{2,1,0:T(8,128)S(1)}, f32[64,8,128]{2,1,0:T(8,128)S(1)}, u32[]{:S(2)}, u32[]{:S(2)}) collective-permute-start(f32[64,8,128]{2,1,0:T(8,128)S(1)} %get-tuple-element.24), channel_id=1, source_target_pairs={{1,2},{2,1},{5,6},{6,5},{9,10},{10,9},{13,14},{14,13},{17,18},{18,... | collective-permute-start | bytes 786440 | tf_op jit(solution)/shard_map/ppermute | solution.py:494
  9.2 9.9 %collective-permute-start.1 = (f32[64,8,128]{2,1,0:T(8,128)S(1)}, f32[64,8,128]{2,1,0:T(8,128)S(1)}, u32[]{:S(2)}, u32[]{:S(2)}) collective-permute-start(f32[64,8,128]{2,1,0:T(8,128)S(1)} %get-tuple-element.25), channel_id=1, source_target_pairs={{0,1},{1,0},{2,3},{3,2},{4,5},{5,4},{6,7},{7,6},{8,9},{9,8},{10,11... | collective-permute-start | bytes 786440 | tf_op jit(solution)/shard_map/ppermute | solution.py:494
  20.0 15.1 %collective-permute-start.4 = (f32[16,64,128]{2,1,0:T(8,128)S(1)}, f32[16,64,128]{2,1,0:T(8,128)S(1)}, u32[]{:S(2)}, u32[]{:S(2)}) collective-permute-start(f32[16,64,128]{2,1,0:T(8,128)S(1)} %get-tuple-element.33), channel_id=1, source_target_pairs={{0,1},{1,0},{2,3},{3,2},{4,5},{5,4},{6,7},{7,6},{8,9},{9,8},{10,11... | collective-permute-start | bytes 1572872 | tf_op jit(solution)/shard_map/ppermute | solution.py:494
  20.4 14.8 %collective-permute-start.5 = (f32[16,64,128]{2,1,0:T(8,128)S(1)}, f32[16,64,128]{2,1,0:T(8,128)S(1)}, u32[]{:S(2)}, u32[]{:S(2)}) collective-permute-start(f32[16,64,128]{2,1,0:T(8,128)S(1)} %get-tuple-element.34), channel_id=1, source_target_pairs={{1,2},{2,1},{5,6},{6,5},{9,10},{10,9},{13,14},{14,13},{17,18},{18,... | collective-permute-start | bytes 1572872 | tf_op jit(solution)/shard_map/ppermute | solution.py:494
  22.8 1.5 %collective-permute-start.6 = (f32[2,2,8,128]{3,2,1,0:T(8,128)S(1)}, f32[2,2,8,128]{3,2,1,0:T(8,128)S(1)}, u32[]{:S(2)}, u32[]{:S(2)}) collective-permute-start(f32[2,2,8,128]{3,2,1,0:T(8,128)S(1)} %get-tuple-element.36.refs_0_), channel_id=1, source_target_pairs={{4,0},{8,4},{12,8},{0,12},{5,1},{9,5},{13,9},{1,13},{6,2},{10,6},{... | collective-permute-start | bytes 49160 | tf_op jit(solution)/shard_map/ppermute | solution.py:551
  22.8 3.9 %collective-permute-start.7 = (f32[2,2,8,128]{3,2,1,0:T(8,128)S(1)}, f32[2,2,8,128]{3,2,1,0:T(8,128)S(1)}, u32[]{:S(2)}, u32[]{:S(2)}) collective-permute-start(f32[2,2,8,128]{3,2,1,0:T(8,128)S(1)} %get-tuple-element.36.refs_0_), channel_id=1, source_target_pairs={{8,0},{12,4},{0,8},{4,12},{9,1},{13,5},{1,9},{5,13},{10,2},{14,6},... | collective-permute-start | bytes 49160 | tf_op jit(solution)/shard_map/ppermute | solution.py:551
  23.4 3.3 %collective-permute-start.8 = (f32[2,2,8,128]{3,2,1,0:T(8,128)S(1)}, f32[2,2,8,128]{3,2,1,0:T(8,128)S(1)}, u32[]{:S(2)}, u32[]{:S(2)}) collective-permute-start(f32[2,2,8,128]{3,2,1,0:T(8,128)S(1)} %get-tuple-element.36.refs_0_), channel_id=1, source_target_pairs={{12,0},{0,4},{4,8},{8,12},{13,1},{1,5},{5,9},{9,13},{14,2},{2,6},{... | collective-permute-start | bytes 49160 | tf_op jit(solution)/shard_map/ppermute | solution.py:551
  26.8 6.3 %collective-permute-start.10 = (f32[2,2,8,128]{3,2,1,0:T(8,128)S(1)}, f32[2,2,8,128]{3,2,1,0:T(8,128)S(1)}, u32[]{:S(2)}, u32[]{:S(2)}) collective-permute-start(f32[2,2,8,128]{3,2,1,0:T(8,128)S(1)} %shard_map.100.own_ref), channel_id=1, source_target_pairs={{0,1},{1,0},{2,3},{3,2},{4,5},{5,4},{6,7},{7,6},{8,9},{9,8},{10,11... | collective-permute-start | bytes 49160 | tf_op jit(solution)/shard_map/ppermute | solution.py:494
  26.9 8.2 %collective-permute-start.9 = (f32[2,2,8,128]{3,2,1,0:T(8,128)S(1)}, f32[2,2,8,128]{3,2,1,0:T(8,128)S(1)}, u32[]{:S(2)}, u32[]{:S(2)}) collective-permute-start(f32[2,2,8,128]{3,2,1,0:T(8,128)S(1)} %shard_map.100.own_ref), channel_id=1, source_target_pairs={{1,2},{2,1},{5,6},{6,5},{9,10},{10,9},{13,14},{14,13},{17,18},{18,... | collective-permute-start | bytes 49160 | tf_op jit(solution)/shard_map/ppermute | solution.py:494
